TPU v7x, 256 devices: a whole 4x4x8 slice. The times are simulated.
256 devices in a mesh: role: 2 (over y_hi), dp: 2 (over y_lo), expert: 64 (over x, z, core).
Axes of the slice: x: 4, y: 4 (y_hi: 2, y_lo: 2; y = y_hi * 2 + y_lo), z: 8, core: 2. Of those that a mesh axis runs over, the one named last changes fastest.
Arguments:
- prompt_pool: bfloat16 [2, 2, 64, 20, 64, 576], P('role', 'dp', 'expert'), may hold values from -6 to 6
- block_table: int32 [2, 2, 64, 4, 4], P(None, 'dp', 'expert'), may hold values from 0 to 19, as said below
- cache_len: int32 [2, 2, 4], P('role', 'dp'), may hold values from 1 to 16384, as said below
- queries: bfloat16 [2, 2, 2, 4, 64, 576], P(None, 'role', 'dp')
- fresh_latent: bfloat16 [2, 2, 2, 4, 576], P(None, 'role', 'dp'), may hold values from -6 to 6
- x_in: bfloat16 [2, 2, 2, 4, 7168], P(None, 'role', 'dp', None, 'expert'), may hold values from -4 to 4
- routes: int32 [2, 2, 2, 4, 8], P(None, 'role', 'dp'), may hold values from 0 to 15, all different within a row; in each aligned block of 4 rows (0 to 3, 4 to 7, ..., all dimensions but the last counted through in order) at most 3 rows name the same one
- gates: float32 [2, 2, 2, 4, 8], P(None, 'role', 'dp'), may hold values from 0.2 to 1
- norm_gain: float32 [7168], replicated, may hold values from 0.5 to 1.5
- value_up: bfloat16 [64, 512, 128], P('expert'), may hold values from -0.25 to 0.25
- out_proj: bfloat16 [8192, 7168], P('expert'), may hold values from -0.1875 to 0.1875
- w_gate: bfloat16 [128, 7168, 128], P(('dp', 'expert')), may hold values from -0.0625 to 0.0625
- w_up: bfloat16 [128, 7168, 128], P(('dp', 'expert')), may hold values from -0.0625 to 0.0625
- w_down: bfloat16 [128, 128, 7168], P(('dp', 'expert')), may hold values from -0.1875 to 0.1875
Outputs:
- layer_out: bfloat16 [2, 2, 2, 4, 7168], P(None, 'role', 'dp', None, 'expert')
Inputs may be any that keep to these rules, and one draw needn't show every extreme that they name: `block_table`: within one device's table (fixed r, d, e) the 16 slots differ. `cache_len`: some request of every group has all 16384 positions cached. `routes`: in each step, at most 3 of one group's 4 requests name the same expert; a request's 8 experts differ.
All inputs are finite; a program needn't handle non-finite values.
Results may differ from a plain program's by a relative error of at most 0.014.
Values may be sent and summed in bfloat16 or wider, within the bound.
No kernel may reach another device: no remote copies, remote signals or barrier semaphores. Data moves between devices by JAX's collectives and lax.ppermute only.
A program may use at most 192 MiB of HBM per device.

v0:
```python
import jax
import jax.numpy as jnp
from jax import lax
from jax.sharding import PartitionSpec as P

SLICES = 8
CAP = 3


SCORE_SCALE = 192.0 ** (-0.5)
EPSILON = 1e-06
MASK_VALUE = -1e30


def swapped(value, axis, distance):
    mask = 2**distance
    pairs = [(source, source ^ mask) for source in range(lax.axis_size(axis))]
    return lax.ppermute(value, axis, pairs)


def block_parts(queries_now, cached, lengths, offset, lat_width):
    scores = (
        jnp.einsum("qhc,qpc->qhp", queries_now, cached, preferred_element_type=jnp.float32)
        * SCORE_SCALE
    )
    places = offset + lax.broadcasted_iota(jnp.int32, (1, 1, cached.shape[1]), 2)
    usable = places < lengths[:, None, None]
    scores = jnp.where(usable, scores, MASK_VALUE)
    maximum = jnp.max(scores, axis=2)
    weights = jnp.where(usable, jnp.exp(scores - maximum[:, :, None]), 0.0)
    totals = jnp.sum(weights, axis=2)
    summed = jnp.einsum(
        "qhp,qpc->qhc",
        weights.astype(jnp.bfloat16),
        cached[:, :, :lat_width],
        preferred_element_type=jnp.float32,
    )
    return (maximum, totals, summed)


def finish_context(maximum, totals, summed, queries_now, fresh, lat_width):
    fresh_scores = (
        jnp.einsum("qhc,tqc->qht", queries_now, fresh, preferred_element_type=jnp.float32)
        * SCORE_SCALE
    )
    highest = jnp.maximum(maximum, jnp.max(fresh_scores, axis=2))
    carried = jnp.exp(maximum - highest)
    fresh_weights = jnp.exp(fresh_scores - highest[:, :, None])
    fresh_part = jnp.einsum(
        "qht,tqc->qhc",
        fresh_weights.astype(jnp.bfloat16),
        fresh[:, :, :lat_width],
        preferred_element_type=jnp.float32,
    )
    numerator = carried[:, :, None] * summed + fresh_part
    denominator = carried * totals + jnp.sum(fresh_weights, axis=2)
    return (numerator / denominator[:, :, None]).astype(jnp.bfloat16)


def body(
    prompt_pool,
    block_table,
    cache_len,
    queries,
    fresh_latent,
    x_in,
    routes,
    gates,
    norm_gain,
    value_up,
    out_proj,
    w_gate,
    w_up,
    w_down,
):
    pool_local = prompt_pool[0, 0, 0]
    tables = block_table[:, 0, 0]
    requests = tables.shape[1]
    span = tables.shape[2] * pool_local.shape[1]
    width_kv = pool_local.shape[2]
    heads_here = value_up.shape[0]
    lat_width = value_up.shape[1]
    role_here = lax.axis_index("role")
    expert_here = lax.axis_index("expert")
    dp_count = lax.axis_size("dp")
    expert_count = lax.axis_size("expert")
    expert_total = dp_count * expert_count // SLICES
    received = swapped(pool_local, "role", 0)
    wanted = lax.dynamic_index_in_dim(tables, role_here, 0, keepdims=False)
    arrived = jnp.take(received, wanted.reshape(-1), axis=0)
    cached = arrived.reshape(requests, span, width_kv)
    lengths = cache_len[0, 0]
    offset = expert_here * span
    expert_ids = lax.broadcasted_iota(jnp.int32, (1, 1, expert_total), 2)
    slot_ids = lax.broadcasted_iota(jnp.int32, (1, 1, CAP), 2).astype(jnp.float32)
    earlier = (
        lax.broadcasted_iota(jnp.int32, (requests, requests), 0)
        > lax.broadcasted_iota(jnp.int32, (requests, requests), 1)
    ).astype(jnp.float32)
    outputs = []
    for step_index in range(queries.shape[0]):
        queries_now = queries[step_index, 0, 0]
        maximum, totals, summed = block_parts(queries_now, cached, lengths, offset, lat_width)
        parts = (
            lax.all_to_all(maximum[None], "expert", split_axis=2, concat_axis=0, tiled=True),
            lax.all_to_all(totals[None], "expert", split_axis=2, concat_axis=0, tiled=True),
            lax.all_to_all(summed[None], "expert", split_axis=2, concat_axis=0, tiled=True),
        )
        overall = jnp.max(parts[0], axis=0)
        factors = jnp.exp(parts[0] - overall[None])
        totals_mine = jnp.sum(factors * parts[1], axis=0)
        summed_mine = jnp.sum(factors[..., None] * parts[2], axis=0)
        queries_mine = lax.dynamic_slice_in_dim(
            queries_now, expert_here * heads_here, heads_here, 1
        )
        context = finish_context(
            overall,
            totals_mine,
            summed_mine,
            queries_mine,
            fresh_latent[: step_index + 1, 0, 0],
            lat_width,
        )
        head_vals = jnp.einsum(
            "qhl,hlv->qhv", context, value_up, preferred_element_type=jnp.float32
        ).astype(jnp.bfloat16)
        partial_out = jnp.dot(
            head_vals.reshape(requests, -1), out_proj, preferred_element_type=jnp.float32
        )
        attended = lax.psum_scatter(partial_out, "expert", scatter_dimension=1, tiled=True)
        resid = (x_in[step_index, 0, 0].astype(jnp.float32) + attended).astype(jnp.bfloat16)
        column_count = resid.shape[1]
        picked = (routes[step_index, 0, 0][:, :, None] == expert_ids).astype(jnp.float32)
        hits = jnp.sum(picked, axis=1)
        mixing = jnp.sum(gates[step_index, 0, 0][:, :, None] * picked, axis=1)
        slots = jnp.dot(earlier, hits, precision=lax.Precision.HIGHEST)
        slot_hot = (slots[:, :, None] == slot_ids).astype(jnp.float32) * hits[:, :, None]
        placing = slot_hot.reshape(requests, expert_total * CAP)
        packed = jnp.einsum(
            "qk,qf->kf", placing.astype(jnp.bfloat16), resid, preferred_element_type=jnp.float32
        ).astype(jnp.bfloat16)
        outgoing = jnp.broadcast_to(
            packed.reshape(expert_total, 1, CAP, column_count),
            (expert_total, SLICES, CAP, column_count),
        ).reshape(dp_count, expert_count, CAP, column_count)
        rows = lax.all_to_all(
            lax.all_to_all(outgoing, "dp", split_axis=0, concat_axis=2, tiled=True),
            "expert",
            split_axis=1,
            concat_axis=3,
            tiled=True,
        )[0, 0]
        flat = rows.astype(jnp.float32)
        normed = (
            flat * lax.rsqrt(jnp.mean(flat * flat, axis=1, keepdims=True) + EPSILON) * norm_gain
        ).astype(jnp.bfloat16)
        gate_part = jnp.dot(normed, w_gate[0], preferred_element_type=jnp.float32)
        up_part = jnp.dot(normed, w_up[0], preferred_element_type=jnp.float32)
        hidden_act = (jax.nn.silu(gate_part) * up_part).astype(jnp.bfloat16)
        expert_part = jnp.dot(hidden_act, w_down[0], preferred_element_type=jnp.float32)
        back = lax.all_to_all(
            lax.all_to_all(
                expert_part[None, None].astype(jnp.bfloat16),
                "dp",
                split_axis=2,
                concat_axis=0,
                tiled=True,
            ),
            "expert",
            split_axis=3,
            concat_axis=1,
            tiled=True,
        ).astype(jnp.float32)
        per_expert = jnp.sum(back.reshape(expert_total, SLICES, CAP, column_count), axis=1)
        weighted = (slot_hot * mixing[:, :, None]).reshape(requests, expert_total * CAP)
        mixed = jnp.dot(
            weighted,
            per_expert.reshape(expert_total * CAP, column_count),
            precision=lax.Precision.HIGHEST,
        )
        outputs.append((resid.astype(jnp.float32) + mixed).astype(jnp.bfloat16))
    return jnp.stack(outputs)[:, None, None]


def solution(mesh):
    placed = (
        P("role", "dp", "expert", None, None, None),
        P(None, "dp", "expert", None, None),
        P("role", "dp", None),
        P(None, "role", "dp", None, None, None),
        P(None, "role", "dp", None, None),
        P(None, "role", "dp", None, "expert"),
        P(None, "role", "dp", None, None),
        P(None, "role", "dp", None, None),
        P(),
        P("expert", None, None),
        P("expert", None),
        P(("dp", "expert"), None, None),
        P(("dp", "expert"), None, None),
        P(("dp", "expert"), None, None),
    )
    return jax.shard_map(
        body,
        mesh=mesh,
        in_specs=placed,
        out_specs=P(None, "role", "dp", None, "expert"),
        check_vma=False,
    )
```

profile of v0, /device:TPU:16, one launch (start us, length us, event | category | flops | bytes accessed | tf_op | source)
XLA Modules:
  0.0 586.8 jit_solution(11533901048735419304)
XLA Ops:
  6.5 2.1 collective-permute-start
  10.1 2.0 fusion.133
  15.4 1.3 slice_bitcast_fusion.3
  16.7 1.5 fusion.73
  18.2 27.6 %collective-permute-done = bf16[20,64,576]{2,1,0:T(8,128)(2,1)S(1)} collective-permute-done((bf16[20,64,576]{2,1,0:T(8,128)(2,1)}, bf16[20,64,576]{2,1,0:T(8,128)(2,1)S(1)}, u32[]{:S(2)}, u32[]{:S(2)}) %collective-permute-start) | collective-permute-done | bytes 1474592 | tf_op jit(solution)/shard_map/ppermute | solution.py:18
  45.8 1.8 gather_fusion
  47.6 1.6 bitcast_select_fusion
  51.7 11.9 %all-to-all-start.7 = ((f32[1,4,64]{1,0,2:T(1,128)}), f32[1,4,64]{1,0,2:T(1,128)S(1)}, u32[]{:S(2)}, u32[]{:S(2)}) async-start(f32[1,4,64]{1,0,2:T(1,128)} %copy.127), calls=%async_computation.7 | async-start | bytes 65536 | tf_op jit(solution)/shard_map/all_to_all | solution.py:105
  65.6 7.5 %all-to-all-done.7 = f32[1,4,64]{1,0,2:T(1,128)S(1)} async-done(((f32[1,4,64]{1,0,2:T(1,128)}), f32[1,4,64]{1,0,2:T(1,128)S(1)}, u32[]{:S(2)}, u32[]{:S(2)}) %all-to-all-start.7) | async-done | bytes 1056 | tf_op jit(solution)/shard_map/all_to_all | solution.py:105
  73.2 4.5 all-to-all-start.9
  79.0 8.1 %all-to-all-done.9 = f32[1,4,64]{1,0,2:T(1,128)S(1)} async-done(((f32[1,4,64]{1,0,2:T(1,128)}), f32[1,4,64]{1,0,2:T(1,128)S(1)}, u32[]{:S(2)}, u32[]{:S(2)}) %all-to-all-start.9) | async-done | bytes 1056 | tf_op jit(solution)/shard_map/all_to_all | solution.py:106
  87.2 4.6 all-to-all-start.2
  97.4 1.4 copy.115
  98.8 2.5 all-to-all-done.2
  101.3 7.8 %all-to-all-start = ((f32[1,4,64]{1,0,2:T(1,128)}), f32[1,4,64]{1,0,2:T(1,128)S(1)}, u32[]{:S(2)}, u32[]{:S(2)}) async-start(f32[1,4,64]{1,0,2:T(1,128)} %copy.115), calls=%async_computation | async-start | bytes 65536 | tf_op jit(solution)/shard_map/all_to_all | solution.py:105
  109.1 1.3 convolution_bitcast_fusion.2
  111.5 7.0 %all-to-all-done = f32[1,4,64]{1,0,2:T(1,128)S(1)} async-done(((f32[1,4,64]{1,0,2:T(1,128)}), f32[1,4,64]{1,0,2:T(1,128)S(1)}, u32[]{:S(2)}, u32[]{:S(2)}) %all-to-all-start) | async-done | bytes 1056 | tf_op jit(solution)/shard_map/all_to_all | solution.py:105
  118.6 5.5 all-to-all-start.8
  130.0 11.1 %all-to-all-done.8 = f32[1,4,64,512]{3,1,0,2:T(4,128)} async-done(((f32[1,4,64,512]{3,1,0,2:T(4,128)}), f32[1,4,64,512]{3,1,0,2:T(4,128)}, u32[]{:S(2)}, u32[]{:S(2)}) %all-to-all-start.8) | async-done | bytes 524320 | tf_op jit(solution)/shard_map/all_to_all | solution.py:107
  141.1 6.4 %all-to-all-start.1 = ((f32[1,4,64,512]{3,1,0,2:T(4,128)}), f32[1,4,64,512]{3,1,0,2:T(4,128)S(1)}, u32[]{:S(2)}, u32[]{:S(2)}) async-start(f32[1,4,64,512]{3,1,0,2:T(4,128)} %copy.116), calls=%async_computation.1 | async-start | bytes 1048576 | tf_op jit(solution)/shard_map/all_to_all | solution.py:107
  148.9 4.2 convolution_bitcast_fusion
  153.3 11.4 %all-to-all-done.1 = f32[1,4,64,512]{3,1,0,2:T(4,128)S(1)} async-done(((f32[1,4,64,512]{3,1,0,2:T(4,128)}), f32[1,4,64,512]{3,1,0,2:T(4,128)S(1)}, u32[]{:S(2)}, u32[]{:S(2)}) %all-to-all-start.1) | async-done | bytes 524320 | tf_op jit(solution)/shard_map/all_to_all | solution.py:107
  164.9 4.2 convolution_bitcast_fusion.1
  169.1 128.2 %reduce-scatter.9.cloned.1.call-done = f32[112,4]{1,0:T(8,128)} async-done(((f32[7168,4]{1,0:T(8,128)}), f32[112,4]{1,0:T(8,128)}) %reduce-scatter.9.cloned.1.call-update) | async-done | bytes 1808
  299.2 3.3 all-to-all-start.10
  302.5 140.8 %reduce-scatter.7.cloned.1.call-done = f32[112,4]{1,0:T(8,128)} async-done(((f32[7168,4]{1,0:T(8,128)}), f32[112,4]{1,0:T(8,128)}) %reduce-scatter.7.cloned.1.call-update) | async-done | bytes 1808
  445.1 3.3 all-to-all-start.3
  449.2 3.6 all-to-all-done.3
  452.8 7.4 %all-to-all-start.11 = ((bf16[1,64,6,112]{3,2,0,1:T(8,128)(2,1)}), bf16[1,64,6,112]{3,2,0,1:T(8,128)(2,1)S(1)}, u32[]{:S(2)}, u32[]{:S(2)}) async-start(bf16[1,64,6,112]{3,2,0,1:T(8,128)(2,1)} %copy.132), calls=%async_computation.11 | async-start | bytes 262144 | tf_op jit(solution)/shard_map/all_to_all | solution.py:146
  461.0 9.5 %all-to-all-done.11 = bf16[1,64,6,112]{3,2,0,1:T(8,128)(2,1)S(1)} async-done(((bf16[1,64,6,112]{3,2,0,1:T(8,128)(2,1)}), bf16[1,64,6,112]{3,2,0,1:T(8,128)(2,1)S(1)}, u32[]{:S(2)}, u32[]{:S(2)}) %all-to-all-start.11) | async-done | bytes 86048 | tf_op jit(solution)/shard_map/all_to_all | solution.py:146
  470.4 4.9 all-to-all-start.4
  475.6 10.1 %all-to-all-done.4 = bf16[1,64,6,112]{3,2,0,1:T(8,128)(2,1)S(1)} async-done(((bf16[1,64,6,112]{3,2,0,1:T(8,128)(2,1)}), bf16[1,64,6,112]{3,2,0,1:T(8,128)(2,1)S(1)}, u32[]{:S(2)}, u32[]{:S(2)}) %all-to-all-start.4) | async-done | bytes 86048 | tf_op jit(solution)/shard_map/all_to_all | solution.py:146
  486.3 1.8 fusion.10
  488.1 2.2 fusion
  492.7 3.3 all-to-all-start.5
  496.3 1.8 fusion.8
  498.2 2.2 fusion.1
  502.3 3.3 all-to-all-start.12
  506.2 6.1 %copy.123 = bf16[2,1,3,7168]{2,0,1,3:T(2,128)(2,1)} copy(bf16[2,1,3,7168]{3,2,0,1:T(4,128)(2,1)S(1)} %all_to_all.173) | data formatting | bytes 172032 | tf_op jit(solution)/shard_map/all_to_all | solution.py:162
  512.3 8.7 %reshape.577 = bf16[64,2,336]{2,1,0:T(2,128)(2,1)} reshape(bf16[7168,1,2,3]{3,2,1,0:T(2,128)(2,1)} %bitcast.287) | data formatting | bytes 172032
  521.0 5.2 all-to-all-start.6
  526.8 6.1 %copy.136 = bf16[2,1,3,7168]{2,0,1,3:T(2,128)(2,1)} copy(bf16[2,1,3,7168]{3,2,0,1:T(4,128)(2,1)S(1)} %all_to_all.194) | data formatting | bytes 172032 | tf_op jit(solution)/shard_map/all_to_all | solution.py:162
  532.9 8.7 %reshape.581 = bf16[64,2,336]{2,1,0:T(2,128)(2,1)} reshape(bf16[7168,1,2,3]{3,2,1,0:T(2,128)(2,1)} %bitcast.288) | data formatting | bytes 172032
  541.6 10.3 %all-to-all-start.13 = ((bf16[64,2,336]{2,1,0:T(2,128)(2,1)}), bf16[64,2,336]{2,1,0:T(2,128)(2,1)S(1)}, u32[]{:S(2)}, u32[]{:S(2)}) async-start(bf16[64,2,336]{2,1,0:T(2,128)(2,1)} %reshape.581), calls=%async_computation.13 | async-start | bytes 196608 | tf_op jit(solution)/shard_map/all_to_all | solution.py:161
  552.3 5.5 reshape.578
  557.7 7.6 %copy.124 = bf16[2,1,3,7168]{3,0,2,1:T(2,128)(2,1)S(1)} copy(bf16[2,1,3,7168]{2,0,1,3:T(2,128)(2,1)} %bitcast.289) | data formatting | bytes 172032 | tf_op jit(solution)/shard_map/all_to_all | solution.py:161
  565.6 5.5 reshape.582
  571.0 7.6 %copy.137 = bf16[2,1,3,7168]{3,0,2,1:T(2,128)(2,1)S(1)} copy(bf16[2,1,3,7168]{2,0,1,3:T(2,128)(2,1)} %bitcast.290) | data formatting | bytes 172032 | tf_op jit(solution)/shard_map/all_to_all | solution.py:161
  (148 shorter events, 38.4 us)
Async XLA Ops:
  6.5 481.6 %copy-start = (bf16[1,128,7168]{2,1,0:T(8,128)(2,1)S(1)}, bf16[1,128,7168]{2,1,0:T(8,128)(2,1)}, u32[]{:S(2)}) copy-start(bf16[1,128,7168]{2,1,0:T(8,128)(2,1)} %param.27) | copy-start | bytes 5505028
  6.5 39.3 %collective-permute-start = (bf16[20,64,576]{2,1,0:T(8,128)(2,1)}, bf16[20,64,576]{2,1,0:T(8,128)(2,1)S(1)}, u32[]{:S(2)}, u32[]{:S(2)}) collective-permute-start(bf16[20,64,576]{2,1,0:T(8,128)(2,1)} %bitcast.315), channel_id=1, source_target_pairs={{0,128},{128,0},{1,129},{129,1},{2,130},{130,2},{3,131},{131,3},{4... | collective-permute-start | bytes 4423688 | tf_op jit(solution)/shard_map/ppermute | solution.py:18
  15.2 48.5 %copy-start.8 = (pred[4,256]{1,0:T(4,128)(4,1)}, pred[4,256]{1,0:T(4,128)(4,1)S(1)}, u32[]{:S(2)}) copy-start(pred[4,256]{1,0:T(4,128)(4,1)S(1)} %broadcast_compare_fusion) | copy-start | bytes 3076
  47.6 1.6 copy-start.1
  50.4 36.8 %copy-start.6 = (f32[4,64]{1,0:T(4,128)}, f32[4,64]{1,0:T(4,128)S(1)}, u32[]{:S(2)}) copy-start(f32[4,64]{1,0:T(4,128)S(1)} %get-tuple-element.32) | copy-start | bytes 3076
  50.4 27.3 %copy-start.3 = (bf16[2,1,1,4,576]{4,3,2,1,0:T(4,128)(2,1)S(1)}, bf16[2,1,1,4,576]{4,3,2,1,0:T(4,128)(2,1)}, u32[]{:S(2)}) copy-start(bf16[2,1,1,4,576]{4,3,2,1,0:T(4,128)(2,1)} %param.18) | copy-start | bytes 27652
  51.0 36.1 %copy-start.5 = (f32[4,64]{1,0:T(4,128)}, f32[4,64]{1,0:T(4,128)S(1)}, u32[]{:S(2)}) copy-start(f32[4,64]{1,0:T(4,128)S(1)} %get-tuple-element.30) | copy-start | bytes 3076
  51.7 21.4 %all-to-all-start.7 = ((f32[1,4,64]{1,0,2:T(1,128)}), f32[1,4,64]{1,0,2:T(1,128)S(1)}, u32[]{:S(2)}, u32[]{:S(2)}) async-start(f32[1,4,64]{1,0,2:T(1,128)} %copy.127), calls=%async_computation.7 | async-start | bytes 65536 | tf_op jit(solution)/shard_map/all_to_all | solution.py:105
  73.2 14.0 %all-to-all-start.9 = ((f32[1,4,64]{1,0,2:T(1,128)}), f32[1,4,64]{1,0,2:T(1,128)S(1)}, u32[]{:S(2)}, u32[]{:S(2)}) async-start(f32[1,4,64]{1,0,2:T(1,128)} %copy.129), calls=%async_computation.9 | async-start | bytes 65536 | tf_op jit(solution)/shard_map/all_to_all | solution.py:106
  87.2 14.1 %all-to-all-start.2 = ((f32[1,4,64]{1,0,2:T(1,128)}), f32[1,4,64]{1,0,2:T(1,128)S(1)}, u32[]{:S(2)}, u32[]{:S(2)}) async-start(f32[1,4,64]{1,0,2:T(1,128)} %copy.117), calls=%async_computation.2 | async-start | bytes 65536 | tf_op jit(solution)/shard_map/all_to_all | solution.py:106
  91.8 0.6 copy-start.17
  101.3 17.3 %all-to-all-start = ((f32[1,4,64]{1,0,2:T(1,128)}), f32[1,4,64]{1,0,2:T(1,128)S(1)}, u32[]{:S(2)}, u32[]{:S(2)}) async-start(f32[1,4,64]{1,0,2:T(1,128)} %copy.115), calls=%async_computation | async-start | bytes 65536 | tf_op jit(solution)/shard_map/all_to_all | solution.py:105
  118.6 22.5 %all-to-all-start.8 = ((f32[1,4,64,512]{3,1,0,2:T(4,128)}), f32[1,4,64,512]{3,1,0,2:T(4,128)}, u32[]{:S(2)}, u32[]{:S(2)}) async-start(f32[1,4,64,512]{3,1,0,2:T(4,128)} %copy.128), calls=%async_computation.8 | async-start | bytes 1048576 | tf_op jit(solution)/shard_map/all_to_all | solution.py:107
  126.3 21.3 %copy-start.19 = (f32[4]{0:T(128)S(1)}, f32[4]{0:T(128)}, u32[]{:S(2)}) copy-start(f32[4]{0:T(128)} %fusion.72) | copy-start | bytes 52
  126.3 22.6 %copy-start.2 = (bf16[1,512,128]{2,1,0:T(8,128)(2,1)S(1)}, bf16[1,512,128]{2,1,0:T(8,128)(2,1)}, u32[]{:S(2)}) copy-start(bf16[1,512,128]{2,1,0:T(8,128)(2,1)} %param.23) | copy-start | bytes 393220
  141.1 23.6 %all-to-all-start.1 = ((f32[1,4,64,512]{3,1,0,2:T(4,128)}), f32[1,4,64,512]{3,1,0,2:T(4,128)S(1)}, u32[]{:S(2)}, u32[]{:S(2)}) async-start(f32[1,4,64,512]{3,1,0,2:T(4,128)} %copy.116), calls=%async_computation.1 | async-start | bytes 1048576 | tf_op jit(solution)/shard_map/all_to_all | solution.py:107
  147.5 149.8 %reduce-scatter.9.cloned.1.call-start = ((), (), s32[]{:S(2)}) async-start(), calls=%async_computation.17 | async-start | bytes 3727360
  153.1 11.8 %copy-start.7 = (bf16[1,4,576]{2,1,0:T(4,128)(2,1)S(1)}, bf16[1,4,576]{2,1,0:T(4,128)(2,1)}, u32[]{:S(2)}) copy-start(bf16[1,4,576]{2,1,0:T(4,128)(2,1)} %slice_bitcast_fusion.3) | copy-start | bytes 13828
  153.1 290.2 %reduce-scatter.7.cloned.1.call-start = ((), (), s32[]{:S(2)}) async-start(), calls=%async_computation.16 | async-start | bytes 3727360
  169.1 129.2 %copy-start.9 = (bf16[2,1,1,4,112]{4,3,2,1,0:T(4,128)(2,1)S(1)}, bf16[2,1,1,4,112]{4,3,2,1,0:T(4,128)(2,1)}, u32[]{:S(2)}) copy-start(bf16[2,1,1,4,112]{4,3,2,1,0:T(4,128)(2,1)} %param.19) | copy-start | bytes 5380
  169.1 129.2 %copy-start.11 = (f32[4,48]{1,0:T(4,128)S(1)}, f32[4,48]{1,0:T(4,128)}, u32[]{:S(2)}) copy-start(f32[4,48]{1,0:T(4,128)} %eq.96) | copy-start | bytes 2308
  169.1 129.2 %copy-start.14 = (f32[48]{0:T(128)S(1)}, f32[48]{0:T(128)}, u32[]{:S(2)}) copy-start(f32[48]{0:T(128)} %eq.87) | copy-start | bytes 580
  169.1 129.2 %copy-start.16 = (bf16[4,48]{1,0:T(4,128)(2,1)S(1)}, bf16[4,48]{1,0:T(4,128)(2,1)}, u32[]{:S(2)}) copy-start(bf16[4,48]{1,0:T(4,128)(2,1)} %mul.275) | copy-start | bytes 1156
  169.1 275.1 %copy-start.10 = (f32[4,48]{1,0:T(4,128)S(1)}, f32[4,48]{1,0:T(4,128)}, u32[]{:S(2)}) copy-start(f32[4,48]{1,0:T(4,128)} %eq.85) | copy-start | bytes 2308
  169.1 275.1 %copy-start.15 = (bf16[4,48]{1,0:T(4,128)(2,1)S(1)}, bf16[4,48]{1,0:T(4,128)(2,1)}, u32[]{:S(2)}) copy-start(bf16[4,48]{1,0:T(4,128)(2,1)} %mul.250) | copy-start | bytes 1156
  169.1 291.0 %copy-start.4 = (f32[7168]{0:T(1024)S(1)}, f32[7168]{0:T(1024)}, u32[]{:S(2)}) copy-start(f32[7168]{0:T(1024)} %param.22) | copy-start | bytes 86020
  299.2 146.0 %all-to-all-start.10 = ((bf16[2,64,3,112]{3,1,2,0:T(8,128)(2,1)}), bf16[2,64,3,112]{3,1,2,0:T(8,128)(2,1)S(1)}, u32[]{:S(2)}, u32[]{:S(2)}) async-start(bf16[2,64,3,112]{3,1,2,0:T(8,128)(2,1)} %copy.131), calls=%async_computation.10 | async-start | bytes 196608 | tf_op jit(solution)/shard_map/all_to_all | solution.py:147
  445.1 7.6 %all-to-all-start.3 = ((bf16[2,64,3,112]{3,1,2,0:T(8,128)(2,1)}), bf16[2,64,3,112]{3,1,2,0:T(8,128)(2,1)S(1)}, u32[]{:S(2)}, u32[]{:S(2)}) async-start(bf16[2,64,3,112]{3,1,2,0:T(8,128)(2,1)} %copy.119), calls=%async_computation.3 | async-start | bytes 196608 | tf_op jit(solution)/shard_map/all_to_all | solution.py:147
  452.8 17.7 %all-to-all-start.11 = ((bf16[1,64,6,112]{3,2,0,1:T(8,128)(2,1)}), bf16[1,64,6,112]{3,2,0,1:T(8,128)(2,1)S(1)}, u32[]{:S(2)}, u32[]{:S(2)}) async-start(bf16[1,64,6,112]{3,2,0,1:T(8,128)(2,1)} %copy.132), calls=%async_computation.11 | async-start | bytes 262144 | tf_op jit(solution)/shard_map/all_to_all | solution.py:146
  470.4 15.2 %all-to-all-start.4 = ((bf16[1,64,6,112]{3,2,0,1:T(8,128)(2,1)}), bf16[1,64,6,112]{3,2,0,1:T(8,128)(2,1)S(1)}, u32[]{:S(2)}, u32[]{:S(2)}) async-start(bf16[1,64,6,112]{3,2,0,1:T(8,128)(2,1)} %copy.120), calls=%async_computation.4 | async-start | bytes 262144 | tf_op jit(solution)/shard_map/all_to_all | solution.py:146
  492.7 9.5 %all-to-all-start.5 = ((bf16[2,2,10752]{2,1,0:T(2,128)(2,1)}), bf16[2,2,10752]{2,1,0:T(2,128)(2,1)S(1)}, u32[]{:S(2)}, u32[]{:S(2)}) async-start(bf16[2,2,10752]{2,1,0:T(2,128)(2,1)} %reshape.575), calls=%async_computation.5 | async-start | bytes 172032 | tf_op jit(solution)/shard_map/all_to_all | solution.py:162
  502.3 18.7 %all-to-all-start.12 = ((bf16[2,2,10752]{2,1,0:T(2,128)(2,1)}), bf16[2,2,10752]{2,1,0:T(2,128)(2,1)S(1)}, u32[]{:S(2)}, u32[]{:S(2)}) async-start(bf16[2,2,10752]{2,1,0:T(2,128)(2,1)} %reshape.579), calls=%async_computation.12 | async-start | bytes 172032 | tf_op jit(solution)/shard_map/all_to_all | solution.py:162
  521.0 20.6 %all-to-all-start.6 = ((bf16[64,2,336]{2,1,0:T(2,128)(2,1)}), bf16[64,2,336]{2,1,0:T(2,128)(2,1)S(1)}, u32[]{:S(2)}, u32[]{:S(2)}) async-start(bf16[64,2,336]{2,1,0:T(2,128)(2,1)} %reshape.577), calls=%async_computation.6 | async-start | bytes 196608 | tf_op jit(solution)/shard_map/all_to_all | solution.py:161
  532.9 19.0 %copy-start.12 = (f32[4,16]{1,0:T(4,128)S(1)}, f32[4,16]{1,0:T(4,128)}, u32[]{:S(2)}) copy-start(f32[4,16]{1,0:T(4,128)} %get-tuple-element.8) | copy-start | bytes 772
  532.9 19.0 %copy-start.13 = (f32[4,16]{1,0:T(4,128)S(1)}, f32[4,16]{1,0:T(4,128)}, u32[]{:S(2)}) copy-start(f32[4,16]{1,0:T(4,128)} %get-tuple-element.34) | copy-start | bytes 772
  532.9 19.0 %copy-start.18 = (f32[3]{0:T(128)S(1)}, f32[3]{0:T(128)}, u32[]{:S(2)}) copy-start(f32[3]{0:T(128)} %copy-done.17) | copy-start | bytes 40
  541.6 23.9 %all-to-all-start.13 = ((bf16[64,2,336]{2,1,0:T(2,128)(2,1)}), bf16[64,2,336]{2,1,0:T(2,128)(2,1)S(1)}, u32[]{:S(2)}, u32[]{:S(2)}) async-start(bf16[64,2,336]{2,1,0:T(2,128)(2,1)} %reshape.581), calls=%async_computation.13 | async-start | bytes 196608 | tf_op jit(solution)/shard_map/all_to_all | solution.py:161
Sparse Core Ops, SparseCore 0:
  153.2 144.1 reduce-scatter.8
  302.1 141.2 reduce-scatter.6
where the time goes:
time: 590 us; the launch traced here: 587 us
  waiting for transfers between devices  368 us (62%)
  starting transfers between devices  84.2 us (14%)
  local copies, waits for them, and re-layouts  83.9 us (14%)
  matrix products  23.9 us (4%)
  between operations  14 us (2%)
  other arithmetic  13.3 us (2%)
    unnamed x4, waiting for transfers between devices  269 us
    unnamed x51, local copies, waits for them, and re-layouts  32.2 us
    ppermute x1, waiting for transfers between devices, swapped(): return lax.ppermute(value, axis, pairs)  27.6 us
    all_to_all x2, waiting for transfers between devices, body(): lax.all_to_all(summed[None], 'expert', split_axis=2, concat_axis=0, tiled...  22.5 us
    all_to_all x2, starting transfers between devices, body(): lax.all_to_all(maximum[None], 'expert', split_axis=2, concat_axis=0, tile...  19.7 us
    all_to_all x2, waiting for transfers between devices, body(): lax.all_to_all(lax.all_to_all(outgoing, 'dp', split_axis=0, concat_axis=2...  19.6 us
    all_to_all x2, starting transfers between devices, body(): lax.all_to_all(lax.all_to_all(expert_part[None, None].astype(jnp.bfloat16...  15.5 us
    all_to_all x2, local copies, waits for them, and re-layouts, body(): lax.all_to_all(lax.all_to_all(expert_part[None, None].astype(jnp.bfloat16...  15.3 us
  transfers between devices with their start and end apart: 17, of which 12 were waited for; matrix products, arithmetic and copies ran while one was open for 16% of the time, Pallas kernels for 0%

commit v1 on v0

v1 whole, which is shorter than its diff:
```python
import jax
import jax.numpy as jnp
from jax import lax
from jax.experimental import pallas as pl
from jax.experimental.pallas import tpu as pltpu
from jax.sharding import Mesh, PartitionSpec as P

SCORE_SCALE = 192.0 ** (-0.5)
EPSILON = 1e-06
MASK_VALUE = -1e30
SLICES = 8
CHIPS = 32
HALF = 3584
CHUNKS = 28
BLOCK = 112
XZ = ("x", "z")
DXZ = ("dp", "x", "z")
bf16 = jnp.bfloat16
f32 = jnp.float32


def swap(value, axis):
    return lax.ppermute(value, axis, [(0, 1), (1, 0)])


def exchange(value, axes):
    return lax.all_to_all(value, axes, 0, 0, tiled=True)


def pieces(value):
    first = value.astype(bf16)
    rest = value - first.astype(f32)
    second = rest.astype(bf16)
    third = (rest - second.astype(f32)).astype(bf16)
    return first, second, third


VM = pl.BlockSpec(memory_space=pltpu.VMEM)
SM = pl.BlockSpec(memory_space=pltpu.SMEM)
LIMIT = 32 * 1024 * 1024


def pick_kernel(ids, queries, out):
    row = lax.broadcasted_iota(jnp.int32, (32, 64), 0)
    col = lax.broadcasted_iota(jnp.int32, (32, 64), 1)
    wanted = jnp.where(col == 2 * row + ids[0], 1.0, 0.0).astype(bf16)
    for i in range(8):
        out[i] = jnp.dot(wanted, queries[i], preferred_element_type=f32).astype(bf16)


def pick_heads(ids, queries):
    return pl.pallas_call(
        pick_kernel,
        out_shape=jax.ShapeDtypeStruct((8, 32, 576), bf16),
        in_specs=[SM, VM],
        out_specs=VM,
        compiler_params=pltpu.CompilerParams(vmem_limit_bytes=LIMIT),
        cost_estimate=pl.CostEstimate(flops=19000000, bytes_accessed=900000, transcendentals=0),
    )(ids, queries)


def attention_kernel(ids, table, table_other, lengths, q, pool, pool_other, out, scratch):
    wanted = ids[1]
    place = ids[2]
    lane = lax.broadcasted_iota(jnp.int32, (1, 512), 1)
    start = jnp.where(lane < 256, place * 256, ((place + 1 - 2 * ids[0]) - 1) * 256)
    places = start + lane
    slot = lax.broadcasted_iota(jnp.int32, (32, 128), 1)
    for r in range(4):
        blocks = [pool[table[wanted, r, j]] for j in range(4)]
        blocks += [pool_other[table_other[wanted, r, j]] for j in range(4)]
        keys = jnp.concatenate(blocks, axis=0)
        asked = jnp.concatenate([q[r], q[4 + r]], axis=0)
        scores = lax.dot_general(
            asked, keys, (((1,), (1,)), ((), ())), preferred_element_type=f32
        )
        usable = places < lengths[r]
        scores = jnp.where(usable, scores * SCORE_SCALE, MASK_VALUE)
        top = jnp.max(scores, axis=1, keepdims=True)
        weights = jnp.where(usable, jnp.exp(scores - top), 0.0)
        total = jnp.sum(weights, axis=1, keepdims=True)
        summed = jnp.dot(weights.astype(bf16), keys[:, :512], preferred_element_type=f32)
        live = total > 0.0
        safe = jnp.where(live, total, 1.0)
        level = jnp.where(live, top + jnp.log(safe), MASK_VALUE)
        value = summed * (1.0 / safe)
        first = level.astype(bf16).astype(f32)
        second = (level - first).astype(bf16).astype(f32)
        third = (level - first) - second
        for s in range(2):
            rows = slice(32 * s, 32 * s + 32)
            tail = jnp.where(
                slot == 0,
                first[rows],
                jnp.where(slot == 1, second[rows], jnp.where(slot == 2, third[rows], 0.0)),
            )
            for k in range(5):
                part = value[rows, 128 * k : 128 * k + 128] if k < 4 else tail
                scratch[k, pl.ds(4 * s + r, 32, stride=8), :] = part
    for k in range(5):
        out[:, :, 128 * k : 128 * k + 128] = scratch[k].reshape(32, 8, 128).astype(bf16)


def attend(ids, table, table_other, lengths, q, pool, pool_other):
    return pl.pallas_call(
        attention_kernel,
        out_shape=jax.ShapeDtypeStruct((32, 8, 640), bf16),
        in_specs=[SM, SM, SM, SM, VM, VM, VM],
        out_specs=VM,
        scratch_shapes=[pltpu.VMEM((5, 256, 128), f32)],
        compiler_params=pltpu.CompilerParams(vmem_limit_bytes=LIMIT),
        cost_estimate=pl.CostEstimate(
            flops=300000000, bytes_accessed=4000000, transcendentals=131072
        ),
    )(ids, table, table_other, lengths, q, pool, pool_other)


def body(
    prompt_pool,
    block_table,
    cache_len,
    queries,
    fresh_latent,
    x_in,
    routes,
    gates,
    norm_gain,
    value_up,
    out_proj,
    w_gate,
    w_up,
    w_down,
):
    role = lax.axis_index("role")
    dp = lax.axis_index("dp")
    core = lax.axis_index("core")
    chip = lax.axis_index("x") * lax.axis_size("z") + lax.axis_index("z")
    place = chip * 2 + core
    ids = jnp.stack([core, 1 - role, place]).astype(jnp.int32)
    q = swap(pick_heads(ids, queries.reshape(8, 64, 576)), "role")
    fresh = swap(fresh_latent.reshape(2, 4, 576), "role")
    x_here = swap(x_in.reshape(8, BLOCK), "role")
    routes_now = swap(routes.reshape(8, 8), "role")
    gates_now = swap(gates.reshape(8, 8), "role")
    lengths = swap(cache_len.reshape(4), "role")
    pool = prompt_pool[0, 0, 0]
    pool_other = swap(pool, "core")
    table = block_table[:, 0, 0]
    table_other = swap(table, "core")
    x_other = swap(x_here, "core")
    proj_other = swap(
        lax.dynamic_slice_in_dim(out_proj, (1 - core) * HALF, HALF, 1), "core"
    )
    proj_mine = lax.dynamic_slice_in_dim(out_proj, core * HALF, HALF, 1)
    down_mine = w_down[0]
    down_other = swap(down_mine, "core")
    sent = attend(ids, table, table_other, lengths, q, pool, pool_other)
    got = exchange(sent, XZ)
    levels = jnp.sum(got[:, :, 512:515].astype(f32), axis=2, keepdims=True)
    q_mine = lax.dynamic_index_in_dim(q, chip, 1, keepdims=False).reshape(2, 4, 576)
    fresh_scores = (
        jnp.einsum("sqc,tqc->sqt", q_mine, fresh, preferred_element_type=f32) * SCORE_SCALE
    )
    fresh_usable = (jnp.arange(2)[None, :] <= jnp.arange(2)[:, None])[:, None, :]
    fresh_scores = jnp.where(fresh_usable, fresh_scores, MASK_VALUE)
    highest = jnp.maximum(
        jnp.max(levels, axis=0).reshape(2, 4, 1), jnp.max(fresh_scores, axis=2, keepdims=True)
    )
    factors = jnp.exp(levels - highest.reshape(1, 8, 1))
    fresh_weights = jnp.where(fresh_usable, jnp.exp(fresh_scores - highest), 0.0)
    numerator = jnp.sum(factors * got[:, :, :512].astype(f32), axis=0).reshape(2, 4, 512)
    numerator = numerator + jnp.einsum(
        "sqt,tqc->sqc", fresh_weights.astype(bf16), fresh[:, :, :512], preferred_element_type=f32
    )
    denominator = jnp.sum(factors, axis=0).reshape(2, 4, 1) + jnp.sum(
        fresh_weights, axis=2, keepdims=True
    )
    context = (numerator / denominator).astype(bf16).reshape(8, 512)
    head_vals = jnp.dot(context, value_up[0], preferred_element_type=f32).astype(bf16)
    vals_other = swap(head_vals, "core")
    base = jnp.zeros((8, 2 * HALF), bf16)
    base = lax.dynamic_update_slice_in_dim(base, x_here, place * BLOCK, 1)
    base = lax.dynamic_update_slice_in_dim(base, x_other, (place + 1 - 2 * core) * BLOCK, 1)
    base = lax.dynamic_slice_in_dim(base, core * HALF, HALF, 1)
    partial = (
        base.astype(f32)
        + jnp.dot(head_vals, proj_mine, preferred_element_type=f32)
        + jnp.dot(vals_other, proj_other, preferred_element_type=f32)
    ).astype(bf16)
    partial = jnp.pad(partial.reshape(8, CHUNKS, 128).transpose(1, 0, 2), ((0, 4), (0, 0), (0, 0)))
    resid_piece = jnp.sum(exchange(partial, XZ).astype(f32), axis=0).astype(bf16)
    rows_half = exchange(jnp.broadcast_to(resid_piece[None], (64, 8, 128)), DXZ)
    rows_other = swap(rows_half, "core")
    first = jnp.where(core == 0, rows_half, rows_other)
    second = jnp.where(core == 0, rows_other, rows_half)
    rows = jnp.stack([first, second]).reshape(2, 2, 32, 8, 128)[:, :, :CHUNKS]
    rows = rows.transpose(1, 3, 0, 2, 4).reshape(16, 2 * HALF)
    flat = rows.astype(f32)
    normed = (
        flat * lax.rsqrt(jnp.mean(flat * flat, axis=1, keepdims=True) + EPSILON) * norm_gain
    ).astype(bf16)
    gate_part = jnp.dot(normed, w_gate[0], preferred_element_type=f32)
    up_part = jnp.dot(normed, w_up[0], preferred_element_type=f32)
    hidden = (jax.nn.silu(gate_part) * up_part).astype(bf16)
    hidden_other = swap(hidden, "core")
    out_rows = jnp.dot(hidden, down_mine, preferred_element_type=f32) + jnp.dot(
        hidden_other, down_other, preferred_element_type=f32
    )
    expert = dp * 8 + chip // 4
    mixing_mine = jnp.sum(jnp.where(routes_now == expert, gates_now, 0.0), axis=1, keepdims=True)
    mixing_theirs = swap(
        jnp.sum(jnp.where(routes_now == (1 - dp) * 8 + chip // 4, gates_now, 0.0), axis=1, keepdims=True),
        "dp",
    )
    mixing = jnp.where(
        dp == 0,
        jnp.concatenate([mixing_mine, mixing_theirs]),
        jnp.concatenate([mixing_theirs, mixing_mine]),
    )
    out_rows = (out_rows * mixing).astype(bf16)
    outgoing = lax.dynamic_index_in_dim(out_rows.reshape(2, 8, 32, 2, BLOCK), core, 3, keepdims=False)
    outgoing = outgoing.transpose(0, 2, 1, 3).reshape(64, 8, BLOCK)
    back = jnp.sum(exchange(outgoing, DXZ).astype(f32), axis=0)
    own_rows = lax.dynamic_slice_in_dim(rows, dp * 8, 8, 0)
    own = lax.dynamic_slice_in_dim(own_rows, place * BLOCK, BLOCK, 1).astype(f32)
    done = swap((own + back).astype(bf16), "role")
    return done.reshape(2, 1, 1, 4, BLOCK)


def solution(mesh):
    split = Mesh(mesh.devices.reshape(2, 2, 4, 8, 2), ("role", "dp", "x", "z", "core"))
    e = ("x", "z", "core")
    slab = ("dp", "x", "z", "core")
    placed = (
        P("role", "dp", e, None, None, None),
        P(None, "dp", e, None, None),
        P("role", "dp", None),
        P(None, "role", "dp", None, None, None),
        P(None, "role", "dp", None, None),
        P(None, "role", "dp", None, e),
        P(None, "role", "dp", None, None),
        P(None, "role", "dp", None, None),
        P(),
        P(e, None, None),
        P(e, None),
        P(slab, None, None),
        P(slab, None, None),
        P(slab, None, None),
    )
    return jax.shard_map(
        body,
        mesh=split,
        in_specs=placed,
        out_specs=P(None, "role", "dp", None, e),
        check_vma=False,
    )
```

time: 590 us -> 118 us (0.20)
  waiting for transfers between devices: 368 us -> 43 us
  local copies, waits for them, and re-layouts: 83.9 us -> 10.9 us
  starting transfers between devices: 84.2 us -> 36.9 us
  matrix products: 23.9 us -> 5.39 us
  blocking collectives: 0 us -> 14.7 us
  between operations: 14 us -> 0.31 us
  other arithmetic: 13.3 us -> 1.42 us
    unnamed x4 -> x0, waiting for transfers between devices: 269 us -> none
    all_to_all x14 -> x3, starting transfers between devices: 81.8 us -> 23.4 us  [exchange(): return lax.all_to_all(value, axes, 0, 0, tiled=True)]
    all_to_all x14 -> x3, waiting for transfers between devices: 71 us -> 26.9 us  [exchange(): return lax.all_to_all(value, axes, 0, 0, tiled=True)]
    all_to_all x10 -> x0, local copies, waits for them, and re-layouts: 30.1 us -> none  [the longest x2 15.3 us: body(): lax.all_to_all(lax.all_to_all(expert_part[None, None].astype(jnp.bfloat16...]
    unnamed x51 -> x26, local copies, waits for them, and re-layouts: 32.2 us -> 5.55 us
    all_to_all x0 -> x1, blocking collectives: none -> 14.7 us  [exchange(): return lax.all_to_all(value, axes, 0, 0, tiled=True)]
    ppermute x1 -> x16, waiting for transfers between devices: 27.6 us -> 16.1 us  [swap(): return lax.ppermute(value, axis, [(0, 1), (1, 0)])]
    ppermute x1 -> x16, starting transfers between devices: 2.07 us -> 13.5 us  [swap(): return lax.ppermute(value, axis, [(0, 1), (1, 0)])]
  transfers between devices with their start and end apart: 17 -> 19, of which waited for: 12 -> 9; matrix products, arithmetic and copies ran while one was open for 16% -> 7% of each run, Pallas kernels for 0% -> 4%
where the time goes in v1:
time: 118 us; the launch traced here: 117 us
  waiting for transfers between devices  43 us (36%)
  starting transfers between devices  36.9 us (31%)
  blocking collectives  14.7 us (12%)
  local copies, waits for them, and re-layouts  10.9 us (9%)
  matrix products  5.39 us (5%)
  Pallas kernels  4.57 us (4%)
  other arithmetic  1.42 us (1%)
    all_to_all x3, waiting for transfers between devices, exchange(): return lax.all_to_all(value, axes, 0, 0, tiled=True)  26.9 us
    all_to_all x3, starting transfers between devices, exchange(): return lax.all_to_all(value, axes, 0, 0, tiled=True)  23.4 us
    ppermute x16, waiting for transfers between devices, swap(): return lax.ppermute(value, axis, [(0, 1), (1, 0)])  16.1 us
    all_to_all x1, blocking collectives, exchange(): return lax.all_to_all(value, axes, 0, 0, tiled=True)  14.7 us
    ppermute x16, starting transfers between devices, swap(): return lax.ppermute(value, axis, [(0, 1), (1, 0)])  13.5 us
    unnamed x26, local copies, waits for them, and re-layouts  5.55 us
    pallas_call x1, Pallas kernels, attend(): pl.pallas_call(attention_kernel, out_shape=jax.ShapeDtypeStruct((32, 8, 6...  3.07 us
  transfers between devices with their start and end apart: 19, of which 9 were waited for; matrix products, arithmetic and copies ran while one was open for 7% of the time, Pallas kernels for 4%

profile of v1, /device:TPU:16, one launch (start us, length us, event | category | flops | bytes accessed | tf_op | source)
XLA Modules:
  0.0 117.1 jit_solution(4366721672822131827)
XLA Ops:
  0.1 1.2 %copy-done.3 = bf16[2,1,1,4,64,576]{5,4,3,2,1,0:T(8,128)(2,1)S(1)} copy-done((bf16[2,1,1,4,64,576]{5,4,3,2,1,0:T(8,128)(2,1)S(1)}, bf16[2,1,1,4,64,576]{5,4,3,2,1,0:T(8,128)(2,1)}, u32[]{:S(2)}) %copy-start.3) | copy-done | bytes 589848
  1.3 1.5 %shard_map.136 = bf16[8,32,576]{2,1,0:T(8,128)(2,1)} custom-call(s32[3]{0:T(128)S(1)} %pad_add_fusion.ids, bf16[8,64,576]{2,1,0:T(8,128)(2,1)S(1)} %bitcast.77), custom_call_target="tpu_custom_call" | custom-call | flops 19000000 | bytes 900000 | tf_op jit(solution)/shard_map/pallas_call | solution.py:52
  2.8 2.1 %collective-permute-start.4 = (bf16[8,32,576]{2,1,0:T(8,128)(2,1)}, bf16[8,32,576]{2,1,0:T(8,128)(2,1)}, u32[]{:S(2)}, u32[]{:S(2)}) collective-permute-start(bf16[8,32,576]{2,1,0:T(8,128)(2,1)} %shard_map.136), channel_id=1, source_target_pairs={{0,128},{128,0},{1,129},{129,1},{2,130},{130,2},{3,131},{131,3},{4... | collective-permute-start | bytes 884744 | tf_op jit(solution)/shard_map/ppermute | solution.py:23
  5.0 1.5 %collective-permute-start.3 = (s32[4]{0:T(128)}, s32[4]{0:T(128)S(1)}, u32[]{:S(2)}, u32[]{:S(2)}) collective-permute-start(s32[4]{0:T(128)} %bitcast.93), channel_id=1, source_target_pairs={{0,128},{128,0},{1,129},{129,1},{2,130},{130,2},{3,131},{131,3},{4... | collective-permute-start | bytes 56 | tf_op jit(solution)/shard_map/ppermute | solution.py:23
  6.4 0.7 copy.63
  7.1 2.2 %collective-permute-start.6 = (bf16[2,4,576]{2,0,1:T(2,128)(2,1)S(1)}, bf16[2,4,576]{2,0,1:T(2,128)(2,1)S(1)}, u32[]{:S(2)}, u32[]{:S(2)}) collective-permute-start(bf16[2,4,576]{2,0,1:T(2,128)(2,1)S(1)} %bitcast.86), channel_id=1, source_target_pairs={{0,128},{128,0},{1,129},{129,1},{2,130},{130,2},{3,131},{131,3},{4... | collective-permute-start | bytes 27656 | tf_op jit(solution)/shard_map/ppermute | solution.py:23
  9.3 5.4 %collective-permute-done.3.lengths = s32[4]{0:T(128)S(1)} collective-permute-done((s32[4]{0:T(128)}, s32[4]{0:T(128)S(1)}, u32[]{:S(2)}, u32[]{:S(2)}) %collective-permute-start.3) | collective-permute-done | bytes 48 | tf_op jit(solution)/shard_map/ppermute | solution.py:23
  14.7 2.1 %collective-permute-start = (bf16[8,112]{1,0:T(8,128)(2,1)}, bf16[8,112]{1,0:T(8,128)(2,1)S(1)}, u32[]{:S(2)}, u32[]{:S(2)}) collective-permute-start(bf16[8,112]{1,0:T(8,128)(2,1)} %bitcast.92), channel_id=1, source_target_pairs={{0,128},{128,0},{1,129},{129,1},{2,130},{130,2},{3,131},{131,3},{4... | collective-permute-start | bytes 5384 | tf_op jit(solution)/shard_map/ppermute | solution.py:23
  16.8 1.4 %copy-done.1 = bf16[1,1,1,20,64,576]{5,4,3,2,1,0:T(8,128)(2,1)S(1)} copy-done((bf16[1,1,1,20,64,576]{5,4,3,2,1,0:T(8,128)(2,1)S(1)}, bf16[1,1,1,20,64,576]{5,4,3,2,1,0:T(8,128)(2,1)}, u32[]{:S(2)}) %copy-start.1) | copy-done | bytes 1474584
  18.3 0.7 copy-done.4
  18.9 3.1 %shard_map.137 = bf16[32,8,640]{2,1,0:T(8,128)(2,1)S(1)} custom-call(s32[3]{0:T(128)S(1)} %pad_add_fusion.ids, s32[2,4,4]{2,1,0:T(4,128)S(1)} %bitcast.79, s32[2,4,4]{2,1,0:T(4,128)S(1)} %collective-permute-done.2.table_other, s32[4]{0:T(128)S(1)} %collective-permute-done.3.lengths, bf16[8,32,576]{2,1,0:T(8,128)(2,1)} %collective-permute-done.4.q, ...), custom_call_target="tpu_custom_call" | custom-call | flops 300000000 | bytes 4000000 | tf_op jit(solution)/shard_map/pallas_call | solution.py:105
  22.0 0.7 copy-done.2
  22.8 9.7 %all-to-all-start = ((bf16[32,8,640]{2,1,0:T(8,128)(2,1)}), bf16[32,8,640]{2,1,0:T(8,128)(2,1)S(1)}, u32[]{:S(2)}, u32[]{:S(2)}) async-start(bf16[32,8,640]{2,1,0:T(8,128)(2,1)} %copy-done.2), calls=%async_computation | async-start | bytes 655360 | tf_op jit(solution)/shard_map/all_to_all | solution.py:27
  32.5 1.0 constant_dynamic-slice_fusion.1
  33.5 0.5 collective-permute-start.1
  34.0 0.2 dynamic_update_slice.6
  34.2 1.4 %collective-permute-done.1 = bf16[8,112]{1,0:T(8,128)(2,1)S(1)} collective-permute-done((bf16[8,112]{1,0:T(8,128)(2,1)S(1)}, bf16[8,112]{1,0:T(8,128)(2,1)S(1)}, u32[]{:S(2)}, u32[]{:S(2)}) %collective-permute-start.1) | collective-permute-done | bytes 1824 | tf_op jit(solution)/shard_map/ppermute | solution.py:23
  35.6 0.2 dynamic_update_slice.7
  35.8 1.0 dynamic-slice_reduce_fusion
  37.3 7.9 %all-to-all-done = bf16[32,8,640]{2,1,0:T(8,128)(2,1)S(1)} async-done(((bf16[32,8,640]{2,1,0:T(8,128)(2,1)}), bf16[32,8,640]{2,1,0:T(8,128)(2,1)S(1)}, u32[]{:S(2)}, u32[]{:S(2)}) %all-to-all-start) | async-done | bytes 327712 | tf_op jit(solution)/shard_map/all_to_all | solution.py:27
  46.6 0.1 convolution_convert_fusion
  46.7 0.2 fusion.12
  47.0 0.9 collective-permute-done.7
  47.9 0.2 fusion.18
  48.1 14.7 %all_to_all.20 = bf16[32,8,128]{2,1,0:T(8,128)(2,1)S(1)} all-to-all(bf16[32,8,128]{2,1,0:T(8,128)(2,1)S(1)} %pad.4), channel_id=1, replica_groups=mesh['role'=2,'dp'=2,'x'=4,'z'=8,'core'=2] {'x','z'}, dimensions={0} | all-to-all | bytes 131072 | tf_op jit(solution)/shard_map/all_to_all | solution.py:27
  62.8 0.7 broadcast_in_dim.51
  63.5 5.6 %all-to-all-start.2 = ((bf16[64,8,128]{2,1,0:T(8,128)(2,1)}), bf16[64,8,128]{2,1,0:T(8,128)(2,1)S(1)}, u32[]{:S(2)}, u32[]{:S(2)}) async-start(bf16[64,8,128]{2,1,0:T(8,128)(2,1)} %broadcast_in_dim.51), calls=%async_computation.2 | async-start | bytes 262144 | tf_op jit(solution)/shard_map/all_to_all | solution.py:27
  69.1 2.3 %collective-permute-start.12 = (s32[8,8]{1,0:T(8,128)S(1)}, s32[8,8]{1,0:T(8,128)S(1)}, u32[]{:S(2)}, u32[]{:S(2)}) collective-permute-start(s32[8,8]{1,0:T(8,128)S(1)} %bitcast.90), channel_id=1, source_target_pairs={{0,128},{128,0},{1,129},{129,1},{2,130},{130,2},{3,131},{131,3},{4... | collective-permute-start | bytes 776 | tf_op jit(solution)/shard_map/ppermute | solution.py:23
  71.4 1.3 %collective-permute-start.13 = (f32[8,8]{1,0:T(8,128)S(1)}, f32[8,8]{1,0:T(8,128)S(1)}, u32[]{:S(2)}, u32[]{:S(2)}) collective-permute-start(f32[8,8]{1,0:T(8,128)S(1)} %bitcast.91), channel_id=1, source_target_pairs={{0,128},{128,0},{1,129},{129,1},{2,130},{130,2},{3,131},{131,3},{4... | collective-permute-start | bytes 776 | tf_op jit(solution)/shard_map/ppermute | solution.py:23
  72.8 7.6 %all-to-all-done.2 = bf16[64,8,128]{2,1,0:T(8,128)(2,1)S(1)} async-done(((bf16[64,8,128]{2,1,0:T(8,128)(2,1)}), bf16[64,8,128]{2,1,0:T(8,128)(2,1)S(1)}, u32[]{:S(2)}, u32[]{:S(2)}) %all-to-all-start.2) | async-done | bytes 131104 | tf_op jit(solution)/shard_map/all_to_all | solution.py:27
  80.4 0.1 select_reduce_fusion.1
  80.5 1.3 %collective-permute-start.14 = (f32[8,1]{0,1:T(1,128)S(1)}, f32[8,1]{0,1:T(1,128)S(1)}, u32[]{:S(2)}, u32[]{:S(2)}) collective-permute-start(f32[8,1]{0,1:T(1,128)S(1)} %bitcast.88), channel_id=1, source_target_pairs={{0,64},{64,0},{1,65},{65,1},{2,66},{66,2},{3,67},{67,3},{4,68},{68... | collective-permute-start | bytes 104 | tf_op jit(solution)/shard_map/ppermute | solution.py:23
  81.8 2.5 %collective-permute-done.14 = f32[8,1]{0,1:T(1,128)S(1)} collective-permute-done((f32[8,1]{0,1:T(1,128)S(1)}, f32[8,1]{0,1:T(1,128)S(1)}, u32[]{:S(2)}, u32[]{:S(2)}) %collective-permute-start.14) | collective-permute-done | bytes 64 | tf_op jit(solution)/shard_map/ppermute | solution.py:23
  84.4 0.2 fusion.14
  84.6 0.1 fusion.16
  84.8 2.0 %fusion.4 = f32[16,128]{1,0:T(8,128)S(1)} fusion(bf16[16,7168]{1,0:T(8,128)(2,1)S(1)} %bitcast.80, bf16[1,7168,128]{2,1,0:T(8,128)(2,1)} %param.25), kind=kOutput, calls=%fused_computation.5 | convolution fusion | flops 29360128 | bytes 2072576 | tf_op jit(solution)/shard_map/dot_general | solution.py:202
  86.8 0.4 fusion.9
  87.2 0.4 fusion.28
  87.6 0.8 collective-permute-done.10
  88.4 1.9 %fusion.1 = bf16[16,7168]{1,0:T(8,128)(2,1)S(1)} fusion(f32[16,7168]{1,0:T(8,128)S(1)} %fusion.28, bf16[16,128]{1,0:T(8,128)(2,1)S(1)} %collective-permute-done.10, bf16[128,7168]{1,0:T(8,128)(2,1)} %collective-permute-done.11, f32[16]{0:T(128)S(1)} %broadcast_select_fusion.2), kind=kOutput, calls=%fused_computation.2 | convolution fusion | flops 29704192 | bytes 2527296 | tf_op jit(solution)/shard_map/dot_general | solution.py:206
  90.2 0.4 reshape.203
  90.6 0.3 constant_dynamic-slice_fusion
  90.9 0.8 copy.56
  91.7 8.1 %all-to-all-start.3 = ((bf16[64,8,112]{2,1,0:T(8,128)(2,1)}), bf16[64,8,112]{2,1,0:T(8,128)(2,1)S(1)}, u32[]{:S(2)}, u32[]{:S(2)}) async-start(bf16[64,8,112]{2,1,0:T(8,128)(2,1)} %bitcast.28), calls=%async_computation.3 | async-start | bytes 262144 | tf_op jit(solution)/shard_map/all_to_all | solution.py:27
  99.8 11.4 %all-to-all-done.3 = bf16[64,8,112]{2,1,0:T(8,128)(2,1)S(1)} async-done(((bf16[64,8,112]{2,1,0:T(8,128)(2,1)}), bf16[64,8,112]{2,1,0:T(8,128)(2,1)S(1)}, u32[]{:S(2)}, u32[]{:S(2)}) %all-to-all-start.3) | async-done | bytes 114720 | tf_op jit(solution)/shard_map/all_to_all | solution.py:27
  111.4 0.1 collective-permute-start.15
  111.6 5.0 %collective-permute-done.15 = bf16[8,112]{1,0:T(8,128)(2,1)S(1)} collective-permute-done((bf16[8,112]{1,0:T(8,128)(2,1)S(1)}, bf16[8,112]{1,0:T(8,128)(2,1)S(1)}, u32[]{:S(2)}, u32[]{:S(2)}) %collective-permute-start.15) | collective-permute-done | bytes 1824 | tf_op jit(solution)/shard_map/ppermute | solution.py:23
  116.6 0.6 copy.67
  (72 shorter events, 2.6 us)
Async XLA Ops:
  0.0 32.5 %copy-start = (bf16[128,7168]{1,0:T(8,128)(2,1)S(1)}, bf16[128,7168]{1,0:T(8,128)(2,1)}, u32[]{:S(2)}) copy-start(bf16[128,7168]{1,0:T(8,128)(2,1)} %param.24) | copy-start | bytes 5505028
  0.0 16.8 %collective-permute-start.5 = (bf16[20,64,576]{2,1,0:T(8,128)(2,1)}, bf16[20,64,576]{2,1,0:T(8,128)(2,1)S(1)}, u32[]{:S(2)}, u32[]{:S(2)}) collective-permute-start(bf16[20,64,576]{2,1,0:T(8,128)(2,1)} %bitcast.75), channel_id=1, source_target_pairs={{0,1},{1,0},{2,3},{3,2},{4,5},{5,4},{6,7},{7,6},{8,9},{9,8},{10,11... | collective-permute-start | bytes 4423688 | tf_op jit(solution)/shard_map/ppermute | solution.py:23
  0.1 1.2 %copy-start.3 = (bf16[2,1,1,4,64,576]{5,4,3,2,1,0:T(8,128)(2,1)S(1)}, bf16[2,1,1,4,64,576]{5,4,3,2,1,0:T(8,128)(2,1)}, u32[]{:S(2)}) copy-start(bf16[2,1,1,4,64,576]{5,4,3,2,1,0:T(8,128)(2,1)} %param.17) | copy-start | bytes 1769476
  2.8 14.0 %collective-permute-start.4 = (bf16[8,32,576]{2,1,0:T(8,128)(2,1)}, bf16[8,32,576]{2,1,0:T(8,128)(2,1)}, u32[]{:S(2)}, u32[]{:S(2)}) collective-permute-start(bf16[8,32,576]{2,1,0:T(8,128)(2,1)} %shard_map.136), channel_id=1, source_target_pairs={{0,128},{128,0},{1,129},{129,1},{2,130},{130,2},{3,131},{131,3},{4... | collective-permute-start | bytes 884744 | tf_op jit(solution)/shard_map/ppermute | solution.py:23
  4.9 11.9 %collective-permute-start.2 = (s32[2,4,4]{2,1,0:T(4,128)}, s32[2,4,4]{2,1,0:T(4,128)S(1)}, u32[]{:S(2)}, u32[]{:S(2)}) collective-permute-start(s32[2,4,4]{2,1,0:T(4,128)} %bitcast.78), channel_id=1, source_target_pairs={{0,1},{1,0},{2,3},{3,2},{4,5},{5,4},{6,7},{7,6},{8,9},{9,8},{10,11... | collective-permute-start | bytes 392 | tf_op jit(solution)/shard_map/ppermute | solution.py:23
  5.0 9.8 %collective-permute-start.3 = (s32[4]{0:T(128)}, s32[4]{0:T(128)S(1)}, u32[]{:S(2)}, u32[]{:S(2)}) collective-permute-start(s32[4]{0:T(128)} %bitcast.93), channel_id=1, source_target_pairs={{0,128},{128,0},{1,129},{129,1},{2,130},{130,2},{3,131},{131,3},{4... | collective-permute-start | bytes 56 | tf_op jit(solution)/shard_map/ppermute | solution.py:23
  7.1 29.6 %collective-permute-start.6 = (bf16[2,4,576]{2,0,1:T(2,128)(2,1)S(1)}, bf16[2,4,576]{2,0,1:T(2,128)(2,1)S(1)}, u32[]{:S(2)}, u32[]{:S(2)}) collective-permute-start(bf16[2,4,576]{2,0,1:T(2,128)(2,1)S(1)} %bitcast.86), channel_id=1, source_target_pairs={{0,128},{128,0},{1,129},{129,1},{2,130},{130,2},{3,131},{131,3},{4... | collective-permute-start | bytes 27656 | tf_op jit(solution)/shard_map/ppermute | solution.py:23
  14.7 18.7 %collective-permute-start = (bf16[8,112]{1,0:T(8,128)(2,1)}, bf16[8,112]{1,0:T(8,128)(2,1)S(1)}, u32[]{:S(2)}, u32[]{:S(2)}) collective-permute-start(bf16[8,112]{1,0:T(8,128)(2,1)} %bitcast.92), channel_id=1, source_target_pairs={{0,128},{128,0},{1,129},{129,1},{2,130},{130,2},{3,131},{131,3},{4... | collective-permute-start | bytes 5384 | tf_op jit(solution)/shard_map/ppermute | solution.py:23
  16.8 1.4 %copy-start.1 = (bf16[1,1,1,20,64,576]{5,4,3,2,1,0:T(8,128)(2,1)S(1)}, bf16[1,1,1,20,64,576]{5,4,3,2,1,0:T(8,128)(2,1)}, u32[]{:S(2)}) copy-start(bf16[1,1,1,20,64,576]{5,4,3,2,1,0:T(8,128)(2,1)} %param.14) | copy-start | bytes 4423684
  18.2 0.7 copy-start.4
  22.0 0.7 copy-start.2
  22.8 23.8 %copy-start.7 = (bf16[1,512,128]{2,1,0:T(8,128)(2,1)S(1)}, bf16[1,512,128]{2,1,0:T(8,128)(2,1)}, u32[]{:S(2)}) copy-start(bf16[1,512,128]{2,1,0:T(8,128)(2,1)} %param.23) | copy-start | bytes 393220
  22.8 22.4 %all-to-all-start = ((bf16[32,8,640]{2,1,0:T(8,128)(2,1)}), bf16[32,8,640]{2,1,0:T(8,128)(2,1)S(1)}, u32[]{:S(2)}, u32[]{:S(2)}) async-start(bf16[32,8,640]{2,1,0:T(8,128)(2,1)} %copy-done.2), calls=%async_computation | async-start | bytes 655360 | tf_op jit(solution)/shard_map/all_to_all | solution.py:27
  33.5 13.5 %collective-permute-start.8 = (bf16[128,3584]{1,0:T(8,128)(2,1)}, bf16[128,3584]{1,0:T(8,128)(2,1)S(1)}, u32[]{:S(2)}, u32[]{:S(2)}) collective-permute-start(bf16[128,3584]{1,0:T(8,128)(2,1)} %constant_dynamic-slice_fusion.1), channel_id=1, source_target_pairs={{0,1},{1,0},{2,3},{3,2},{4,5},{5,4},{6,7},{7,6},{8,9},{9,8},{10,11... | collective-permute-start | bytes 2752520 | tf_op jit(solution)/shard_map/ppermute | solution.py:23
  33.5 2.1 %collective-permute-start.1 = (bf16[8,112]{1,0:T(8,128)(2,1)S(1)}, bf16[8,112]{1,0:T(8,128)(2,1)S(1)}, u32[]{:S(2)}, u32[]{:S(2)}) collective-permute-start(bf16[8,112]{1,0:T(8,128)(2,1)S(1)} %collective-permute-done), channel_id=1, source_target_pairs={{0,1},{1,0},{2,3},{3,2},{4,5},{5,4},{6,7},{7,6},{8,9},{9,8},{10,11... | collective-permute-start | bytes 5384 | tf_op jit(solution)/shard_map/ppermute | solution.py:23
  36.9 32.2 %copy-start.9 = (s32[2,1,1,4,8]{4,3,2,1,0:T(4,128)S(1)}, s32[2,1,1,4,8]{4,3,2,1,0:T(4,128)}, u32[]{:S(2)}) copy-start(s32[2,1,1,4,8]{4,3,2,1,0:T(4,128)} %param.20) | copy-start | bytes 772
  36.9 34.5 %copy-start.10 = (f32[2,1,1,4,8]{4,3,2,1,0:T(4,128)S(1)}, f32[2,1,1,4,8]{4,3,2,1,0:T(4,128)}, u32[]{:S(2)}) copy-start(f32[2,1,1,4,8]{4,3,2,1,0:T(4,128)} %param.21) | copy-start | bytes 772
  37.3 35.5 %copy-start.8 = (f32[7168]{0:T(1024)S(1)}, f32[7168]{0:T(1024)}, u32[]{:S(2)}) copy-start(f32[7168]{0:T(1024)} %param.22) | copy-start | bytes 86020
  46.7 1.2 collective-permute-start.7
  63.5 16.8 %all-to-all-start.2 = ((bf16[64,8,128]{2,1,0:T(8,128)(2,1)}), bf16[64,8,128]{2,1,0:T(8,128)(2,1)S(1)}, u32[]{:S(2)}, u32[]{:S(2)}) async-start(bf16[64,8,128]{2,1,0:T(8,128)(2,1)} %broadcast_in_dim.51), calls=%async_computation.2 | async-start | bytes 262144 | tf_op jit(solution)/shard_map/all_to_all | solution.py:27
  69.1 11.2 %collective-permute-start.12 = (s32[8,8]{1,0:T(8,128)S(1)}, s32[8,8]{1,0:T(8,128)S(1)}, u32[]{:S(2)}, u32[]{:S(2)}) collective-permute-start(s32[8,8]{1,0:T(8,128)S(1)} %bitcast.90), channel_id=1, source_target_pairs={{0,128},{128,0},{1,129},{129,1},{2,130},{130,2},{3,131},{131,3},{4... | collective-permute-start | bytes 776 | tf_op jit(solution)/shard_map/ppermute | solution.py:23
  71.4 8.9 %collective-permute-start.13 = (f32[8,8]{1,0:T(8,128)S(1)}, f32[8,8]{1,0:T(8,128)S(1)}, u32[]{:S(2)}, u32[]{:S(2)}) collective-permute-start(f32[8,8]{1,0:T(8,128)S(1)} %bitcast.91), channel_id=1, source_target_pairs={{0,128},{128,0},{1,129},{129,1},{2,130},{130,2},{3,131},{131,3},{4... | collective-permute-start | bytes 776 | tf_op jit(solution)/shard_map/ppermute | solution.py:23
  72.7 14.9 %collective-permute-start.11 = (bf16[128,7168]{1,0:T(8,128)(2,1)}, bf16[128,7168]{1,0:T(8,128)(2,1)}, u32[]{:S(2)}, u32[]{:S(2)}) collective-permute-start(bf16[128,7168]{1,0:T(8,128)(2,1)} %bitcast.82), channel_id=1, source_target_pairs={{0,1},{1,0},{2,3},{3,2},{4,5},{5,4},{6,7},{7,6},{8,9},{9,8},{10,11... | collective-permute-start | bytes 5505032 | tf_op jit(solution)/shard_map/ppermute | solution.py:23
  80.3 6.4 %copy-start.5 = (bf16[1,7168,128]{2,1,0:T(8,128)(2,1)S(1)}, bf16[1,7168,128]{2,1,0:T(8,128)(2,1)}, u32[]{:S(2)}) copy-start(bf16[1,7168,128]{2,1,0:T(8,128)(2,1)} %param.26) | copy-start | bytes 5505028
  80.3 4.1 %collective-permute-start.9 = (bf16[64,8,128]{2,1,0:T(8,128)(2,1)S(1)}, bf16[64,8,128]{2,1,0:T(8,128)(2,1)S(1)}, u32[]{:S(2)}, u32[]{:S(2)}) collective-permute-start(bf16[64,8,128]{2,1,0:T(8,128)(2,1)S(1)} %all-to-all-done.2), channel_id=1, source_target_pairs={{0,1},{1,0},{2,3},{3,2},{4,5},{5,4},{6,7},{7,6},{8,9},{9,8},{10,11... | collective-permute-start | bytes 393224 | tf_op jit(solution)/shard_map/ppermute | solution.py:23
  80.5 3.8 %collective-permute-start.14 = (f32[8,1]{0,1:T(1,128)S(1)}, f32[8,1]{0,1:T(1,128)S(1)}, u32[]{:S(2)}, u32[]{:S(2)}) collective-permute-start(f32[8,1]{0,1:T(1,128)S(1)} %bitcast.88), channel_id=1, source_target_pairs={{0,64},{64,0},{1,65},{65,1},{2,66},{66,2},{3,67},{67,3},{4,68},{68... | collective-permute-start | bytes 104 | tf_op jit(solution)/shard_map/ppermute | solution.py:23
  84.8 2.5 %copy-start.6 = (bf16[1,128,7168]{2,1,0:T(8,128)(2,1)S(1)}, bf16[1,128,7168]{2,1,0:T(8,128)(2,1)}, u32[]{:S(2)}) copy-start(bf16[1,128,7168]{2,1,0:T(8,128)(2,1)} %param.27) | copy-start | bytes 5505028
  87.1 1.3 %collective-permute-start.10 = (bf16[16,128]{1,0:T(8,128)(2,1)S(1)}, bf16[16,128]{1,0:T(8,128)(2,1)S(1)}, u32[]{:S(2)}, u32[]{:S(2)}) collective-permute-start(bf16[16,128]{1,0:T(8,128)(2,1)S(1)} %fusion.9), channel_id=1, source_target_pairs={{0,1},{1,0},{2,3},{3,2},{4,5},{5,4},{6,7},{7,6},{8,9},{9,8},{10,11... | collective-permute-start | bytes 12296 | tf_op jit(solution)/shard_map/ppermute | solution.py:23
  91.7 19.5 %all-to-all-start.3 = ((bf16[64,8,112]{2,1,0:T(8,128)(2,1)}), bf16[64,8,112]{2,1,0:T(8,128)(2,1)S(1)}, u32[]{:S(2)}, u32[]{:S(2)}) async-start(bf16[64,8,112]{2,1,0:T(8,128)(2,1)} %bitcast.28), calls=%async_computation.3 | async-start | bytes 262144 | tf_op jit(solution)/shard_map/all_to_all | solution.py:27
  111.4 5.1 %collective-permute-start.15 = (bf16[8,112]{1,0:T(8,128)(2,1)S(1)}, bf16[8,112]{1,0:T(8,128)(2,1)S(1)}, u32[]{:S(2)}, u32[]{:S(2)}) collective-permute-start(bf16[8,112]{1,0:T(8,128)(2,1)S(1)} %add_convert_fusion.1), channel_id=1, source_target_pairs={{0,128},{128,0},{1,129},{129,1},{2,130},{130,2},{3,131},{131,3},{4... | collective-permute-start | bytes 5384 | tf_op jit(solution)/shard_map/ppermute | solution.py:23

commit v2 on v1

v2 whole, which is shorter than its diff:
```python
import jax
import jax.numpy as jnp
from jax import lax
from jax.experimental import pallas as pl
from jax.experimental.pallas import tpu as pltpu
from jax.sharding import Mesh, PartitionSpec as P

SCORE_SCALE = 192.0 ** (-0.5)
EPSILON = 1e-06
MASK_VALUE = -1e30
HALF = 3584
CHUNKS = 28
BLOCK = 112
XZ = ("x", "z")
DXZ = ("dp", "x", "z")
bf16 = jnp.bfloat16
f32 = jnp.float32

VM = pl.BlockSpec(memory_space=pltpu.VMEM)
SM = pl.BlockSpec(memory_space=pltpu.SMEM)
ANY = pl.BlockSpec(memory_space=pl.ANY)
FAR = pl.BlockSpec(memory_space=pltpu.HBM)
MIB = 1024 * 1024


def call(kernel, outs, specs, args, flops, moved, scratch=(), limit=16, exps=0):
    many = isinstance(outs, list)
    return pl.pallas_call(
        kernel,
        out_shape=outs,
        in_specs=specs,
        out_specs=[VM] * len(outs) if many else VM,
        scratch_shapes=list(scratch),
        compiler_params=pltpu.CompilerParams(vmem_limit_bytes=limit * MIB),
        cost_estimate=pl.CostEstimate(flops=flops, bytes_accessed=moved, transcendentals=exps),
    )(*args)


def shape(*dims, dtype=bf16):
    return jax.ShapeDtypeStruct(dims, dtype)


def far(value):
    return pltpu.with_memory_space_constraint(value, pltpu.HBM)


def swap(value, axis):
    return lax.ppermute(value, axis, [(0, 1), (1, 0)])


def exchange(value, axes):
    return lax.all_to_all(value, axes, 0, 0, tiled=True)


def split(value):
    first = value.astype(bf16).astype(f32)
    second = (value - first).astype(bf16).astype(f32)
    return first, second, (value - first) - second


def pick_kernel(ids, *refs):
    sources, pool, (out, keys), landed, (wide, sems) = refs[:7], refs[7], refs[8:10], refs[10:17], refs[17:]
    copies = [
        pltpu.make_async_copy(
            sources[0].at[pl.ds(2 * i, 2)], landed[0].at[pl.ds(2 * i, 2)], sems.at[i]
        )
        for i in range(4)
    ] + [pltpu.make_async_copy(sources[i], landed[i], sems.at[3 + i]) for i in range(1, 7)]
    for one in copies:
        one.start()
    queries, fresh, x_in, routes, gates, lengths, table = landed
    copies[9].wait()
    gathered = [
        pltpu.make_async_copy(
            pool.at[table[ids[1], i // 4, i % 4]], keys.at[i], sems.at[10 + i]
        )
        for i in range(16)
    ]
    for one in gathered:
        one.start()
    for i in range(8):
        if i % 2 == 0:
            copies[i // 2].wait()
        asked = queries[i].astype(f32)
        for k in range(5):
            lanes = slice(128 * k, min(128 * k + 128, 576))
            wide[k, 64 * i : 64 * i + 64, 0 : lanes.stop - lanes.start] = asked[:, lanes]
        for k in range(5):
            lanes = slice(128 * k, min(128 * k + 128, 576))
            half = wide[k, pl.ds(64 * i + ids[0], 32, stride=2), :]
            out[i, :, lanes] = half[:, 0 : lanes.stop - lanes.start].astype(bf16)
    lane = lax.broadcasted_iota(jnp.int32, (4, 128), 1)
    for one in copies[4:9]:
        one.wait()
    count = jnp.concatenate([lengths[...], jnp.zeros((1, 124), jnp.int32)], axis=1)
    high = lax.shift_right_logical(count, 7)
    told = pltpu.roll(high.astype(f32), 64, 1) + pltpu.roll((count - 128 * high).astype(f32), 68, 1)
    rows = []
    blocks = []
    for s in range(2):
        note = jnp.zeros((4, 128), f32)
        for k in range(8):
            note = note + jnp.where(lane == routes[s][:, k : k + 1], gates[s][:, k : k + 1], 0.0)
        parts = split(note)
        note = parts[0] + pltpu.roll(parts[1], 16, 1) + pltpu.roll(parts[2], 32, 1) + told
        rows.append(fresh[s].astype(f32))
        block = jnp.concatenate([x_in[s].astype(f32), jnp.zeros((4, 16), f32)], axis=1)
        blocks.append(jnp.concatenate([block, note, jnp.zeros((4, 320), f32)], axis=1))
    blank = [jnp.zeros((8, 576), f32)]
    out[8] = jnp.concatenate(rows + blank + blocks + blank, axis=0).astype(bf16)
    for one in gathered:
        one.wait()


def attention_kernel(ids, q, keys_mine, keys_other, *rest):
    out, told, scratch = rest[-3:]
    lane = lax.broadcasted_iota(jnp.int32, (1, 512), 1)
    start = jnp.where(lane < 256, ids[2] * 256, (ids[2] - 2 * ids[0]) * 256)
    places = (start + lane).astype(f32)
    slot = lax.broadcasted_iota(jnp.int32, (32, 128), 1)
    extra = q[8]
    notes = extra[16:32, 128:256].astype(f32)
    told[0:8, :] = extra[16:32, 0:128].astype(f32)[0:8]
    told[8:16, :] = notes[0:8]
    fresh = extra[0:16]
    row = lax.broadcasted_iota(jnp.int32, (64, 16), 0)
    col = lax.broadcasted_iota(jnp.int32, (64, 16), 1)
    for r in range(4):
        keys = jnp.concatenate(
            [side[4 * r + j] for side in (keys_mine, keys_other) for j in range(4)], axis=0
        )
        asked = jnp.concatenate([q[r], q[4 + r]], axis=0)
        scores = lax.dot_general(
            asked, keys, (((1,), (1,)), ((), ())), preferred_element_type=f32
        )
        late = lax.dot_general(
            asked, fresh, (((1,), (1,)), ((), ())), preferred_element_type=f32
        )
        usable = places < notes[0:1, 64 + r : 65 + r] * 128.0 + notes[0:1, 68 + r : 69 + r]
        counted = (ids[3] == 0) & ((col == r) | ((col == 4 + r) & (row >= 32)))
        scores = jnp.where(usable, scores * SCORE_SCALE, MASK_VALUE)
        late = jnp.where(counted, late * SCORE_SCALE, MASK_VALUE)
        top = jnp.maximum(
            jnp.max(scores, axis=1, keepdims=True), jnp.max(late, axis=1, keepdims=True)
        )
        weights = jnp.where(usable, jnp.exp(scores - top), 0.0)
        late = jnp.where(counted, jnp.exp(late - top), 0.0)
        total = jnp.sum(weights, axis=1, keepdims=True) + jnp.sum(late, axis=1, keepdims=True)
        summed = jnp.dot(weights.astype(bf16), keys[:, :512], preferred_element_type=f32)
        summed = summed + jnp.dot(
            late.astype(bf16), fresh[:, :512], preferred_element_type=f32
        )
        live = total > 0.0
        safe = jnp.where(live, total, 1.0)
        level = jnp.where(live, top + jnp.log(safe), MASK_VALUE)
        value = summed * (1.0 / safe)
        first, second, third = split(level)
        for s in range(2):
            rows = slice(32 * s, 32 * s + 32)
            tail = jnp.where(
                slot == 0,
                first[rows],
                jnp.where(slot == 1, second[rows], jnp.where(slot == 2, third[rows], 0.0)),
            )
            for k in range(5):
                part = value[rows, 128 * k : 128 * k + 128] if k < 4 else tail
                scratch[k, pl.ds(4 * s + r, 32, stride=8), :] = part
    for k in range(5):
        out[:, :, 128 * k : 128 * k + 128] = scratch[k].reshape(32, 8, 128).astype(bf16)


def context_kernel(ids, got, told, value_up, proj, kept, sent):
    level = jnp.sum(got[:, :, 512:640].astype(f32), axis=2, keepdims=True)
    factors = jnp.exp(level - jnp.max(level, axis=0, keepdims=True))
    denominator = jnp.sum(factors, axis=0)
    numerator = jnp.zeros((8, 512), f32)
    for i in range(32):
        numerator = numerator + factors[i] * got[i, :, 0:512].astype(f32)
    context = (numerator / denominator).astype(bf16)
    vals = jnp.dot(context, value_up[...], preferred_element_type=f32).astype(bf16)
    start = jnp.concatenate([told[0:8, :], jnp.zeros((8, HALF - 128), f32)], axis=1)
    start = pltpu.roll(start, (ids[2] % 32) * BLOCK, 1)
    for out, half in ((sent, 1 - ids[0]), (kept, ids[0])):
        lanes = pl.ds(pl.multiple_of(half * HALF, 128), HALF)
        total = jnp.dot(vals, proj[:, lanes], preferred_element_type=f32)
        total = total + jnp.where(ids[2] // 32 == half, start, 0.0)
        for k in range(CHUNKS):
            out[k] = total[:, 128 * k : 128 * k + 128].astype(out.dtype)


def join_kernel(kept, other, out):
    for k in range(CHUNKS):
        out[k] = (kept[k] + other[k].astype(f32)).astype(bf16)
    for k in range(CHUNKS, 32):
        out[k] = jnp.zeros((8, 128), bf16)


def spread_kernel(ids, got, told, out):
    total = got[0].astype(f32)
    for i in range(1, 32):
        total = total + got[i].astype(f32)
    piece = jnp.where(ids[3] == CHUNKS, told[8:16, :], total).astype(bf16)
    for i in range(64):
        out[i] = piece


def raise_kernel(ids, rows, gain, gate, up, gate_other, up_other, out, scaled, own):
    squares = [jnp.zeros((8, 128), f32) for _ in range(2)]
    for k in range(CHUNKS):
        lanes = slice(128 * k, 128 * k + 128)
        parts = [rows[32 * d + k].astype(f32) for d in range(2)]
        squares = [squares[d] + parts[d] * parts[d] for d in range(2)]
        both = jnp.concatenate(parts, axis=0) * gain[pl.ds(ids[0] * CHUNKS + k, 1), :]
        scaled[:, lanes] = both.astype(bf16)
        own[:, lanes] = jnp.where(ids[4] == 0, parts[0], parts[1])
    here = pl.ds(pl.multiple_of(ids[0] * HALF, 128), HALF)
    asked = scaled[...]
    out[:, 0:128] = jnp.dot(asked, gate[here, :], preferred_element_type=f32)
    out[:, 128:256] = jnp.dot(asked, up[here, :], preferred_element_type=f32)
    out[:, 256:384] = jnp.dot(asked, gate_other[here, :], preferred_element_type=f32)
    out[:, 384:512] = jnp.dot(asked, up_other[here, :], preferred_element_type=f32)
    out[:, 512:640] = jnp.concatenate(squares, axis=0)
    shift = HALF - (ids[3] % 16) * (2 * BLOCK)
    turned = pltpu.roll(own[...], shift, 1)[:, 0:256]
    out[0:8, 640:896] = jnp.where(ids[0] == ids[3] // 16, turned, 0.0)
    out[8:16, 640:896] = jnp.zeros((8, 256), f32)


def lower_kernel(ids, mine, other, rows, down, down_other, out, own, product):
    squares = jnp.sum(mine[:, 512:640] + other[:, 512:640], axis=1, keepdims=True)
    scale = lax.rsqrt(squares * (1.0 / (2 * HALF)) + EPSILON)

    def active(near, near_at, far, far_at):
        gate = (near[:, near_at : near_at + 128] + far[:, far_at : far_at + 128]) * scale
        up = (
            near[:, near_at + 128 : near_at + 256] + far[:, far_at + 128 : far_at + 256]
        ) * scale
        return (gate / (1.0 + jnp.exp(-gate)) * up).astype(bf16)

    told = jnp.concatenate([rows[CHUNKS].astype(f32), rows[32 + CHUNKS].astype(f32)], axis=0)
    lane = lax.broadcasted_iota(jnp.int32, (16, 128), 1)
    wanted = (lane % 16 == ids[4] * 8 + ids[3] // 4) & (lane < 48)
    mixing = jnp.sum(jnp.where(wanted, told, 0.0), axis=1, keepdims=True)
    here = active(mine, 0, other, 256)
    there = active(other, 0, mine, 256)
    for k in range(14):
        lanes = slice(512 * k, 512 * k + 512)
        total = jnp.dot(here, down[:, lanes], preferred_element_type=f32)
        total = total + jnp.dot(there, down_other[:, lanes], preferred_element_type=f32)
        product[:, lanes] = total * mixing
    product[:, 7168:7296] = jnp.zeros((16, 128), f32)
    both = mine[0:8, 640:896] + other[0:8, 640:896]

    def fill(core):
        for k in range(32):
            at = (2 * k + core) * BLOCK
            base, turn = at // 128 * 128, at % 128
            for d in range(2):
                part = product[8 * d : 8 * d + 8, base : base + 256]
                if turn:
                    part = pltpu.roll(part, 256 - turn, 1)
                out[32 * d + k] = part[:, 0:128].astype(bf16)
        part = pltpu.roll(both, 256 - BLOCK, 1) if core else both
        own[...] = part[:, 0:128]

    @pl.when(ids[0] == 0)
    def _():
        fill(0)

    @pl.when(ids[0] == 1)
    def _():
        fill(1)


def finish_kernel(got, own, out):
    total = own[...]
    for i in range(64):
        total = total + got[i].astype(f32)
    for s in range(2):
        out[s] = total[4 * s : 4 * s + 4, 0:BLOCK].astype(bf16)


def body(
    prompt_pool,
    block_table,
    cache_len,
    queries,
    fresh_latent,
    x_in,
    routes,
    gates,
    norm_gain,
    value_up,
    out_proj,
    w_gate,
    w_up,
    w_down,
):
    role = lax.axis_index("role")
    dp = lax.axis_index("dp")
    core = lax.axis_index("core")
    chip = lax.axis_index("x") * lax.axis_size("z") + lax.axis_index("z")
    ids = jnp.stack([core, 1 - role, chip * 2 + core, chip, dp]).astype(jnp.int32)
    half_there = (1 - core) * HALF
    gate_other, up_other, down_other = [
        swap(one, "core") for one in (w_gate[0], w_up[0], w_down[0])
    ]
    given = (
        queries.reshape(8, 64, 576),
        fresh_latent.reshape(2, 4, 576),
        x_in.reshape(2, 4, BLOCK),
        routes.reshape(2, 4, 8),
        gates.reshape(2, 4, 8),
        cache_len.reshape(1, 4),
        block_table[:, 0, 0],
    )
    picked, keys = call(
        pick_kernel,
        [shape(9, 32, 576), shape(16, 64, 576)],
        [SM] + [FAR] * 8,
        (ids,) + tuple(far(one) for one in given + (prompt_pool[0, 0, 0],)),
        19000000,
        900000,
        [pltpu.VMEM(one.shape, one.dtype) for one in given[:6]]
        + [pltpu.SMEM((2, 4, 4), jnp.int32), pltpu.VMEM((5, 512, 128), f32)]
        + [pltpu.SemaphoreType.DMA((26,))],
        8,
    )
    q = swap(picked, "role")
    keys_other = swap(keys, "core")
    after = (gate_other, up_other, down_other)[:EXTRA]
    sent, told = call(
        attention_kernel,
        [shape(32, 8, 640), shape(16, 128, dtype=f32)],
        [SM, VM, VM, VM] + [ANY] * len(after),
        (ids, q, keys, keys_other) + after,
        300000000,
        4000000,
        [pltpu.VMEM((5, 256, 128), f32)],
        16,
        131072,
    )
    got = exchange(sent, XZ)
    kept, passed = call(
        context_kernel,
        [shape(CHUNKS, 8, 128, dtype=f32), shape(CHUNKS, 8, 128)],
        [SM] + [VM] * 4,
        (ids, got, told, value_up[0], out_proj),
        20000000,
        2500000,
        (),
        8,
    )
    partial = call(
        join_kernel, shape(32, 8, 128), [VM] * 2, (kept, swap(passed, "core")), 30000, 200000, (), 4
    )
    rows = exchange(
        call(
            spread_kernel,
            shape(64, 8, 128),
            [SM, VM, VM],
            (ids, exchange(partial, XZ), told),
            40000,
            200000,
            (),
            4,
        ),
        DXZ,
    )
    raised = call(
        raise_kernel,
        shape(16, 896, dtype=f32),
        [SM] + [VM] * 6,
        (ids, rows, norm_gain.reshape(56, 128), w_gate[0], w_up[0], gate_other, up_other),
        60000000,
        6000000,
        [pltpu.VMEM((16, HALF), bf16), pltpu.VMEM((8, HALF), f32)],
        16,
    )
    raised_other = swap(raised, "core")
    outgoing, own = call(
        lower_kernel,
        [shape(64, 8, 128), shape(8, 128, dtype=f32)],
        [SM] + [VM] * 5,
        (ids, raised, raised_other, rows, w_down[0], down_other),
        60000000,
        4000000,
        [pltpu.VMEM((16, 7296), f32)],
        16,
        4096,
    )
    done = call(
        finish_kernel, shape(2, 4, BLOCK), [VM] * 2, (exchange(outgoing, DXZ), own), 70000, 140000, (), 4
    )
    return swap(done, "role").reshape(2, 1, 1, 4, BLOCK)


EXTRA = 6


def solution(mesh):
    split = Mesh(mesh.devices.reshape(2, 2, 4, 8, 2), ("role", "dp", "x", "z", "core"))
    e = ("x", "z", "core")
    slab = ("dp", "x", "z", "core")
    placed = (
        P("role", "dp", e, None, None, None),
        P(None, "dp", e, None, None),
        P("role", "dp", None),
        P(None, "role", "dp", None, None, None),
        P(None, "role", "dp", None, None),
        P(None, "role", "dp", None, e),
        P(None, "role", "dp", None, None),
        P(None, "role", "dp", None, None),
        P(),
        P(e, None, None),
        P(e, None),
        P(slab, None, None),
        P(slab, None, None),
        P(slab, None, None),
    )
    return jax.shard_map(
        body,
        mesh=split,
        in_specs=placed,
        out_specs=P(None, "role", "dp", None, e),
        check_vma=False,
    )
```

time: 118 us -> 104 us (0.88)
  blocking collectives: 14.7 us -> 70.1 us
  starting transfers between devices: 36.9 us -> 4.04 us
  waiting for transfers between devices: 43 us -> 17 us
  local copies, waits for them, and re-layouts: 10.9 us -> 0.7 us
  Pallas kernels: 4.57 us -> 12 us
  matrix products: 5.39 us -> 0 us
  other arithmetic: 1.42 us -> 0 us
    all_to_all x1 -> x4, blocking collectives: 14.7 us -> 70.1 us  [exchange(): return lax.all_to_all(value, axes, 0, 0, tiled=True)]
    all_to_all x3 -> x0, waiting for transfers between devices: 26.9 us -> none  [exchange(): return lax.all_to_all(value, axes, 0, 0, tiled=True)]
    all_to_all x3 -> x0, starting transfers between devices: 23.4 us -> none  [exchange(): return lax.all_to_all(value, axes, 0, 0, tiled=True)]
    ppermute x16 -> x8, starting transfers between devices: 13.5 us -> 4.04 us  [swap(): return lax.ppermute(value, axis, [(0, 1), (1, 0)])]
    pallas_call x2 -> x8, Pallas kernels: 4.57 us -> 12 us  [call(): pl.pallas_call(kernel, out_shape=outs, in_specs=specs, out_specs=[VM] * l...]
    dot_general x9 -> x0, matrix products: 5.39 us -> none  [the longest x1 1.99 us: body(): gate_part = jnp.dot(normed, w_gate[0], preferred_element_type=f32)]
    unnamed x26 -> x13, local copies, waits for them, and re-layouts: 5.55 us -> 0.61 us
    dynamic_slice x3 -> x0, local copies, waits for them, and re-layouts: 2.26 us -> none  [the longest x1 0.99 us: body(): lax.dynamic_slice_in_dim(out_proj, (1 - core) * HALF, HALF, 1)]
  transfers between devices with their start and end apart: 19 -> 8, of which waited for: 9 -> 4; matrix products, arithmetic and copies ran while one was open for 7% -> 0% of each run, Pallas kernels for 4% -> 3%
where the time goes in v2:
time: 104 us
  blocking collectives  70.1 us (67%)
  waiting for transfers between devices  17 us (16%)
  Pallas kernels  12 us (12%)
  starting transfers between devices  4.04 us (4%)
    all_to_all x4, blocking collectives, exchange(): return lax.all_to_all(value, axes, 0, 0, tiled=True)  70.1 us
    ppermute x8, waiting for transfers between devices, swap(): return lax.ppermute(value, axis, [(0, 1), (1, 0)])  17 us
    pallas_call x8, Pallas kernels, call(): pl.pallas_call(kernel, out_shape=outs, in_specs=specs, out_specs=[VM] * l...  12 us
    ppermute x8, starting transfers between devices, swap(): return lax.ppermute(value, axis, [(0, 1), (1, 0)])  4.04 us
  transfers between devices with their start and end apart: 8, of which 4 were waited for; matrix products, arithmetic and copies ran while one was open for 0% of the time, Pallas kernels for 3%

profile of v2, /device:TPU:16, one launch (start us, length us, event | category | flops | bytes accessed | tf_op | source)
XLA Modules:
  0.0 104.0 jit_solution(11909815731201454142)
XLA Ops:
  0.0 0.0 collective-permute-start.2
  0.0 0.5 collective-permute-start.3
  0.5 0.0 collective-permute-start.4
  0.5 0.1 stack.23.ids
  0.6 3.0 %shard_map.136 = (bf16[9,32,576]{2,1,0:T(8,128)(2,1)S(1)}, bf16[16,64,576]{2,1,0:T(8,128)(2,1)S(1)}) custom-call(s32[5]{0:T(128)S(1)} %stack.23.ids, bf16[8,64,576]{2,1,0:T(8,128)(2,1)} %bitcast.30, bf16[2,4,576]{2,1,0:T(4,128)(2,1)} %bitcast.31, bf16[2,4,112]{2,1,0:T(4,128)(2,1)} %bitcast.36, s32[2,4,8]{2,1,0:T(4,128)} %bitcast.32, f32[2,4,8]{2,1,0:T(4,128)} %bitcast.33, ...), custom_call_target="tpu_custom_call" | custom-call | flops 19000000 | bytes 900000 | tf_op jit(solution)/shard_map/pallas_call | solution.py:28
  3.6 0.6 collective-permute-start.1
  4.2 0.0 copy-start.4
  4.2 2.1 %collective-permute-start = (bf16[9,32,576]{2,1,0:T(8,128)(2,1)S(1)}, bf16[9,32,576]{2,1,0:T(8,128)(2,1)S(1)}, u32[]{:S(2)}, u32[]{:S(2)}) collective-permute-start(bf16[9,32,576]{2,1,0:T(8,128)(2,1)S(1)} %get-tuple-element.13), channel_id=1, source_target_pairs={{0,128},{128,0},{1,129},{129,1},{2,130},{130,2},{3,131},{131,3},{4... | collective-permute-start | bytes 995336 | tf_op jit(solution)/shard_map/ppermute | solution.py:48
  6.2 10.0 %collective-permute-done.q = bf16[9,32,576]{2,1,0:T(8,128)(2,1)S(1)} collective-permute-done((bf16[9,32,576]{2,1,0:T(8,128)(2,1)S(1)}, bf16[9,32,576]{2,1,0:T(8,128)(2,1)S(1)}, u32[]{:S(2)}, u32[]{:S(2)}) %collective-permute-start) | collective-permute-done | bytes 331808 | tf_op jit(solution)/shard_map/ppermute | solution.py:48
  16.3 0.0 collective-permute-done.1.keys_other
  16.3 0.0 collective-permute-done.2.rest_0_.gate_other
  16.3 0.0 collective-permute-done.3.rest_1_.up_other
  16.3 0.0 collective-permute-done.4.rest_2_.down_other
  16.3 0.0 copy-start
  16.3 3.0 %shard_map.137 = (bf16[32,8,640]{2,1,0:T(8,128)(2,1)S(1)}, f32[16,128]{1,0:T(8,128)S(1)}) custom-call(s32[5]{0:T(128)S(1)} %stack.23.ids, bf16[9,32,576]{2,1,0:T(8,128)(2,1)S(1)} %collective-permute-done.q, bf16[16,64,576]{2,1,0:T(8,128)(2,1)S(1)} %get-tuple-element.14.keys_mine, bf16[16,64,576]{2,1,0:T(8,128)(2,1)S(1)} %collective-permute-done.1.keys_other, ...), custom_call_target="tpu_custom_call" | custom-call | flops 300000000 | bytes 4000000 | tf_op jit(solution)/shard_map/pallas_call | solution.py:28
  19.3 0.0 copy-start.1
  19.4 0.0 copy-start.2
  19.4 0.0 copy-start.5
  19.4 24.2 %all_to_all.20.got = bf16[32,8,640]{2,1,0:T(8,128)(2,1)S(1)} all-to-all(bf16[32,8,640]{2,1,0:T(8,128)(2,1)S(1)} %get-tuple-element.15), channel_id=1, replica_groups=mesh['role'=2,'dp'=2,'x'=4,'z'=8,'core'=2] {'x','z'}, dimensions={0} | all-to-all | bytes 655360 | tf_op jit(solution)/shard_map/all_to_all | solution.py:52
  43.6 0.0 copy-done.4
  43.6 0.0 copy-done
  43.6 1.2 %shard_map.138 = (f32[28,8,128]{2,1,0:T(8,128)S(1)}, bf16[28,8,128]{2,1,0:T(8,128)(2,1)S(1)}) custom-call(s32[5]{0:T(128)S(1)} %stack.23.ids, bf16[32,8,640]{2,1,0:T(8,128)(2,1)S(1)} %all_to_all.20.got, f32[16,128]{1,0:T(8,128)S(1)} %get-tuple-element.16.told, bf16[512,128]{1,0:T(8,128)(2,1)S(1)} %bitcast.27, bf16[128,7168]{1,0:T(8,128)(2,1)S(1)} %copy-done), custom_call_target="tpu_custom_call" | custom-call | flops 20000000 | bytes 2500000 | tf_op jit(solution)/shard_map/pallas_call | solution.py:28
  44.8 0.1 collective-permute-start.5
  44.8 1.2 %collective-permute-done.5.other = bf16[28,8,128]{2,1,0:T(8,128)(2,1)S(1)} collective-permute-done((bf16[28,8,128]{2,1,0:T(8,128)(2,1)S(1)}, bf16[28,8,128]{2,1,0:T(8,128)(2,1)S(1)}, u32[]{:S(2)}, u32[]{:S(2)}) %collective-permute-start.5) | collective-permute-done | bytes 57376 | tf_op jit(solution)/shard_map/ppermute | solution.py:48
  46.1 14.7 %all_to_all.21.got = bf16[32,8,128]{2,1,0:T(8,128)(2,1)S(1)} all-to-all(bf16[32,8,128]{2,1,0:T(8,128)(2,1)S(1)} %shard_map.139), channel_id=1, replica_groups=mesh['role'=2,'dp'=2,'x'=4,'z'=8,'core'=2] {'x','z'}, dimensions={0} | all-to-all | bytes 131072 | tf_op jit(solution)/shard_map/all_to_all | solution.py:52
  60.8 0.6 shard_map.140
  61.4 15.7 %all_to_all.22.rows = bf16[64,8,128]{2,1,0:T(8,128)(2,1)S(1)} all-to-all(bf16[64,8,128]{2,1,0:T(8,128)(2,1)S(1)} %shard_map.140), channel_id=1, replica_groups=mesh['role'=2,'dp'=2,'x'=4,'z'=8,'core'=2] {'dp','x','z'}, dimensions={0} | all-to-all | bytes 262144 | tf_op jit(solution)/shard_map/all_to_all | solution.py:52
  77.1 0.0 copy-done.1
  77.1 0.0 copy-done.2
  77.1 0.0 copy-done.5
  77.1 0.0 copy-start.3
  77.1 2.8 %shard_map.141.mine = f32[16,896]{1,0:T(8,128)S(1)} custom-call(s32[5]{0:T(128)S(1)} %stack.23.ids, bf16[64,8,128]{2,1,0:T(8,128)(2,1)S(1)} %all_to_all.22.rows, f32[56,128]{1,0:T(8,128)S(1)} %bitcast.28, bf16[7168,128]{1,0:T(8,128)(2,1)S(1)} %bitcast.22, bf16[7168,128]{1,0:T(8,128)(2,1)S(1)} %bitcast.24, ...), custom_call_target="tpu_custom_call" | custom-call | flops 60000000 | bytes 6000000 | tf_op jit(solution)/shard_map/pallas_call | solution.py:28
  79.9 0.1 collective-permute-start.6
  80.0 1.2 %collective-permute-done.6.other = f32[16,896]{1,0:T(8,128)S(1)} collective-permute-done((f32[16,896]{1,0:T(8,128)S(1)}, f32[16,896]{1,0:T(8,128)S(1)}, u32[]{:S(2)}, u32[]{:S(2)}) %collective-permute-start.6) | collective-permute-done | bytes 57376 | tf_op jit(solution)/shard_map/ppermute | solution.py:48
  81.2 0.0 copy-done.3
  81.2 1.3 %shard_map.142 = (bf16[64,8,128]{2,1,0:T(8,128)(2,1)S(1)}, f32[8,128]{1,0:T(8,128)S(1)}) custom-call(s32[5]{0:T(128)S(1)} %stack.23.ids, f32[16,896]{1,0:T(8,128)S(1)} %shard_map.141.mine, f32[16,896]{1,0:T(8,128)S(1)} %collective-permute-done.6.other, bf16[64,8,128]{2,1,0:T(8,128)(2,1)S(1)} %all_to_all.22.rows, bf16[128,7168]{1,0:T(8,128)(2,1)S(1)} %bitcast.26, ...), custom_call_target="tpu_custom_call" | custom-call | flops 60000000 | bytes 4000000 | tf_op jit(solution)/shard_map/pallas_call | solution.py:28
  82.6 15.5 %all_to_all.23.got = bf16[64,8,128]{2,1,0:T(8,128)(2,1)S(1)} all-to-all(bf16[64,8,128]{2,1,0:T(8,128)(2,1)S(1)} %get-tuple-element.19), channel_id=1, replica_groups=mesh['role'=2,'dp'=2,'x'=4,'z'=8,'core'=2] {'dp','x','z'}, dimensions={0} | all-to-all | bytes 262144 | tf_op jit(solution)/shard_map/all_to_all | solution.py:52
  98.1 0.1 shard_map.143
  98.2 0.7 collective-permute-start.7
  98.9 4.5 %collective-permute-done.7 = bf16[2,4,112]{2,1,0:T(4,128)(2,1)S(1)} collective-permute-done((bf16[2,4,112]{2,1,0:T(4,128)(2,1)S(1)}, bf16[2,4,112]{2,1,0:T(4,128)(2,1)S(1)}, u32[]{:S(2)}, u32[]{:S(2)}) %collective-permute-start.7) | collective-permute-done | bytes 1824 | tf_op jit(solution)/shard_map/ppermute | solution.py:48
  103.4 0.6 copy.17
  (1 shorter events, 0.0 us)
Async XLA Ops:
  0.0 16.3 %collective-permute-start.2 = (bf16[7168,128]{1,0:T(8,128)(2,1)}, bf16[7168,128]{1,0:T(8,128)(2,1)}, u32[]{:S(2)}, u32[]{:S(2)}) collective-permute-start(bf16[7168,128]{1,0:T(8,128)(2,1)} %bitcast.21), channel_id=1, source_target_pairs={{0,1},{1,0},{2,3},{3,2},{4,5},{5,4},{6,7},{7,6},{8,9},{9,8},{10,11... | collective-permute-start | bytes 5505032 | tf_op jit(solution)/shard_map/ppermute | solution.py:48
  0.0 16.3 %collective-permute-start.3 = (bf16[7168,128]{1,0:T(8,128)(2,1)}, bf16[7168,128]{1,0:T(8,128)(2,1)}, u32[]{:S(2)}, u32[]{:S(2)}) collective-permute-start(bf16[7168,128]{1,0:T(8,128)(2,1)} %bitcast.23), channel_id=1, source_target_pairs={{0,1},{1,0},{2,3},{3,2},{4,5},{5,4},{6,7},{7,6},{8,9},{9,8},{10,11... | collective-permute-start | bytes 5505032 | tf_op jit(solution)/shard_map/ppermute | solution.py:48
  0.5 15.8 %collective-permute-start.4 = (bf16[128,7168]{1,0:T(8,128)(2,1)}, bf16[128,7168]{1,0:T(8,128)(2,1)S(1)}, u32[]{:S(2)}, u32[]{:S(2)}) collective-permute-start(bf16[128,7168]{1,0:T(8,128)(2,1)} %bitcast.25), channel_id=1, source_target_pairs={{0,1},{1,0},{2,3},{3,2},{4,5},{5,4},{6,7},{7,6},{8,9},{9,8},{10,11... | collective-permute-start | bytes 5505032 | tf_op jit(solution)/shard_map/ppermute | solution.py:48
  3.6 12.7 %collective-permute-start.1 = (bf16[16,64,576]{2,1,0:T(8,128)(2,1)S(1)}, bf16[16,64,576]{2,1,0:T(8,128)(2,1)S(1)}, u32[]{:S(2)}, u32[]{:S(2)}) collective-permute-start(bf16[16,64,576]{2,1,0:T(8,128)(2,1)S(1)} %get-tuple-element.14.keys_mine), channel_id=1, source_target_pairs={{0,1},{1,0},{2,3},{3,2},{4,5},{5,4},{6,7},{7,6},{8,9},{9,8},{10,11... | collective-permute-start | bytes 3538952 | tf_op jit(solution)/shard_map/ppermute | solution.py:48
  4.2 39.4 %copy-start.4 = (bf16[1,512,128]{2,1,0:T(8,128)(2,1)S(1)}, bf16[1,512,128]{2,1,0:T(8,128)(2,1)}, u32[]{:S(2)}) copy-start(bf16[1,512,128]{2,1,0:T(8,128)(2,1)} %param.23) | copy-start | bytes 393220
  4.2 12.1 %collective-permute-start = (bf16[9,32,576]{2,1,0:T(8,128)(2,1)S(1)}, bf16[9,32,576]{2,1,0:T(8,128)(2,1)S(1)}, u32[]{:S(2)}, u32[]{:S(2)}) collective-permute-start(bf16[9,32,576]{2,1,0:T(8,128)(2,1)S(1)} %get-tuple-element.13), channel_id=1, source_target_pairs={{0,128},{128,0},{1,129},{129,1},{2,130},{130,2},{3,131},{131,3},{4... | collective-permute-start | bytes 995336 | tf_op jit(solution)/shard_map/ppermute | solution.py:48
  16.3 27.3 %copy-start = (bf16[128,7168]{1,0:T(8,128)(2,1)S(1)}, bf16[128,7168]{1,0:T(8,128)(2,1)}, u32[]{:S(2)}) copy-start(bf16[128,7168]{1,0:T(8,128)(2,1)} %proj.1) | copy-start | bytes 5505028
  19.3 57.7 %copy-start.1 = (bf16[1,7168,128]{2,1,0:T(8,128)(2,1)S(1)}, bf16[1,7168,128]{2,1,0:T(8,128)(2,1)}, u32[]{:S(2)}) copy-start(bf16[1,7168,128]{2,1,0:T(8,128)(2,1)} %param.25) | copy-start | bytes 5505028
  19.4 57.7 %copy-start.2 = (bf16[1,7168,128]{2,1,0:T(8,128)(2,1)S(1)}, bf16[1,7168,128]{2,1,0:T(8,128)(2,1)}, u32[]{:S(2)}) copy-start(bf16[1,7168,128]{2,1,0:T(8,128)(2,1)} %param.26) | copy-start | bytes 5505028
  19.4 57.7 %copy-start.5 = (f32[7168]{0:T(1024)S(1)}, f32[7168]{0:T(1024)}, u32[]{:S(2)}) copy-start(f32[7168]{0:T(1024)} %param.22) | copy-start | bytes 86020
  44.8 1.3 %collective-permute-start.5 = (bf16[28,8,128]{2,1,0:T(8,128)(2,1)S(1)}, bf16[28,8,128]{2,1,0:T(8,128)(2,1)S(1)}, u32[]{:S(2)}, u32[]{:S(2)}) collective-permute-start(bf16[28,8,128]{2,1,0:T(8,128)(2,1)S(1)} %get-tuple-element.18), channel_id=1, source_target_pairs={{0,1},{1,0},{2,3},{3,2},{4,5},{5,4},{6,7},{7,6},{8,9},{9,8},{10,11... | collective-permute-start | bytes 172040 | tf_op jit(solution)/shard_map/ppermute | solution.py:48
  77.1 4.2 %copy-start.3 = (bf16[1,128,7168]{2,1,0:T(8,128)(2,1)S(1)}, bf16[1,128,7168]{2,1,0:T(8,128)(2,1)}, u32[]{:S(2)}) copy-start(bf16[1,128,7168]{2,1,0:T(8,128)(2,1)} %param.27) | copy-start | bytes 5505028
  79.9 1.3 %collective-permute-start.6 = (f32[16,896]{1,0:T(8,128)S(1)}, f32[16,896]{1,0:T(8,128)S(1)}, u32[]{:S(2)}, u32[]{:S(2)}) collective-permute-start(f32[16,896]{1,0:T(8,128)S(1)} %shard_map.141.mine), channel_id=1, source_target_pairs={{0,1},{1,0},{2,3},{3,2},{4,5},{5,4},{6,7},{7,6},{8,9},{9,8},{10,11... | collective-permute-start | bytes 172040 | tf_op jit(solution)/shard_map/ppermute | solution.py:48
  98.2 5.2 %collective-permute-start.7 = (bf16[2,4,112]{2,1,0:T(4,128)(2,1)S(1)}, bf16[2,4,112]{2,1,0:T(4,128)(2,1)S(1)}, u32[]{:S(2)}, u32[]{:S(2)}) collective-permute-start(bf16[2,4,112]{2,1,0:T(4,128)(2,1)S(1)} %shard_map.143), channel_id=1, source_target_pairs={{0,128},{128,0},{1,129},{129,1},{2,130},{130,2},{3,131},{131,3},{4... | collective-permute-start | bytes 5384 | tf_op jit(solution)/shard_map/ppermute | solution.py:48

commit v3 on v2

--- a/solution.py
+++ b/solution.py
@@ -112,6 +112,16 @@
         one.wait()
 
 
+def stash_kernel(ids, *refs):
+    sources, outs, sems = refs[:4], refs[5:9], refs[9]
+    here = pl.ds(pl.multiple_of(ids[0] * HALF, 128), HALF)
+    copies = [pltpu.make_async_copy(sources[i].at[here], outs[i], sems.at[i]) for i in range(4)]
+    for one in copies:
+        one.start()
+    for one in copies:
+        one.wait()
+
+
 def attention_kernel(ids, q, keys_mine, keys_other, *rest):
     out, told, scratch = rest[-3:]
     lane = lax.broadcasted_iota(jnp.int32, (1, 512), 1)
@@ -125,34 +135,38 @@
     fresh = extra[0:16]
     row = lax.broadcasted_iota(jnp.int32, (64, 16), 0)
     col = lax.broadcasted_iota(jnp.int32, (64, 16), 1)
+    keys, scores, late, weights, late_weights, top, total = ([None] * 4 for _ in range(7))
     for r in range(4):
-        keys = jnp.concatenate(
+        keys[r] = jnp.concatenate(
             [side[4 * r + j] for side in (keys_mine, keys_other) for j in range(4)], axis=0
         )
         asked = jnp.concatenate([q[r], q[4 + r]], axis=0)
-        scores = lax.dot_general(
-            asked, keys, (((1,), (1,)), ((), ())), preferred_element_type=f32
-        )
-        late = lax.dot_general(
+        scores[r] = lax.dot_general(
+            asked, keys[r], (((1,), (1,)), ((), ())), preferred_element_type=f32
+        )
+        late[r] = lax.dot_general(
             asked, fresh, (((1,), (1,)), ((), ())), preferred_element_type=f32
         )
+    for r in range(4):
         usable = places < notes[0:1, 64 + r : 65 + r] * 128.0 + notes[0:1, 68 + r : 69 + r]
         counted = (ids[3] == 0) & ((col == r) | ((col == 4 + r) & (row >= 32)))
-        scores = jnp.where(usable, scores * SCORE_SCALE, MASK_VALUE)
-        late = jnp.where(counted, late * SCORE_SCALE, MASK_VALUE)
-        top = jnp.maximum(
-            jnp.max(scores, axis=1, keepdims=True), jnp.max(late, axis=1, keepdims=True)
-        )
-        weights = jnp.where(usable, jnp.exp(scores - top), 0.0)
-        late = jnp.where(counted, jnp.exp(late - top), 0.0)
-        total = jnp.sum(weights, axis=1, keepdims=True) + jnp.sum(late, axis=1, keepdims=True)
-        summed = jnp.dot(weights.astype(bf16), keys[:, :512], preferred_element_type=f32)
+        scaled = jnp.where(usable, scores[r] * SCORE_SCALE, MASK_VALUE)
+        late_scaled = jnp.where(counted, late[r] * SCORE_SCALE, MASK_VALUE)
+        top[r] = jnp.maximum(
+            jnp.max(scaled, axis=1, keepdims=True), jnp.max(late_scaled, axis=1, keepdims=True)
+        )
+        weights[r] = jnp.where(usable, jnp.exp(scaled - top[r]), 0.0)
+        late_weights[r] = jnp.where(counted, jnp.exp(late_scaled - top[r]), 0.0)
+        total[r] = jnp.sum(weights[r], axis=1, keepdims=True)
+        total[r] = total[r] + jnp.sum(late_weights[r], axis=1, keepdims=True)
+    for r in range(4):
+        summed = jnp.dot(weights[r].astype(bf16), keys[r][:, :512], preferred_element_type=f32)
         summed = summed + jnp.dot(
-            late.astype(bf16), fresh[:, :512], preferred_element_type=f32
-        )
-        live = total > 0.0
-        safe = jnp.where(live, total, 1.0)
-        level = jnp.where(live, top + jnp.log(safe), MASK_VALUE)
+            late_weights[r].astype(bf16), fresh[:, :512], preferred_element_type=f32
+        )
+        live = total[r] > 0.0
+        safe = jnp.where(live, total[r], 1.0)
+        level = jnp.where(live, top[r] + jnp.log(safe), MASK_VALUE)
         value = summed * (1.0 / safe)
         first, second, third = split(level)
         for s in range(2):
@@ -213,12 +227,11 @@
         both = jnp.concatenate(parts, axis=0) * gain[pl.ds(ids[0] * CHUNKS + k, 1), :]
         scaled[:, lanes] = both.astype(bf16)
         own[:, lanes] = jnp.where(ids[4] == 0, parts[0], parts[1])
-    here = pl.ds(pl.multiple_of(ids[0] * HALF, 128), HALF)
     asked = scaled[...]
-    out[:, 0:128] = jnp.dot(asked, gate[here, :], preferred_element_type=f32)
-    out[:, 128:256] = jnp.dot(asked, up[here, :], preferred_element_type=f32)
-    out[:, 256:384] = jnp.dot(asked, gate_other[here, :], preferred_element_type=f32)
-    out[:, 384:512] = jnp.dot(asked, up_other[here, :], preferred_element_type=f32)
+    out[:, 0:128] = jnp.dot(asked, gate[...], preferred_element_type=f32)
+    out[:, 128:256] = jnp.dot(asked, up[...], preferred_element_type=f32)
+    out[:, 256:384] = jnp.dot(asked, gate_other[...], preferred_element_type=f32)
+    out[:, 384:512] = jnp.dot(asked, up_other[...], preferred_element_type=f32)
     out[:, 512:640] = jnp.concatenate(squares, axis=0)
     shift = HALF - (ids[3] % 16) * (2 * BLOCK)
     turned = pltpu.roll(own[...], shift, 1)[:, 0:256]
@@ -328,7 +341,16 @@
     )
     q = swap(picked, "role")
     keys_other = swap(keys, "core")
-    after = (gate_other, up_other, down_other)[:EXTRA]
+    halves = pl.pallas_call(
+        stash_kernel,
+        out_shape=[pltpu.VMEM((HALF, 128), bf16)] * 4,
+        in_specs=[SM] + [FAR] * 4 + [ANY],
+        out_specs=[VM] * 4,
+        scratch_shapes=[pltpu.SemaphoreType.DMA((4,))],
+        compiler_params=pltpu.CompilerParams(vmem_limit_bytes=4 * MIB),
+        cost_estimate=pl.CostEstimate(flops=0, bytes_accessed=7400000, transcendentals=0),
+    )(ids, *[far(one) for one in (w_gate[0], w_up[0], gate_other, up_other)], picked)
+    after = (*halves, down_other)[:EXTRA]
     sent, told = call(
         attention_kernel,
         [shape(32, 8, 640), shape(16, 128, dtype=f32)],
@@ -371,7 +393,7 @@
         raise_kernel,
         shape(16, 896, dtype=f32),
         [SM] + [VM] * 6,
-        (ids, rows, norm_gain.reshape(56, 128), w_gate[0], w_up[0], gate_other, up_other),
+        (ids, rows, norm_gain.reshape(56, 128), *halves),
         60000000,
         6000000,
         [pltpu.VMEM((16, HALF), bf16), pltpu.VMEM((8, HALF), f32)],

time: 104 us -> 101 us (0.971)
  waiting for transfers between devices: 17 us -> 14.3 us
    ppermute x8, waiting for transfers between devices: 17 us -> 14.3 us  [swap(): return lax.ppermute(value, axis, [(0, 1), (1, 0)])]
    pallas_call x0 -> x1, Pallas kernels: none -> 2.59 us  [body(): pl.pallas_call(stash_kernel, out_shape=[pltpu.VMEM((HALF, 128), bf16)] *...]
    pallas_call x8, Pallas kernels: 12 us -> 9.46 us  [call(): pl.pallas_call(kernel, out_shape=outs, in_specs=specs, out_specs=[VM] * l...]
  transfers between devices with their start and end apart: 8 -> 8, of which waited for: 4 -> 5; matrix products, arithmetic and copies ran while one was open for 0% -> 0% of each run, Pallas kernels for 3% -> 5%
where the time goes in v3:
time: 101 us
  blocking collectives  69.8 us (69%)
  waiting for transfers between devices  14.3 us (14%)
  Pallas kernels  12 us (12%)
  starting transfers between devices  4.04 us (4%)
    all_to_all x4, blocking collectives, exchange(): return lax.all_to_all(value, axes, 0, 0, tiled=True)  69.8 us
    ppermute x8, waiting for transfers between devices, swap(): return lax.ppermute(value, axis, [(0, 1), (1, 0)])  14.3 us
    pallas_call x8, Pallas kernels, call(): pl.pallas_call(kernel, out_shape=outs, in_specs=specs, out_specs=[VM] * l...  9.46 us
    ppermute x8, starting transfers between devices, swap(): return lax.ppermute(value, axis, [(0, 1), (1, 0)])  4.04 us
    pallas_call x1, Pallas kernels, body(): pl.pallas_call(stash_kernel, out_shape=[pltpu.VMEM((HALF, 128), bf16)] *...  2.59 us
  transfers between devices with their start and end apart: 8, of which 5 were waited for; matrix products, arithmetic and copies ran while one was open for 0% of the time, Pallas kernels for 5%

profile of v3, /device:TPU:16, one launch (start us, length us, event | category | flops | bytes accessed | tf_op | source)
XLA Modules:
  0.0 101.0 jit_solution(6021501962613194509)
XLA Ops:
  0.0 0.0 collective-permute-start.2
  0.0 0.5 collective-permute-start.3
  0.5 0.0 collective-permute-start.4
  0.5 0.1 stack.23.ids
  0.6 3.0 %shard_map.136 = (bf16[9,32,576]{2,1,0:T(8,128)(2,1)S(1)}, bf16[16,64,576]{2,1,0:T(8,128)(2,1)S(1)}) custom-call(s32[5]{0:T(128)S(1)} %stack.23.ids, bf16[8,64,576]{2,1,0:T(8,128)(2,1)} %bitcast.30, bf16[2,4,576]{2,1,0:T(4,128)(2,1)} %bitcast.31, bf16[2,4,112]{2,1,0:T(4,128)(2,1)} %bitcast.36, s32[2,4,8]{2,1,0:T(4,128)} %bitcast.32, f32[2,4,8]{2,1,0:T(4,128)} %bitcast.33, ...), custom_call_target="tpu_custom_call" | custom-call | flops 19000000 | bytes 900000 | tf_op jit(solution)/shard_map/pallas_call | solution.py:28
  3.6 0.6 collective-permute-start.1
  4.2 2.1 %collective-permute-start = (bf16[9,32,576]{2,1,0:T(8,128)(2,1)S(1)}, bf16[9,32,576]{2,1,0:T(8,128)(2,1)S(1)}, u32[]{:S(2)}, u32[]{:S(2)}) collective-permute-start(bf16[9,32,576]{2,1,0:T(8,128)(2,1)S(1)} %get-tuple-element.17.refs_4_), channel_id=1, source_target_pairs={{0,128},{128,0},{1,129},{129,1},{2,130},{130,2},{3,131},{131,3},{4... | collective-permute-start | bytes 995336 | tf_op jit(solution)/shard_map/ppermute | solution.py:48
  6.2 0.0 collective-permute-done.2.refs_2_
  6.2 3.1 %collective-permute-done.3.refs_3_ = bf16[7168,128]{1,0:T(8,128)(2,1)} collective-permute-done((bf16[7168,128]{1,0:T(8,128)(2,1)}, bf16[7168,128]{1,0:T(8,128)(2,1)}, u32[]{:S(2)}, u32[]{:S(2)}) %collective-permute-start.3) | collective-permute-done | bytes 1835040 | tf_op jit(solution)/shard_map/ppermute | solution.py:48
  9.4 2.6 %shard_map.137 = (bf16[3584,128]{1,0:T(8,128)(2,1)S(1)}, bf16[3584,128]{1,0:T(8,128)(2,1)S(1)}, bf16[3584,128]{1,0:T(8,128)(2,1)S(1)}, bf16[3584,128]{1,0:T(8,128)(2,1)S(1)}) custom-call(s32[5]{0:T(128)S(1)} %stack.23.ids, bf16[7168,128]{1,0:T(8,128)(2,1)} %bitcast.26, bf16[7168,128]{1,0:T(8,128)(2,1)} %bitcast.28, ...), custom_call_target="tpu_custom_call" | custom-call | bytes 7400000 | tf_op jit(solution)/shard_map/pallas_call | solution.py:344
  12.0 4.3 %collective-permute-done.q = bf16[9,32,576]{2,1,0:T(8,128)(2,1)S(1)} collective-permute-done((bf16[9,32,576]{2,1,0:T(8,128)(2,1)S(1)}, bf16[9,32,576]{2,1,0:T(8,128)(2,1)S(1)}, u32[]{:S(2)}, u32[]{:S(2)}) %collective-permute-start) | collective-permute-done | bytes 331808 | tf_op jit(solution)/shard_map/ppermute | solution.py:48
  16.3 0.0 collective-permute-done.1.keys_other
  16.3 0.0 collective-permute-done.4.rest_4_.down_other
  16.3 0.0 copy-start
  16.3 0.0 copy-start.2
  16.3 2.1 %shard_map.138 = (bf16[32,8,640]{2,1,0:T(8,128)(2,1)S(1)}, f32[16,128]{1,0:T(8,128)S(1)}) custom-call(s32[5]{0:T(128)S(1)} %stack.23.ids, bf16[9,32,576]{2,1,0:T(8,128)(2,1)S(1)} %collective-permute-done.q, bf16[16,64,576]{2,1,0:T(8,128)(2,1)S(1)} %get-tuple-element.18.keys_mine, bf16[16,64,576]{2,1,0:T(8,128)(2,1)S(1)} %collective-permute-done.1.keys_other, ...), custom_call_target="tpu_custom_call" | custom-call | flops 300000000 | bytes 4000000 | tf_op jit(solution)/shard_map/pallas_call | solution.py:28
  18.4 0.0 copy-start.3
  18.4 23.9 %all_to_all.20.got = bf16[32,8,640]{2,1,0:T(8,128)(2,1)S(1)} all-to-all(bf16[32,8,640]{2,1,0:T(8,128)(2,1)S(1)} %get-tuple-element.23), channel_id=1, replica_groups=mesh['role'=2,'dp'=2,'x'=4,'z'=8,'core'=2] {'x','z'}, dimensions={0} | all-to-all | bytes 655360 | tf_op jit(solution)/shard_map/all_to_all | solution.py:52
  42.3 0.0 copy-done
  42.3 0.0 copy-done.2
  42.4 1.2 %shard_map.139 = (f32[28,8,128]{2,1,0:T(8,128)S(1)}, bf16[28,8,128]{2,1,0:T(8,128)(2,1)S(1)}) custom-call(s32[5]{0:T(128)S(1)} %stack.23.ids, bf16[32,8,640]{2,1,0:T(8,128)(2,1)S(1)} %all_to_all.20.got, f32[16,128]{1,0:T(8,128)S(1)} %get-tuple-element.24.told, bf16[512,128]{1,0:T(8,128)(2,1)S(1)} %bitcast.23, bf16[128,7168]{1,0:T(8,128)(2,1)S(1)} %copy-done), custom_call_target="tpu_custom_call" | custom-call | flops 20000000 | bytes 2500000 | tf_op jit(solution)/shard_map/pallas_call | solution.py:28
  43.5 0.1 collective-permute-start.5
  43.6 1.2 %collective-permute-done.5.other = bf16[28,8,128]{2,1,0:T(8,128)(2,1)S(1)} collective-permute-done((bf16[28,8,128]{2,1,0:T(8,128)(2,1)S(1)}, bf16[28,8,128]{2,1,0:T(8,128)(2,1)S(1)}, u32[]{:S(2)}, u32[]{:S(2)}) %collective-permute-start.5) | collective-permute-done | bytes 57376 | tf_op jit(solution)/shard_map/ppermute | solution.py:48
  44.8 14.7 %all_to_all.21.got = bf16[32,8,128]{2,1,0:T(8,128)(2,1)S(1)} all-to-all(bf16[32,8,128]{2,1,0:T(8,128)(2,1)S(1)} %shard_map.140), channel_id=1, replica_groups=mesh['role'=2,'dp'=2,'x'=4,'z'=8,'core'=2] {'x','z'}, dimensions={0} | all-to-all | bytes 131072 | tf_op jit(solution)/shard_map/all_to_all | solution.py:52
  59.5 0.6 shard_map.141
  60.1 15.7 %all_to_all.22.rows = bf16[64,8,128]{2,1,0:T(8,128)(2,1)S(1)} all-to-all(bf16[64,8,128]{2,1,0:T(8,128)(2,1)S(1)} %shard_map.141), channel_id=1, replica_groups=mesh['role'=2,'dp'=2,'x'=4,'z'=8,'core'=2] {'dp','x','z'}, dimensions={0} | all-to-all | bytes 262144 | tf_op jit(solution)/shard_map/all_to_all | solution.py:52
  75.8 0.0 copy-done.3
  75.8 0.0 copy-start.1
  75.8 1.2 %shard_map.142.mine = f32[16,896]{1,0:T(8,128)S(1)} custom-call(s32[5]{0:T(128)S(1)} %stack.23.ids, bf16[64,8,128]{2,1,0:T(8,128)(2,1)S(1)} %all_to_all.22.rows, f32[56,128]{1,0:T(8,128)S(1)} %bitcast.24, bf16[3584,128]{1,0:T(8,128)(2,1)S(1)} %get-tuple-element.19.rest_0_.gate, bf16[3584,128]{1,0:T(8,128)(2,1)S(1)} %get-tuple-element.20.rest_1_.up, ...), custom_call_target="tpu_custom_call" | custom-call | flops 60000000 | bytes 6000000 | tf_op jit(solution)/shard_map/pallas_call | solution.py:28
  77.0 0.1 collective-permute-start.6
  77.1 1.2 %collective-permute-done.6.other = f32[16,896]{1,0:T(8,128)S(1)} collective-permute-done((f32[16,896]{1,0:T(8,128)S(1)}, f32[16,896]{1,0:T(8,128)S(1)}, u32[]{:S(2)}, u32[]{:S(2)}) %collective-permute-start.6) | collective-permute-done | bytes 57376 | tf_op jit(solution)/shard_map/ppermute | solution.py:48
  78.3 0.0 copy-done.1
  78.3 1.3 %shard_map.143 = (bf16[64,8,128]{2,1,0:T(8,128)(2,1)S(1)}, f32[8,128]{1,0:T(8,128)S(1)}) custom-call(s32[5]{0:T(128)S(1)} %stack.23.ids, f32[16,896]{1,0:T(8,128)S(1)} %shard_map.142.mine, f32[16,896]{1,0:T(8,128)S(1)} %collective-permute-done.6.other, bf16[64,8,128]{2,1,0:T(8,128)(2,1)S(1)} %all_to_all.22.rows, bf16[128,7168]{1,0:T(8,128)(2,1)S(1)} %bitcast.22, ...), custom_call_target="tpu_custom_call" | custom-call | flops 60000000 | bytes 4000000 | tf_op jit(solution)/shard_map/pallas_call | solution.py:28
  79.7 15.5 %all_to_all.23.got = bf16[64,8,128]{2,1,0:T(8,128)(2,1)S(1)} all-to-all(bf16[64,8,128]{2,1,0:T(8,128)(2,1)S(1)} %get-tuple-element.27), channel_id=1, replica_groups=mesh['role'=2,'dp'=2,'x'=4,'z'=8,'core'=2] {'dp','x','z'}, dimensions={0} | all-to-all | bytes 262144 | tf_op jit(solution)/shard_map/all_to_all | solution.py:52
  95.2 0.1 shard_map.144
  95.3 0.7 collective-permute-start.7
  96.0 4.5 %collective-permute-done.7 = bf16[2,4,112]{2,1,0:T(4,128)(2,1)S(1)} collective-permute-done((bf16[2,4,112]{2,1,0:T(4,128)(2,1)S(1)}, bf16[2,4,112]{2,1,0:T(4,128)(2,1)S(1)}, u32[]{:S(2)}, u32[]{:S(2)}) %collective-permute-start.7) | collective-permute-done | bytes 1824 | tf_op jit(solution)/shard_map/ppermute | solution.py:48
  100.5 0.6 copy.17
  (1 shorter events, 0.0 us)
Async XLA Ops:
  0.0 6.2 %collective-permute-start.2 = (bf16[7168,128]{1,0:T(8,128)(2,1)}, bf16[7168,128]{1,0:T(8,128)(2,1)}, u32[]{:S(2)}, u32[]{:S(2)}) collective-permute-start(bf16[7168,128]{1,0:T(8,128)(2,1)} %bitcast.25), channel_id=1, source_target_pairs={{0,1},{1,0},{2,3},{3,2},{4,5},{5,4},{6,7},{7,6},{8,9},{9,8},{10,11... | collective-permute-start | bytes 5505032 | tf_op jit(solution)/shard_map/ppermute | solution.py:48
  0.0 9.4 %collective-permute-start.3 = (bf16[7168,128]{1,0:T(8,128)(2,1)}, bf16[7168,128]{1,0:T(8,128)(2,1)}, u32[]{:S(2)}, u32[]{:S(2)}) collective-permute-start(bf16[7168,128]{1,0:T(8,128)(2,1)} %bitcast.27), channel_id=1, source_target_pairs={{0,1},{1,0},{2,3},{3,2},{4,5},{5,4},{6,7},{7,6},{8,9},{9,8},{10,11... | collective-permute-start | bytes 5505032 | tf_op jit(solution)/shard_map/ppermute | solution.py:48
  0.5 15.7 %collective-permute-start.4 = (bf16[128,7168]{1,0:T(8,128)(2,1)}, bf16[128,7168]{1,0:T(8,128)(2,1)S(1)}, u32[]{:S(2)}, u32[]{:S(2)}) collective-permute-start(bf16[128,7168]{1,0:T(8,128)(2,1)} %bitcast.21), channel_id=1, source_target_pairs={{0,1},{1,0},{2,3},{3,2},{4,5},{5,4},{6,7},{7,6},{8,9},{9,8},{10,11... | collective-permute-start | bytes 5505032 | tf_op jit(solution)/shard_map/ppermute | solution.py:48
  3.6 12.7 %collective-permute-start.1 = (bf16[16,64,576]{2,1,0:T(8,128)(2,1)S(1)}, bf16[16,64,576]{2,1,0:T(8,128)(2,1)S(1)}, u32[]{:S(2)}, u32[]{:S(2)}) collective-permute-start(bf16[16,64,576]{2,1,0:T(8,128)(2,1)S(1)} %get-tuple-element.18.keys_mine), channel_id=1, source_target_pairs={{0,1},{1,0},{2,3},{3,2},{4,5},{5,4},{6,7},{7,6},{8,9},{9,8},{10,11... | collective-permute-start | bytes 3538952 | tf_op jit(solution)/shard_map/ppermute | solution.py:48
  4.2 12.1 %collective-permute-start = (bf16[9,32,576]{2,1,0:T(8,128)(2,1)S(1)}, bf16[9,32,576]{2,1,0:T(8,128)(2,1)S(1)}, u32[]{:S(2)}, u32[]{:S(2)}) collective-permute-start(bf16[9,32,576]{2,1,0:T(8,128)(2,1)S(1)} %get-tuple-element.17.refs_4_), channel_id=1, source_target_pairs={{0,128},{128,0},{1,129},{129,1},{2,130},{130,2},{3,131},{131,3},{4... | collective-permute-start | bytes 995336 | tf_op jit(solution)/shard_map/ppermute | solution.py:48
  16.3 26.1 %copy-start = (bf16[128,7168]{1,0:T(8,128)(2,1)S(1)}, bf16[128,7168]{1,0:T(8,128)(2,1)}, u32[]{:S(2)}) copy-start(bf16[128,7168]{1,0:T(8,128)(2,1)} %proj.1) | copy-start | bytes 5505028
  16.3 26.1 %copy-start.2 = (bf16[1,512,128]{2,1,0:T(8,128)(2,1)S(1)}, bf16[1,512,128]{2,1,0:T(8,128)(2,1)}, u32[]{:S(2)}) copy-start(bf16[1,512,128]{2,1,0:T(8,128)(2,1)} %param.23) | copy-start | bytes 393220
  18.4 57.4 %copy-start.3 = (f32[7168]{0:T(1024)S(1)}, f32[7168]{0:T(1024)}, u32[]{:S(2)}) copy-start(f32[7168]{0:T(1024)} %param.22) | copy-start | bytes 86020
  43.5 1.3 %collective-permute-start.5 = (bf16[28,8,128]{2,1,0:T(8,128)(2,1)S(1)}, bf16[28,8,128]{2,1,0:T(8,128)(2,1)S(1)}, u32[]{:S(2)}, u32[]{:S(2)}) collective-permute-start(bf16[28,8,128]{2,1,0:T(8,128)(2,1)S(1)} %get-tuple-element.26), channel_id=1, source_target_pairs={{0,1},{1,0},{2,3},{3,2},{4,5},{5,4},{6,7},{7,6},{8,9},{9,8},{10,11... | collective-permute-start | bytes 172040 | tf_op jit(solution)/shard_map/ppermute | solution.py:48
  75.8 2.5 %copy-start.1 = (bf16[1,128,7168]{2,1,0:T(8,128)(2,1)S(1)}, bf16[1,128,7168]{2,1,0:T(8,128)(2,1)}, u32[]{:S(2)}) copy-start(bf16[1,128,7168]{2,1,0:T(8,128)(2,1)} %param.27) | copy-start | bytes 5505028
  77.0 1.3 %collective-permute-start.6 = (f32[16,896]{1,0:T(8,128)S(1)}, f32[16,896]{1,0:T(8,128)S(1)}, u32[]{:S(2)}, u32[]{:S(2)}) collective-permute-start(f32[16,896]{1,0:T(8,128)S(1)} %shard_map.142.mine), channel_id=1, source_target_pairs={{0,1},{1,0},{2,3},{3,2},{4,5},{5,4},{6,7},{7,6},{8,9},{9,8},{10,11... | collective-permute-start | bytes 172040 | tf_op jit(solution)/shard_map/ppermute | solution.py:48
  95.3 5.2 %collective-permute-start.7 = (bf16[2,4,112]{2,1,0:T(4,128)(2,1)S(1)}, bf16[2,4,112]{2,1,0:T(4,128)(2,1)S(1)}, u32[]{:S(2)}, u32[]{:S(2)}) collective-permute-start(bf16[2,4,112]{2,1,0:T(4,128)(2,1)S(1)} %shard_map.144), channel_id=1, source_target_pairs={{0,128},{128,0},{1,129},{129,1},{2,130},{130,2},{3,131},{131,3},{4... | collective-permute-start | bytes 5384 | tf_op jit(solution)/shard_map/ppermute | solution.py:48

commit v4 on v3

--- a/solution.py
+++ b/solution.py
@@ -66,7 +66,8 @@
         )
         for i in range(4)
     ] + [pltpu.make_async_copy(sources[i], landed[i], sems.at[3 + i]) for i in range(1, 7)]
-    for one in copies:
+    copies[9].start()
+    for one in copies[:9]:
         one.start()
     queries, fresh, x_in, routes, gates, lengths, table = landed
     copies[9].wait()
@@ -88,7 +89,9 @@
         for k in range(5):
             lanes = slice(128 * k, min(128 * k + 128, 576))
             half = wide[k, pl.ds(64 * i + ids[0], 32, stride=2), :]
-            out[i, :, lanes] = half[:, 0 : lanes.stop - lanes.start].astype(bf16)
+            half = half[:, 0 : lanes.stop - lanes.start].astype(bf16)
+            out[2 * i, :, lanes] = half[0:16]
+            out[2 * i + 1, :, lanes] = half[16:32]
     lane = lax.broadcasted_iota(jnp.int32, (4, 128), 1)
     for one in copies[4:9]:
         one.wait()
@@ -106,16 +109,20 @@
         rows.append(fresh[s].astype(f32))
         block = jnp.concatenate([x_in[s].astype(f32), jnp.zeros((4, 16), f32)], axis=1)
         blocks.append(jnp.concatenate([block, note, jnp.zeros((4, 320), f32)], axis=1))
-    blank = [jnp.zeros((8, 576), f32)]
-    out[8] = jnp.concatenate(rows + blank + blocks + blank, axis=0).astype(bf16)
+    out[16] = jnp.concatenate(rows + blocks, axis=0).astype(bf16)
     for one in gathered:
         one.wait()
 
 
 def stash_kernel(ids, *refs):
-    sources, outs, sems = refs[:4], refs[5:9], refs[9]
+    sources, (raising, sems) = refs[:4], refs[5:]
     here = pl.ds(pl.multiple_of(ids[0] * HALF, 128), HALF)
-    copies = [pltpu.make_async_copy(sources[i].at[here], outs[i], sems.at[i]) for i in range(4)]
+    copies = [
+        pltpu.make_async_copy(
+            sources[i].at[here], raising.at[:, pl.ds(128 * i, 128)], sems.at[i]
+        )
+        for i in range(4)
+    ]
     for one in copies:
         one.start()
     for one in copies:
@@ -128,11 +135,11 @@
     start = jnp.where(lane < 256, ids[2] * 256, (ids[2] - 2 * ids[0]) * 256)
     places = (start + lane).astype(f32)
     slot = lax.broadcasted_iota(jnp.int32, (32, 128), 1)
-    extra = q[8]
-    notes = extra[16:32, 128:256].astype(f32)
-    told[0:8, :] = extra[16:32, 0:128].astype(f32)[0:8]
-    told[8:16, :] = notes[0:8]
-    fresh = extra[0:16]
+    fresh = q[16]
+    notes = fresh[:, 0:256].astype(f32)
+    told[0:8, :] = notes[8:16, 0:128]
+    told[8:16, :] = notes[8:16, 128:256]
+    notes = notes[8:9, 128:256]
     row = lax.broadcasted_iota(jnp.int32, (64, 16), 0)
     col = lax.broadcasted_iota(jnp.int32, (64, 16), 1)
     keys, scores, late, weights, late_weights, top, total = ([None] * 4 for _ in range(7))
@@ -140,7 +147,7 @@
         keys[r] = jnp.concatenate(
             [side[4 * r + j] for side in (keys_mine, keys_other) for j in range(4)], axis=0
         )
-        asked = jnp.concatenate([q[r], q[4 + r]], axis=0)
+        asked = jnp.concatenate([q[2 * r], q[2 * r + 1], q[2 * r + 8], q[2 * r + 9]], axis=0)
         scores[r] = lax.dot_general(
             asked, keys[r], (((1,), (1,)), ((), ())), preferred_element_type=f32
         )
@@ -183,7 +190,17 @@
         out[:, :, 128 * k : 128 * k + 128] = scratch[k].reshape(32, 8, 128).astype(bf16)
 
 
-def context_kernel(ids, got, told, value_up, proj, kept, sent):
+def project(ids, half, vals, told, proj, out):
+    lanes = pl.ds(pl.multiple_of(half * HALF, 128), HALF)
+    total = jnp.dot(vals[...], proj[:, lanes], preferred_element_type=f32)
+    start = jnp.concatenate([told[0:8, :], jnp.zeros((8, HALF - 128), f32)], axis=1)
+    start = pltpu.roll(start, (ids[2] % 32) * BLOCK, 1)
+    total = total + jnp.where(ids[2] // 32 == half, start, 0.0)
+    for k in range(CHUNKS):
+        out[k] = total[:, 128 * k : 128 * k + 128].astype(out.dtype)
+
+
+def context_kernel(ids, got, told, value_up, proj, vals, sent):
     level = jnp.sum(got[:, :, 512:640].astype(f32), axis=2, keepdims=True)
     factors = jnp.exp(level - jnp.max(level, axis=0, keepdims=True))
     denominator = jnp.sum(factors, axis=0)
@@ -191,15 +208,12 @@
     for i in range(32):
         numerator = numerator + factors[i] * got[i, :, 0:512].astype(f32)
     context = (numerator / denominator).astype(bf16)
-    vals = jnp.dot(context, value_up[...], preferred_element_type=f32).astype(bf16)
-    start = jnp.concatenate([told[0:8, :], jnp.zeros((8, HALF - 128), f32)], axis=1)
-    start = pltpu.roll(start, (ids[2] % 32) * BLOCK, 1)
-    for out, half in ((sent, 1 - ids[0]), (kept, ids[0])):
-        lanes = pl.ds(pl.multiple_of(half * HALF, 128), HALF)
-        total = jnp.dot(vals, proj[:, lanes], preferred_element_type=f32)
-        total = total + jnp.where(ids[2] // 32 == half, start, 0.0)
-        for k in range(CHUNKS):
-            out[k] = total[:, 128 * k : 128 * k + 128].astype(out.dtype)
+    vals[...] = jnp.dot(context, value_up[...], preferred_element_type=f32).astype(bf16)
+    project(ids, 1 - ids[0], vals, told, proj, sent)
+
+
+def kept_kernel(ids, vals, told, proj, kept):
+    project(ids, ids[0], vals, told, proj, kept)
 
 
 def join_kernel(kept, other, out):
@@ -218,7 +232,7 @@
         out[i] = piece
 
 
-def raise_kernel(ids, rows, gain, gate, up, gate_other, up_other, out, scaled, own):
+def raise_kernel(ids, rows, gain, weights, out, scaled, own):
     squares = [jnp.zeros((8, 128), f32) for _ in range(2)]
     for k in range(CHUNKS):
         lanes = slice(128 * k, 128 * k + 128)
@@ -227,11 +241,7 @@
         both = jnp.concatenate(parts, axis=0) * gain[pl.ds(ids[0] * CHUNKS + k, 1), :]
         scaled[:, lanes] = both.astype(bf16)
         own[:, lanes] = jnp.where(ids[4] == 0, parts[0], parts[1])
-    asked = scaled[...]
-    out[:, 0:128] = jnp.dot(asked, gate[...], preferred_element_type=f32)
-    out[:, 128:256] = jnp.dot(asked, up[...], preferred_element_type=f32)
-    out[:, 256:384] = jnp.dot(asked, gate_other[...], preferred_element_type=f32)
-    out[:, 384:512] = jnp.dot(asked, up_other[...], preferred_element_type=f32)
+    out[:, 0:512] = jnp.dot(scaled[...], weights[...], preferred_element_type=f32)
     out[:, 512:640] = jnp.concatenate(squares, axis=0)
     shift = HALF - (ids[3] % 16) * (2 * BLOCK)
     turned = pltpu.roll(own[...], shift, 1)[:, 0:256]
@@ -329,7 +339,7 @@
     )
     picked, keys = call(
         pick_kernel,
-        [shape(9, 32, 576), shape(16, 64, 576)],
+        [shape(17, 16, 576), shape(16, 64, 576)],
         [SM] + [FAR] * 8,
         (ids,) + tuple(far(one) for one in given + (prompt_pool[0, 0, 0],)),
         19000000,
@@ -341,16 +351,20 @@
     )
     q = swap(picked, "role")
     keys_other = swap(keys, "core")
-    halves = pl.pallas_call(
+    raising = pl.pallas_call(
         stash_kernel,
-        out_shape=[pltpu.VMEM((HALF, 128), bf16)] * 4,
+        out_shape=pltpu.VMEM((HALF, 512), bf16),
         in_specs=[SM] + [FAR] * 4 + [ANY],
-        out_specs=[VM] * 4,
+        out_specs=VM,
         scratch_shapes=[pltpu.SemaphoreType.DMA((4,))],
         compiler_params=pltpu.CompilerParams(vmem_limit_bytes=4 * MIB),
         cost_estimate=pl.CostEstimate(flops=0, bytes_accessed=7400000, transcendentals=0),
-    )(ids, *[far(one) for one in (w_gate[0], w_up[0], gate_other, up_other)], picked)
-    after = (*halves, down_other)[:EXTRA]
+    )(
+        ids,
+        *[far(one) for one in (w_gate[0], w_up[0], gate_other, up_other)],
+        picked,
+    )
+    after = (raising, down_other)
     sent, told = call(
         attention_kernel,
         [shape(32, 8, 640), shape(16, 128, dtype=f32)],
@@ -363,13 +377,23 @@
         131072,
     )
     got = exchange(sent, XZ)
-    kept, passed = call(
+    vals, passed = call(
         context_kernel,
-        [shape(CHUNKS, 8, 128, dtype=f32), shape(CHUNKS, 8, 128)],
+        [shape(8, 128), shape(CHUNKS, 8, 128)],
         [SM] + [VM] * 4,
         (ids, got, told, value_up[0], out_proj),
-        20000000,
-        2500000,
+        12000000,
+        1500000,
+        (),
+        8,
+    )
+    kept = call(
+        kept_kernel,
+        shape(CHUNKS, 8, 128, dtype=f32),
+        [SM] + [VM] * 3,
+        (ids, vals, told, out_proj),
+        8000000,
+        1000000,
         (),
         8,
     )
@@ -392,8 +416,8 @@
     raised = call(
         raise_kernel,
         shape(16, 896, dtype=f32),
-        [SM] + [VM] * 6,
-        (ids, rows, norm_gain.reshape(56, 128), *halves),
+        [SM] + [VM] * 3,
+        (ids, rows, norm_gain.reshape(56, 128), raising),
         60000000,
         6000000,
         [pltpu.VMEM((16, HALF), bf16), pltpu.VMEM((8, HALF), f32)],
@@ -415,9 +439,6 @@
         finish_kernel, shape(2, 4, BLOCK), [VM] * 2, (exchange(outgoing, DXZ), own), 70000, 140000, (), 4
     )
     return swap(done, "role").reshape(2, 1, 1, 4, BLOCK)
-
-
-EXTRA = 6
 
 
 def solution(mesh):

time: 101 us -> 101 us (level)
  waiting for transfers between devices: 14.3 us -> 13.2 us
    ppermute x8, waiting for transfers between devices: 14.3 us -> 13.2 us  [swap(): return lax.ppermute(value, axis, [(0, 1), (1, 0)])]
    pallas_call x8 -> x9, Pallas kernels: 9.46 us -> 9.93 us  [call(): pl.pallas_call(kernel, out_shape=outs, in_specs=specs, out_specs=[VM] * l...]
  transfers between devices with their start and end apart: 8 -> 8, of which waited for: 5 -> 5; matrix products, arithmetic and copies ran while one was open for 0% -> 0% of each run, Pallas kernels for 5% -> 6%
where the time goes in v4:
time: 101 us; the launch traced here: 100 us
  blocking collectives  69.8 us (69%)
  waiting for transfers between devices  13.2 us (13%)
  Pallas kernels  12.5 us (12%)
  starting transfers between devices  3.98 us (4%)
    all_to_all x4, blocking collectives, exchange(): return lax.all_to_all(value, axes, 0, 0, tiled=True)  69.8 us
    ppermute x8, waiting for transfers between devices, swap(): return lax.ppermute(value, axis, [(0, 1), (1, 0)])  13.2 us
    pallas_call x9, Pallas kernels, call(): pl.pallas_call(kernel, out_shape=outs, in_specs=specs, out_specs=[VM] * l...  9.93 us
    ppermute x8, starting transfers between devices, swap(): return lax.ppermute(value, axis, [(0, 1), (1, 0)])  3.98 us
    pallas_call x1, Pallas kernels, body(): pl.pallas_call(stash_kernel, out_shape=pltpu.VMEM((HALF, 512), bf16), in_...  2.59 us
  transfers between devices with their start and end apart: 8, of which 5 were waited for; matrix products, arithmetic and copies ran while one was open for 0% of the time, Pallas kernels for 6%

profile of v4, /device:TPU:16, one launch (start us, length us, event | category | flops | bytes accessed | tf_op | source)
XLA Modules:
  0.0 100.3 jit_solution(18236686742282447021)
XLA Ops:
  0.0 0.0 collective-permute-start.2
  0.0 0.5 collective-permute-start.3
  0.5 0.0 collective-permute-start.4
  0.5 0.1 stack.23.ids
  0.6 2.8 %shard_map.136 = (bf16[17,16,576]{2,1,0:T(8,128)(2,1)S(1)}, bf16[16,64,576]{2,1,0:T(8,128)(2,1)S(1)}) custom-call(s32[5]{0:T(128)S(1)} %stack.23.ids, bf16[8,64,576]{2,1,0:T(8,128)(2,1)} %bitcast.30, bf16[2,4,576]{2,1,0:T(4,128)(2,1)} %bitcast.31, bf16[2,4,112]{2,1,0:T(4,128)(2,1)} %bitcast.36, s32[2,4,8]{2,1,0:T(4,128)} %bitcast.32, f32[2,4,8]{2,1,0:T(4,128)} %bitcast.33, ...), custom_call_target="tpu_custom_call" | custom-call | flops 19000000 | bytes 900000 | tf_op jit(solution)/shard_map/pallas_call | solution.py:28
  3.4 0.6 collective-permute-start.1
  4.0 2.1 %collective-permute-start = (bf16[17,16,576]{2,1,0:T(8,128)(2,1)S(1)}, bf16[17,16,576]{2,1,0:T(8,128)(2,1)S(1)}, u32[]{:S(2)}, u32[]{:S(2)}) collective-permute-start(bf16[17,16,576]{2,1,0:T(8,128)(2,1)S(1)} %get-tuple-element.13.refs_4_), channel_id=1, source_target_pairs={{0,128},{128,0},{1,129},{129,1},{2,130},{130,2},{3,131},{131,3},{4... | collective-permute-start | bytes 940040 | tf_op jit(solution)/shard_map/ppermute | solution.py:48
  6.1 0.0 collective-permute-done.2.refs_2_
  6.1 3.3 %collective-permute-done.3.refs_3_ = bf16[7168,128]{1,0:T(8,128)(2,1)} collective-permute-done((bf16[7168,128]{1,0:T(8,128)(2,1)}, bf16[7168,128]{1,0:T(8,128)(2,1)}, u32[]{:S(2)}, u32[]{:S(2)}) %collective-permute-start.3) | collective-permute-done | bytes 1835040 | tf_op jit(solution)/shard_map/ppermute | solution.py:48
  9.4 2.6 %shard_map.137.rest_0_.weights = bf16[3584,512]{1,0:T(8,128)(2,1)S(1)} custom-call(s32[5]{0:T(128)S(1)} %stack.23.ids, bf16[7168,128]{1,0:T(8,128)(2,1)} %bitcast.26, bf16[7168,128]{1,0:T(8,128)(2,1)} %bitcast.28, bf16[7168,128]{1,0:T(8,128)(2,1)} %collective-permute-done.2.refs_2_, bf16[7168,128]{1,0:T(8,128)(2,1)} %collective-permute-done.3.refs_3_, ...), custom_call_target="tpu_custom_call" | custom-call | bytes 7400000 | tf_op jit(solution)/shard_map/pallas_call | solution.py:354
  12.0 0.0 copy-start.2
  12.0 3.7 %collective-permute-done.q = bf16[17,16,576]{2,1,0:T(8,128)(2,1)S(1)} collective-permute-done((bf16[17,16,576]{2,1,0:T(8,128)(2,1)S(1)}, bf16[17,16,576]{2,1,0:T(8,128)(2,1)S(1)}, u32[]{:S(2)}, u32[]{:S(2)}) %collective-permute-start) | collective-permute-done | bytes 313376 | tf_op jit(solution)/shard_map/ppermute | solution.py:48
  15.7 0.0 collective-permute-done.1.keys_other
  15.7 0.0 collective-permute-done.4.rest_1_.down_other
  15.7 0.0 copy-start
  15.7 2.1 %shard_map.138 = (bf16[32,8,640]{2,1,0:T(8,128)(2,1)S(1)}, f32[16,128]{1,0:T(8,128)S(1)}) custom-call(s32[5]{0:T(128)S(1)} %stack.23.ids, bf16[17,16,576]{2,1,0:T(8,128)(2,1)S(1)} %collective-permute-done.q, bf16[16,64,576]{2,1,0:T(8,128)(2,1)S(1)} %get-tuple-element.14.keys_mine, bf16[16,64,576]{2,1,0:T(8,128)(2,1)S(1)} %collective-permute-done.1.keys_other, ...), custom_call_target="tpu_custom_call" | custom-call | flops 300000000 | bytes 4000000 | tf_op jit(solution)/shard_map/pallas_call | solution.py:28
  17.8 23.9 %all_to_all.20.got = bf16[32,8,640]{2,1,0:T(8,128)(2,1)S(1)} all-to-all(bf16[32,8,640]{2,1,0:T(8,128)(2,1)S(1)} %get-tuple-element.15), channel_id=1, replica_groups=mesh['role'=2,'dp'=2,'x'=4,'z'=8,'core'=2] {'x','z'}, dimensions={0} | all-to-all | bytes 655360 | tf_op jit(solution)/shard_map/all_to_all | solution.py:52
  41.8 0.0 copy-done.2
  41.8 0.0 copy-done
  41.8 1.1 %shard_map.139 = (bf16[8,128]{1,0:T(8,128)(2,1)S(1)}, bf16[28,8,128]{2,1,0:T(8,128)(2,1)S(1)}) custom-call(s32[5]{0:T(128)S(1)} %stack.23.ids, bf16[32,8,640]{2,1,0:T(8,128)(2,1)S(1)} %all_to_all.20.got, f32[16,128]{1,0:T(8,128)S(1)} %get-tuple-element.16.told, bf16[512,128]{1,0:T(8,128)(2,1)S(1)} %bitcast.23, bf16[128,7168]{1,0:T(8,128)(2,1)S(1)} %copy-done), custom_call_target="tpu_custom_call" | custom-call | flops 12000000 | bytes 1500000 | tf_op jit(solution)/shard_map/pallas_call | solution.py:28
  42.8 0.0 copy-start.3
  42.8 0.1 collective-permute-start.5
  42.9 0.8 shard_map.140.kept
  43.7 0.5 collective-permute-done.5.other
  44.2 14.7 %all_to_all.21.got = bf16[32,8,128]{2,1,0:T(8,128)(2,1)S(1)} all-to-all(bf16[32,8,128]{2,1,0:T(8,128)(2,1)S(1)} %shard_map.141), channel_id=1, replica_groups=mesh['role'=2,'dp'=2,'x'=4,'z'=8,'core'=2] {'x','z'}, dimensions={0} | all-to-all | bytes 131072 | tf_op jit(solution)/shard_map/all_to_all | solution.py:52
  58.9 0.6 shard_map.142
  59.5 15.7 %all_to_all.22.rows = bf16[64,8,128]{2,1,0:T(8,128)(2,1)S(1)} all-to-all(bf16[64,8,128]{2,1,0:T(8,128)(2,1)S(1)} %shard_map.142), channel_id=1, replica_groups=mesh['role'=2,'dp'=2,'x'=4,'z'=8,'core'=2] {'dp','x','z'}, dimensions={0} | all-to-all | bytes 262144 | tf_op jit(solution)/shard_map/all_to_all | solution.py:52
  75.2 0.0 copy-done.3
  75.2 0.0 copy-start.1
  75.2 1.1 %shard_map.143.mine = f32[16,896]{1,0:T(8,128)S(1)} custom-call(s32[5]{0:T(128)S(1)} %stack.23.ids, bf16[64,8,128]{2,1,0:T(8,128)(2,1)S(1)} %all_to_all.22.rows, f32[56,128]{1,0:T(8,128)S(1)} %bitcast.24, bf16[3584,512]{1,0:T(8,128)(2,1)S(1)} %shard_map.137.rest_0_.weights), custom_call_target="tpu_custom_call" | custom-call | flops 60000000 | bytes 6000000 | tf_op jit(solution)/shard_map/pallas_call | solution.py:28
  76.3 0.0 collective-permute-start.6
  76.3 1.3 %collective-permute-done.6.other = f32[16,896]{1,0:T(8,128)S(1)} collective-permute-done((f32[16,896]{1,0:T(8,128)S(1)}, f32[16,896]{1,0:T(8,128)S(1)}, u32[]{:S(2)}, u32[]{:S(2)}) %collective-permute-start.6) | collective-permute-done | bytes 57376 | tf_op jit(solution)/shard_map/ppermute | solution.py:48
  77.5 0.0 copy-done.1
  77.6 1.3 %shard_map.144 = (bf16[64,8,128]{2,1,0:T(8,128)(2,1)S(1)}, f32[8,128]{1,0:T(8,128)S(1)}) custom-call(s32[5]{0:T(128)S(1)} %stack.23.ids, f32[16,896]{1,0:T(8,128)S(1)} %shard_map.143.mine, f32[16,896]{1,0:T(8,128)S(1)} %collective-permute-done.6.other, bf16[64,8,128]{2,1,0:T(8,128)(2,1)S(1)} %all_to_all.22.rows, bf16[128,7168]{1,0:T(8,128)(2,1)S(1)} %bitcast.22, ...), custom_call_target="tpu_custom_call" | custom-call | flops 60000000 | bytes 4000000 | tf_op jit(solution)/shard_map/pallas_call | solution.py:28
  78.9 15.5 %all_to_all.23.got = bf16[64,8,128]{2,1,0:T(8,128)(2,1)S(1)} all-to-all(bf16[64,8,128]{2,1,0:T(8,128)(2,1)S(1)} %get-tuple-element.19), channel_id=1, replica_groups=mesh['role'=2,'dp'=2,'x'=4,'z'=8,'core'=2] {'dp','x','z'}, dimensions={0} | all-to-all | bytes 262144 | tf_op jit(solution)/shard_map/all_to_all | solution.py:52
  94.4 0.1 shard_map.145
  94.5 0.7 collective-permute-start.7
  95.2 4.5 %collective-permute-done.7 = bf16[2,4,112]{2,1,0:T(4,128)(2,1)S(1)} collective-permute-done((bf16[2,4,112]{2,1,0:T(4,128)(2,1)S(1)}, bf16[2,4,112]{2,1,0:T(4,128)(2,1)S(1)}, u32[]{:S(2)}, u32[]{:S(2)}) %collective-permute-start.7) | collective-permute-done | bytes 1824 | tf_op jit(solution)/shard_map/ppermute | solution.py:48
  99.7 0.6 copy.17
  (1 shorter events, 0.0 us)
Async XLA Ops:
  0.0 6.1 %collective-permute-start.2 = (bf16[7168,128]{1,0:T(8,128)(2,1)}, bf16[7168,128]{1,0:T(8,128)(2,1)}, u32[]{:S(2)}, u32[]{:S(2)}) collective-permute-start(bf16[7168,128]{1,0:T(8,128)(2,1)} %bitcast.25), channel_id=1, source_target_pairs={{0,1},{1,0},{2,3},{3,2},{4,5},{5,4},{6,7},{7,6},{8,9},{9,8},{10,11... | collective-permute-start | bytes 5505032 | tf_op jit(solution)/shard_map/ppermute | solution.py:48
  0.0 9.4 %collective-permute-start.3 = (bf16[7168,128]{1,0:T(8,128)(2,1)}, bf16[7168,128]{1,0:T(8,128)(2,1)}, u32[]{:S(2)}, u32[]{:S(2)}) collective-permute-start(bf16[7168,128]{1,0:T(8,128)(2,1)} %bitcast.27), channel_id=1, source_target_pairs={{0,1},{1,0},{2,3},{3,2},{4,5},{5,4},{6,7},{7,6},{8,9},{9,8},{10,11... | collective-permute-start | bytes 5505032 | tf_op jit(solution)/shard_map/ppermute | solution.py:48
  0.5 15.2 %collective-permute-start.4 = (bf16[128,7168]{1,0:T(8,128)(2,1)}, bf16[128,7168]{1,0:T(8,128)(2,1)S(1)}, u32[]{:S(2)}, u32[]{:S(2)}) collective-permute-start(bf16[128,7168]{1,0:T(8,128)(2,1)} %bitcast.21), channel_id=1, source_target_pairs={{0,1},{1,0},{2,3},{3,2},{4,5},{5,4},{6,7},{7,6},{8,9},{9,8},{10,11... | collective-permute-start | bytes 5505032 | tf_op jit(solution)/shard_map/ppermute | solution.py:48
  3.4 12.3 %collective-permute-start.1 = (bf16[16,64,576]{2,1,0:T(8,128)(2,1)S(1)}, bf16[16,64,576]{2,1,0:T(8,128)(2,1)S(1)}, u32[]{:S(2)}, u32[]{:S(2)}) collective-permute-start(bf16[16,64,576]{2,1,0:T(8,128)(2,1)S(1)} %get-tuple-element.14.keys_mine), channel_id=1, source_target_pairs={{0,1},{1,0},{2,3},{3,2},{4,5},{5,4},{6,7},{7,6},{8,9},{9,8},{10,11... | collective-permute-start | bytes 3538952 | tf_op jit(solution)/shard_map/ppermute | solution.py:48
  4.0 11.7 %collective-permute-start = (bf16[17,16,576]{2,1,0:T(8,128)(2,1)S(1)}, bf16[17,16,576]{2,1,0:T(8,128)(2,1)S(1)}, u32[]{:S(2)}, u32[]{:S(2)}) collective-permute-start(bf16[17,16,576]{2,1,0:T(8,128)(2,1)S(1)} %get-tuple-element.13.refs_4_), channel_id=1, source_target_pairs={{0,128},{128,0},{1,129},{129,1},{2,130},{130,2},{3,131},{131,3},{4... | collective-permute-start | bytes 940040 | tf_op jit(solution)/shard_map/ppermute | solution.py:48
  12.0 29.8 %copy-start.2 = (bf16[1,512,128]{2,1,0:T(8,128)(2,1)S(1)}, bf16[1,512,128]{2,1,0:T(8,128)(2,1)}, u32[]{:S(2)}) copy-start(bf16[1,512,128]{2,1,0:T(8,128)(2,1)} %param.23) | copy-start | bytes 393220
  15.7 26.1 %copy-start = (bf16[128,7168]{1,0:T(8,128)(2,1)S(1)}, bf16[128,7168]{1,0:T(8,128)(2,1)}, u32[]{:S(2)}) copy-start(bf16[128,7168]{1,0:T(8,128)(2,1)} %proj.3) | copy-start | bytes 5505028
  42.8 32.3 %copy-start.3 = (f32[7168]{0:T(1024)S(1)}, f32[7168]{0:T(1024)}, u32[]{:S(2)}) copy-start(f32[7168]{0:T(1024)} %param.22) | copy-start | bytes 86020
  42.8 1.3 %collective-permute-start.5 = (bf16[28,8,128]{2,1,0:T(8,128)(2,1)S(1)}, bf16[28,8,128]{2,1,0:T(8,128)(2,1)S(1)}, u32[]{:S(2)}, u32[]{:S(2)}) collective-permute-start(bf16[28,8,128]{2,1,0:T(8,128)(2,1)S(1)} %get-tuple-element.18), channel_id=1, source_target_pairs={{0,1},{1,0},{2,3},{3,2},{4,5},{5,4},{6,7},{7,6},{8,9},{9,8},{10,11... | collective-permute-start | bytes 172040 | tf_op jit(solution)/shard_map/ppermute | solution.py:48
  75.2 2.4 %copy-start.1 = (bf16[1,128,7168]{2,1,0:T(8,128)(2,1)S(1)}, bf16[1,128,7168]{2,1,0:T(8,128)(2,1)}, u32[]{:S(2)}) copy-start(bf16[1,128,7168]{2,1,0:T(8,128)(2,1)} %param.27) | copy-start | bytes 5505028
  76.3 1.3 %collective-permute-start.6 = (f32[16,896]{1,0:T(8,128)S(1)}, f32[16,896]{1,0:T(8,128)S(1)}, u32[]{:S(2)}, u32[]{:S(2)}) collective-permute-start(f32[16,896]{1,0:T(8,128)S(1)} %shard_map.143.mine), channel_id=1, source_target_pairs={{0,1},{1,0},{2,3},{3,2},{4,5},{5,4},{6,7},{7,6},{8,9},{9,8},{10,11... | collective-permute-start | bytes 172040 | tf_op jit(solution)/shard_map/ppermute | solution.py:48
  94.5 5.2 %collective-permute-start.7 = (bf16[2,4,112]{2,1,0:T(4,128)(2,1)S(1)}, bf16[2,4,112]{2,1,0:T(4,128)(2,1)S(1)}, u32[]{:S(2)}, u32[]{:S(2)}) collective-permute-start(bf16[2,4,112]{2,1,0:T(4,128)(2,1)S(1)} %shard_map.145), channel_id=1, source_target_pairs={{0,128},{128,0},{1,129},{129,1},{2,130},{130,2},{3,131},{131,3},{4... | collective-permute-start | bytes 5384 | tf_op jit(solution)/shard_map/ppermute | solution.py:48

commit v5 on v4

--- a/solution.py
+++ b/solution.py
@@ -17,7 +17,6 @@
 f32 = jnp.float32
 
 VM = pl.BlockSpec(memory_space=pltpu.VMEM)
-SM = pl.BlockSpec(memory_space=pltpu.SMEM)
 ANY = pl.BlockSpec(memory_space=pl.ANY)
 FAR = pl.BlockSpec(memory_space=pltpu.HBM)
 MIB = 1024 * 1024
@@ -52,13 +51,20 @@
     return lax.all_to_all(value, axes, 0, 0, tiled=True)
 
 
+def spot():
+    core = lax.axis_index("core")
+    chip = lax.axis_index("x") * 8 + lax.axis_index("z")
+    return core, 1 - lax.axis_index("role"), chip * 2 + core, chip, lax.axis_index("dp")
+
+
 def split(value):
     first = value.astype(bf16).astype(f32)
     second = (value - first).astype(bf16).astype(f32)
     return first, second, (value - first) - second
 
 
-def pick_kernel(ids, *refs):
+def pick_kernel(*refs):
+    ids = spot()
     sources, pool, (out, keys), landed, (wide, sems) = refs[:7], refs[7], refs[8:10], refs[10:17], refs[17:]
     copies = [
         pltpu.make_async_copy(
@@ -114,7 +120,8 @@
         one.wait()
 
 
-def stash_kernel(ids, *refs):
+def stash_kernel(*refs):
+    ids = spot()
     sources, (raising, sems) = refs[:4], refs[5:]
     here = pl.ds(pl.multiple_of(ids[0] * HALF, 128), HALF)
     copies = [
@@ -129,7 +136,8 @@
         one.wait()
 
 
-def attention_kernel(ids, q, keys_mine, keys_other, *rest):
+def attention_kernel(q, keys_mine, keys_other, *rest):
+    ids = spot()
     out, told, scratch = rest[-3:]
     lane = lax.broadcasted_iota(jnp.int32, (1, 512), 1)
     start = jnp.where(lane < 256, ids[2] * 256, (ids[2] - 2 * ids[0]) * 256)
@@ -200,7 +208,8 @@
         out[k] = total[:, 128 * k : 128 * k + 128].astype(out.dtype)
 
 
-def context_kernel(ids, got, told, value_up, proj, vals, sent):
+def context_kernel(got, told, value_up, proj, vals, sent):
+    ids = spot()
     level = jnp.sum(got[:, :, 512:640].astype(f32), axis=2, keepdims=True)
     factors = jnp.exp(level - jnp.max(level, axis=0, keepdims=True))
     denominator = jnp.sum(factors, axis=0)
@@ -212,7 +221,8 @@
     project(ids, 1 - ids[0], vals, told, proj, sent)
 
 
-def kept_kernel(ids, vals, told, proj, kept):
+def kept_kernel(vals, told, proj, kept):
+    ids = spot()
     project(ids, ids[0], vals, told, proj, kept)
 
 
@@ -223,7 +233,8 @@
         out[k] = jnp.zeros((8, 128), bf16)
 
 
-def spread_kernel(ids, got, told, out):
+def spread_kernel(got, told, out):
+    ids = spot()
     total = got[0].astype(f32)
     for i in range(1, 32):
         total = total + got[i].astype(f32)
@@ -232,7 +243,8 @@
         out[i] = piece
 
 
-def raise_kernel(ids, rows, gain, weights, out, scaled, own):
+def raise_kernel(rows, gain, weights, out, scaled, own):
+    ids = spot()
     squares = [jnp.zeros((8, 128), f32) for _ in range(2)]
     for k in range(CHUNKS):
         lanes = slice(128 * k, 128 * k + 128)
@@ -249,7 +261,8 @@
     out[8:16, 640:896] = jnp.zeros((8, 256), f32)
 
 
-def lower_kernel(ids, mine, other, rows, down, down_other, out, own, product):
+def lower_kernel(mine, other, rows, down, down_other, out, own, product):
+    ids = spot()
     squares = jnp.sum(mine[:, 512:640] + other[:, 512:640], axis=1, keepdims=True)
     scale = lax.rsqrt(squares * (1.0 / (2 * HALF)) + EPSILON)
 
@@ -319,12 +332,6 @@
     w_up,
     w_down,
 ):
-    role = lax.axis_index("role")
-    dp = lax.axis_index("dp")
-    core = lax.axis_index("core")
-    chip = lax.axis_index("x") * lax.axis_size("z") + lax.axis_index("z")
-    ids = jnp.stack([core, 1 - role, chip * 2 + core, chip, dp]).astype(jnp.int32)
-    half_there = (1 - core) * HALF
     gate_other, up_other, down_other = [
         swap(one, "core") for one in (w_gate[0], w_up[0], w_down[0])
     ]
@@ -340,8 +347,8 @@
     picked, keys = call(
         pick_kernel,
         [shape(17, 16, 576), shape(16, 64, 576)],
-        [SM] + [FAR] * 8,
-        (ids,) + tuple(far(one) for one in given + (prompt_pool[0, 0, 0],)),
+        [FAR] * 8,
+        tuple(far(one) for one in given + (prompt_pool[0, 0, 0],)),
         19000000,
         900000,
         [pltpu.VMEM(one.shape, one.dtype) for one in given[:6]]
@@ -354,13 +361,12 @@
     raising = pl.pallas_call(
         stash_kernel,
         out_shape=pltpu.VMEM((HALF, 512), bf16),
-        in_specs=[SM] + [FAR] * 4 + [ANY],
+        in_specs=[FAR] * 4 + [ANY],
         out_specs=VM,
         scratch_shapes=[pltpu.SemaphoreType.DMA((4,))],
         compiler_params=pltpu.CompilerParams(vmem_limit_bytes=4 * MIB),
         cost_estimate=pl.CostEstimate(flops=0, bytes_accessed=7400000, transcendentals=0),
     )(
-        ids,
         *[far(one) for one in (w_gate[0], w_up[0], gate_other, up_other)],
         picked,
     )
@@ -368,8 +374,8 @@
     sent, told = call(
         attention_kernel,
         [shape(32, 8, 640), shape(16, 128, dtype=f32)],
-        [SM, VM, VM, VM] + [ANY] * len(after),
-        (ids, q, keys, keys_other) + after,
+        [VM, VM, VM] + [ANY] * len(after),
+        (q, keys, keys_other) + after,
         300000000,
         4000000,
         [pltpu.VMEM((5, 256, 128), f32)],
@@ -380,8 +386,8 @@
     vals, passed = call(
         context_kernel,
         [shape(8, 128), shape(CHUNKS, 8, 128)],
-        [SM] + [VM] * 4,
-        (ids, got, told, value_up[0], out_proj),
+        [VM] * 4,
+        (got, told, value_up[0], out_proj),
         12000000,
         1500000,
         (),
@@ -390,8 +396,8 @@
     kept = call(
         kept_kernel,
         shape(CHUNKS, 8, 128, dtype=f32),
-        [SM] + [VM] * 3,
-        (ids, vals, told, out_proj),
+        [VM] * 3,
+        (vals, told, out_proj),
         8000000,
         1000000,
         (),
@@ -404,8 +410,8 @@
         call(
             spread_kernel,
             shape(64, 8, 128),
-            [SM, VM, VM],
-            (ids, exchange(partial, XZ), told),
+            [VM, VM],
+            (exchange(partial, XZ), told),
             40000,
             200000,
             (),
@@ -416,8 +422,8 @@
     raised = call(
         raise_kernel,
         shape(16, 896, dtype=f32),
-        [SM] + [VM] * 3,
-        (ids, rows, norm_gain.reshape(56, 128), raising),
+        [VM] * 3,
+        (rows, norm_gain.reshape(56, 128), raising),
         60000000,
         6000000,
         [pltpu.VMEM((16, HALF), bf16), pltpu.VMEM((8, HALF), f32)],
@@ -427,8 +433,8 @@
     outgoing, own = call(
         lower_kernel,
         [shape(64, 8, 128), shape(8, 128, dtype=f32)],
-        [SM] + [VM] * 5,
-        (ids, raised, raised_other, rows, w_down[0], down_other),
+        [VM] * 5,
+        (raised, raised_other, rows, w_down[0], down_other),
         60000000,
         4000000,
         [pltpu.VMEM((16, 7296), f32)],

time: 101 us -> 97.2 us (0.962)
  Pallas kernels: 12.5 us -> 8.17 us
  local copies, waits for them, and re-layouts: 0.68 us -> 1.95 us
    pallas_call x9, Pallas kernels: 9.93 us -> 6.13 us  [call(): pl.pallas_call(kernel, out_shape=outs, in_specs=specs, out_specs=[VM] * l...]
    unnamed x9 -> x13, local copies, waits for them, and re-layouts: 0.6 us -> 1.95 us
  transfers between devices with their start and end apart: 8 -> 8, of which waited for: 5 -> 5; matrix products, arithmetic and copies ran while one was open for 0% -> 0% of each run, Pallas kernels for 6% -> 5%
where the time goes in v5:
time: 97.2 us; the launch traced here: 96.9 us
  blocking collectives  69.8 us (72%)
  waiting for transfers between devices  12.9 us (13%)
  Pallas kernels  8.17 us (8%)
  starting transfers between devices  3.97 us (4%)
  local copies, waits for them, and re-layouts  1.95 us (2%)
    all_to_all x4, blocking collectives, exchange(): return lax.all_to_all(value, axes, 0, 0, tiled=True)  69.8 us
    ppermute x8, waiting for transfers between devices, swap(): return lax.ppermute(value, axis, [(0, 1), (1, 0)])  12.9 us
    pallas_call x9, Pallas kernels, call(): pl.pallas_call(kernel, out_shape=outs, in_specs=specs, out_specs=[VM] * l...  6.13 us
    ppermute x8, starting transfers between devices, swap(): return lax.ppermute(value, axis, [(0, 1), (1, 0)])  3.97 us
    pallas_call x1, Pallas kernels, body(): pl.pallas_call(stash_kernel, out_shape=pltpu.VMEM((HALF, 512), bf16), in_...  2.04 us
    unnamed x13, local copies, waits for them, and re-layouts  1.95 us
  transfers between devices with their start and end apart: 8, of which 5 were waited for; matrix products, arithmetic and copies ran while one was open for 0% of the time, Pallas kernels for 5%

profile of v5, /device:TPU:16, one launch (start us, length us, event | category | flops | bytes accessed | tf_op | source)
XLA Modules:
  0.0 96.9 jit_solution(1879527319098998875)
XLA Ops:
  0.0 0.0 collective-permute-start.2
  0.0 0.5 collective-permute-start.3
  0.5 0.0 collective-permute-start.4
  0.5 2.3 %shard_map.136 = (bf16[17,16,576]{2,1,0:T(8,128)(2,1)S(1)}, bf16[16,64,576]{2,1,0:T(8,128)(2,1)S(1)}) custom-call(bf16[8,64,576]{2,1,0:T(8,128)(2,1)} %bitcast.25, bf16[2,4,576]{2,1,0:T(4,128)(2,1)} %bitcast.26, bf16[2,4,112]{2,1,0:T(4,128)(2,1)} %bitcast.30, s32[2,4,8]{2,1,0:T(4,128)} %bitcast.27, f32[2,4,8]{2,1,0:T(4,128)} %bitcast.28, s32[1,4]{1,0:T(1,128)} %bitcast.32, ...), custom_call_target="tpu_custom_call" | custom-call | flops 19000000 | bytes 900000 | tf_op jit(solution)/shard_map/pallas_call | solution.py:27
  2.8 0.6 collective-permute-start.1
  3.4 2.1 %collective-permute-start = (bf16[17,16,576]{2,1,0:T(8,128)(2,1)S(1)}, bf16[17,16,576]{2,1,0:T(8,128)(2,1)S(1)}, u32[]{:S(2)}, u32[]{:S(2)}) collective-permute-start(bf16[17,16,576]{2,1,0:T(8,128)(2,1)S(1)} %get-tuple-element.13.refs_4_), channel_id=1, source_target_pairs={{0,128},{128,0},{1,129},{129,1},{2,130},{130,2},{3,131},{131,3},{4... | collective-permute-start | bytes 940040 | tf_op jit(solution)/shard_map/ppermute | solution.py:47
  5.5 0.0 collective-permute-done.2.refs_2_
  5.5 0.0 copy-start.4
  5.5 1.1 %collective-permute-done.3.refs_3_ = bf16[7168,128]{1,0:T(8,128)(2,1)S(1)} collective-permute-done((bf16[7168,128]{1,0:T(8,128)(2,1)}, bf16[7168,128]{1,0:T(8,128)(2,1)S(1)}, u32[]{:S(2)}, u32[]{:S(2)}) %collective-permute-start.3) | collective-permute-done | bytes 1835040 | tf_op jit(solution)/shard_map/ppermute | solution.py:47
  6.6 0.1 copy-done.4
  6.7 0.0 copy-start.5
  6.7 1.2 %copy-done.5 = bf16[7168,128]{1,0:T(8,128)(2,1)} copy-done((bf16[7168,128]{1,0:T(8,128)(2,1)}, bf16[7168,128]{1,0:T(8,128)(2,1)S(1)}, u32[]{:S(2)}) %copy-start.5) | copy-done | bytes 1835032
  8.0 2.0 %shard_map.137.rest_0_.weights = bf16[3584,512]{1,0:T(8,128)(2,1)S(1)} custom-call(bf16[7168,128]{1,0:T(8,128)(2,1)} %bitcast.21, bf16[7168,128]{1,0:T(8,128)(2,1)} %bitcast.23, bf16[7168,128]{1,0:T(8,128)(2,1)} %copy-done.4, bf16[7168,128]{1,0:T(8,128)(2,1)} %copy-done.5, bf16[17,16,576]{2,1,0:T(8,128)(2,1)S(1)} %get-tuple-element.13.refs_4_), custom_call_target="tpu_custom_call" | custom-call | bytes 7400000 | tf_op jit(solution)/shard_map/pallas_call | solution.py:361
  10.0 0.0 copy-start.2
  10.0 5.0 %collective-permute-done.q = bf16[17,16,576]{2,1,0:T(8,128)(2,1)S(1)} collective-permute-done((bf16[17,16,576]{2,1,0:T(8,128)(2,1)S(1)}, bf16[17,16,576]{2,1,0:T(8,128)(2,1)S(1)}, u32[]{:S(2)}, u32[]{:S(2)}) %collective-permute-start) | collective-permute-done | bytes 313376 | tf_op jit(solution)/shard_map/ppermute | solution.py:47
  15.1 0.0 collective-permute-done.1.keys_other
  15.1 0.0 collective-permute-done.4.rest_1_.down_other
  15.1 0.0 copy-start
  15.1 1.6 %shard_map.138 = (bf16[32,8,640]{2,1,0:T(8,128)(2,1)S(1)}, f32[16,128]{1,0:T(8,128)S(1)}) custom-call(bf16[17,16,576]{2,1,0:T(8,128)(2,1)S(1)} %collective-permute-done.q, bf16[16,64,576]{2,1,0:T(8,128)(2,1)S(1)} %get-tuple-element.14.keys_mine, bf16[16,64,576]{2,1,0:T(8,128)(2,1)S(1)} %collective-permute-done.1.keys_other, ...), custom_call_target="tpu_custom_call" | custom-call | flops 300000000 | bytes 4000000 | tf_op jit(solution)/shard_map/pallas_call | solution.py:27
  16.6 23.9 %all_to_all.20.got = bf16[32,8,640]{2,1,0:T(8,128)(2,1)S(1)} all-to-all(bf16[32,8,640]{2,1,0:T(8,128)(2,1)S(1)} %get-tuple-element.15), channel_id=1, replica_groups=mesh['role'=2,'dp'=2,'x'=4,'z'=8,'core'=2] {'x','z'}, dimensions={0} | all-to-all | bytes 655360 | tf_op jit(solution)/shard_map/all_to_all | solution.py:51
  40.6 0.0 copy-done.2
  40.6 0.0 copy-done
  40.6 0.5 shard_map.139
  41.1 0.0 copy-start.3
  41.1 0.1 collective-permute-start.5
  41.2 0.2 shard_map.140.kept
  41.4 1.0 %collective-permute-done.5.other = bf16[28,8,128]{2,1,0:T(8,128)(2,1)S(1)} collective-permute-done((bf16[28,8,128]{2,1,0:T(8,128)(2,1)S(1)}, bf16[28,8,128]{2,1,0:T(8,128)(2,1)S(1)}, u32[]{:S(2)}, u32[]{:S(2)}) %collective-permute-start.5) | collective-permute-done | bytes 57376 | tf_op jit(solution)/shard_map/ppermute | solution.py:47
  42.4 14.7 %all_to_all.21.got = bf16[32,8,128]{2,1,0:T(8,128)(2,1)S(1)} all-to-all(bf16[32,8,128]{2,1,0:T(8,128)(2,1)S(1)} %shard_map.141), channel_id=1, replica_groups=mesh['role'=2,'dp'=2,'x'=4,'z'=8,'core'=2] {'x','z'}, dimensions={0} | all-to-all | bytes 131072 | tf_op jit(solution)/shard_map/all_to_all | solution.py:51
  57.2 15.7 %all_to_all.22.rows = bf16[64,8,128]{2,1,0:T(8,128)(2,1)S(1)} all-to-all(bf16[64,8,128]{2,1,0:T(8,128)(2,1)S(1)} %shard_map.142), channel_id=1, replica_groups=mesh['role'=2,'dp'=2,'x'=4,'z'=8,'core'=2] {'dp','x','z'}, dimensions={0} | all-to-all | bytes 262144 | tf_op jit(solution)/shard_map/all_to_all | solution.py:51
  72.9 0.0 copy-done.3
  72.9 0.0 copy-start.1
  72.9 0.6 shard_map.143.mine
  73.5 0.0 collective-permute-start.6
  73.5 1.3 %collective-permute-done.6.other = f32[16,896]{1,0:T(8,128)S(1)} collective-permute-done((f32[16,896]{1,0:T(8,128)S(1)}, f32[16,896]{1,0:T(8,128)S(1)}, u32[]{:S(2)}, u32[]{:S(2)}) %collective-permute-start.6) | collective-permute-done | bytes 57376 | tf_op jit(solution)/shard_map/ppermute | solution.py:47
  74.7 0.0 copy-done.1
  74.7 0.8 shard_map.144
  75.5 15.5 %all_to_all.23.got = bf16[64,8,128]{2,1,0:T(8,128)(2,1)S(1)} all-to-all(bf16[64,8,128]{2,1,0:T(8,128)(2,1)S(1)} %get-tuple-element.19), channel_id=1, replica_groups=mesh['role'=2,'dp'=2,'x'=4,'z'=8,'core'=2] {'dp','x','z'}, dimensions={0} | all-to-all | bytes 262144 | tf_op jit(solution)/shard_map/all_to_all | solution.py:51
  91.1 0.1 shard_map.145
  91.1 0.7 collective-permute-start.7
  91.9 4.5 %collective-permute-done.7 = bf16[2,4,112]{2,1,0:T(4,128)(2,1)S(1)} collective-permute-done((bf16[2,4,112]{2,1,0:T(4,128)(2,1)S(1)}, bf16[2,4,112]{2,1,0:T(4,128)(2,1)S(1)}, u32[]{:S(2)}, u32[]{:S(2)}) %collective-permute-start.7) | collective-permute-done | bytes 1824 | tf_op jit(solution)/shard_map/ppermute | solution.py:47
  96.3 0.6 copy.17
  (2 shorter events, 0.1 us)
Async XLA Ops:
  0.0 5.5 %collective-permute-start.2 = (bf16[7168,128]{1,0:T(8,128)(2,1)}, bf16[7168,128]{1,0:T(8,128)(2,1)S(1)}, u32[]{:S(2)}, u32[]{:S(2)}) collective-permute-start(bf16[7168,128]{1,0:T(8,128)(2,1)} %bitcast.20), channel_id=1, source_target_pairs={{0,1},{1,0},{2,3},{3,2},{4,5},{5,4},{6,7},{7,6},{8,9},{9,8},{10,11... | collective-permute-start | bytes 5505032 | tf_op jit(solution)/shard_map/ppermute | solution.py:47
  0.0 6.6 %collective-permute-start.3 = (bf16[7168,128]{1,0:T(8,128)(2,1)}, bf16[7168,128]{1,0:T(8,128)(2,1)S(1)}, u32[]{:S(2)}, u32[]{:S(2)}) collective-permute-start(bf16[7168,128]{1,0:T(8,128)(2,1)} %bitcast.22), channel_id=1, source_target_pairs={{0,1},{1,0},{2,3},{3,2},{4,5},{5,4},{6,7},{7,6},{8,9},{9,8},{10,11... | collective-permute-start | bytes 5505032 | tf_op jit(solution)/shard_map/ppermute | solution.py:47
  0.5 14.6 %collective-permute-start.4 = (bf16[128,7168]{1,0:T(8,128)(2,1)}, bf16[128,7168]{1,0:T(8,128)(2,1)S(1)}, u32[]{:S(2)}, u32[]{:S(2)}) collective-permute-start(bf16[128,7168]{1,0:T(8,128)(2,1)} %bitcast.16), channel_id=1, source_target_pairs={{0,1},{1,0},{2,3},{3,2},{4,5},{5,4},{6,7},{7,6},{8,9},{9,8},{10,11... | collective-permute-start | bytes 5505032 | tf_op jit(solution)/shard_map/ppermute | solution.py:47
  2.8 12.3 %collective-permute-start.1 = (bf16[16,64,576]{2,1,0:T(8,128)(2,1)S(1)}, bf16[16,64,576]{2,1,0:T(8,128)(2,1)S(1)}, u32[]{:S(2)}, u32[]{:S(2)}) collective-permute-start(bf16[16,64,576]{2,1,0:T(8,128)(2,1)S(1)} %get-tuple-element.14.keys_mine), channel_id=1, source_target_pairs={{0,1},{1,0},{2,3},{3,2},{4,5},{5,4},{6,7},{7,6},{8,9},{9,8},{10,11... | collective-permute-start | bytes 3538952 | tf_op jit(solution)/shard_map/ppermute | solution.py:47
  3.4 11.7 %collective-permute-start = (bf16[17,16,576]{2,1,0:T(8,128)(2,1)S(1)}, bf16[17,16,576]{2,1,0:T(8,128)(2,1)S(1)}, u32[]{:S(2)}, u32[]{:S(2)}) collective-permute-start(bf16[17,16,576]{2,1,0:T(8,128)(2,1)S(1)} %get-tuple-element.13.refs_4_), channel_id=1, source_target_pairs={{0,128},{128,0},{1,129},{129,1},{2,130},{130,2},{3,131},{131,3},{4... | collective-permute-start | bytes 940040 | tf_op jit(solution)/shard_map/ppermute | solution.py:47
  5.5 1.3 %copy-start.4 = (bf16[7168,128]{1,0:T(8,128)(2,1)}, bf16[7168,128]{1,0:T(8,128)(2,1)S(1)}, u32[]{:S(2)}) copy-start(bf16[7168,128]{1,0:T(8,128)(2,1)S(1)} %collective-permute-done.2.refs_2_) | copy-start | bytes 5505028
  6.7 1.2 %copy-start.5 = (bf16[7168,128]{1,0:T(8,128)(2,1)}, bf16[7168,128]{1,0:T(8,128)(2,1)S(1)}, u32[]{:S(2)}) copy-start(bf16[7168,128]{1,0:T(8,128)(2,1)S(1)} %collective-permute-done.3.refs_3_) | copy-start | bytes 5505028
  10.0 30.5 %copy-start.2 = (bf16[1,512,128]{2,1,0:T(8,128)(2,1)S(1)}, bf16[1,512,128]{2,1,0:T(8,128)(2,1)}, u32[]{:S(2)}) copy-start(bf16[1,512,128]{2,1,0:T(8,128)(2,1)} %param.23) | copy-start | bytes 393220
  15.1 25.5 %copy-start = (bf16[128,7168]{1,0:T(8,128)(2,1)S(1)}, bf16[128,7168]{1,0:T(8,128)(2,1)}, u32[]{:S(2)}) copy-start(bf16[128,7168]{1,0:T(8,128)(2,1)} %proj.3) | copy-start | bytes 5505028
  41.1 31.8 %copy-start.3 = (f32[7168]{0:T(1024)S(1)}, f32[7168]{0:T(1024)}, u32[]{:S(2)}) copy-start(f32[7168]{0:T(1024)} %param.22) | copy-start | bytes 86020
  41.1 1.3 %collective-permute-start.5 = (bf16[28,8,128]{2,1,0:T(8,128)(2,1)S(1)}, bf16[28,8,128]{2,1,0:T(8,128)(2,1)S(1)}, u32[]{:S(2)}, u32[]{:S(2)}) collective-permute-start(bf16[28,8,128]{2,1,0:T(8,128)(2,1)S(1)} %get-tuple-element.18), channel_id=1, source_target_pairs={{0,1},{1,0},{2,3},{3,2},{4,5},{5,4},{6,7},{7,6},{8,9},{9,8},{10,11... | collective-permute-start | bytes 172040 | tf_op jit(solution)/shard_map/ppermute | solution.py:47
  72.9 1.8 %copy-start.1 = (bf16[1,128,7168]{2,1,0:T(8,128)(2,1)S(1)}, bf16[1,128,7168]{2,1,0:T(8,128)(2,1)}, u32[]{:S(2)}) copy-start(bf16[1,128,7168]{2,1,0:T(8,128)(2,1)} %param.27) | copy-start | bytes 5505028
  73.5 1.3 %collective-permute-start.6 = (f32[16,896]{1,0:T(8,128)S(1)}, f32[16,896]{1,0:T(8,128)S(1)}, u32[]{:S(2)}, u32[]{:S(2)}) collective-permute-start(f32[16,896]{1,0:T(8,128)S(1)} %shard_map.143.mine), channel_id=1, source_target_pairs={{0,1},{1,0},{2,3},{3,2},{4,5},{5,4},{6,7},{7,6},{8,9},{9,8},{10,11... | collective-permute-start | bytes 172040 | tf_op jit(solution)/shard_map/ppermute | solution.py:47
  91.1 5.2 %collective-permute-start.7 = (bf16[2,4,112]{2,1,0:T(4,128)(2,1)S(1)}, bf16[2,4,112]{2,1,0:T(4,128)(2,1)S(1)}, u32[]{:S(2)}, u32[]{:S(2)}) collective-permute-start(bf16[2,4,112]{2,1,0:T(4,128)(2,1)S(1)} %shard_map.145), channel_id=1, source_target_pairs={{0,128},{128,0},{1,129},{129,1},{2,130},{130,2},{3,131},{131,3},{4... | collective-permute-start | bytes 5384 | tf_op jit(solution)/shard_map/ppermute | solution.py:47

commit v6 on v5

--- a/solution.py
+++ b/solution.py
@@ -206,6 +206,8 @@
     total = total + jnp.where(ids[2] // 32 == half, start, 0.0)
     for k in range(CHUNKS):
         out[k] = total[:, 128 * k : 128 * k + 128].astype(out.dtype)
+    for k in range(CHUNKS, 32):
+        out[k] = jnp.zeros((8, 128), out.dtype)
 
 
 def context_kernel(got, told, value_up, proj, vals, sent):
@@ -226,21 +228,33 @@
     project(ids, ids[0], vals, told, proj, kept)
 
 
-def join_kernel(kept, other, out):
-    for k in range(CHUNKS):
-        out[k] = (kept[k] + other[k].astype(f32)).astype(bf16)
-    for k in range(CHUNKS, 32):
-        out[k] = jnp.zeros((8, 128), bf16)
+def join_kernel(kept, other, own, *outs):
+    for k in range(4):
+        group = pl.ds(lax.rem(lax.axis_index("x") + k, 4) * 8, 8)
+        total = kept[group] + other[group].astype(f32)
+        if k == 0:
+            own[...] = total
+        else:
+            outs[k - 1][...] = total.astype(bf16)
+
+
+def sum_kernel(own, first, second, third, out):
+    total = own[...] + first[...].astype(f32) + second[...].astype(f32) + third[...].astype(f32)
+    total = total.astype(bf16)
+    for i in range(8):
+        out[i] = total
 
 
 def spread_kernel(got, told, out):
-    ids = spot()
-    total = got[0].astype(f32)
-    for i in range(1, 32):
-        total = total + got[i].astype(f32)
-    piece = jnp.where(ids[3] == CHUNKS, told[8:16, :], total).astype(bf16)
-    for i in range(64):
-        out[i] = piece
+    for k in range(8):
+        total = got[0, k].astype(f32)
+        for i in range(1, 8):
+            total = total + got[i, k].astype(f32)
+        if k == CHUNKS % 8:
+            total = jnp.where(lax.axis_index("x") == CHUNKS // 8, told[8:16, :], total)
+        piece = total.astype(bf16)
+        for i in range(8):
+            out[i, k] = piece
 
 
 def raise_kernel(rows, gain, weights, out, scaled, own):
@@ -385,7 +399,7 @@
     got = exchange(sent, XZ)
     vals, passed = call(
         context_kernel,
-        [shape(8, 128), shape(CHUNKS, 8, 128)],
+        [shape(8, 128), shape(32, 8, 128)],
         [VM] * 4,
         (got, told, value_up[0], out_proj),
         12000000,
@@ -395,7 +409,7 @@
     )
     kept = call(
         kept_kernel,
-        shape(CHUNKS, 8, 128, dtype=f32),
+        shape(32, 8, 128, dtype=f32),
         [VM] * 3,
         (vals, told, out_proj),
         8000000,
@@ -403,22 +417,32 @@
         (),
         8,
     )
-    partial = call(
-        join_kernel, shape(32, 8, 128), [VM] * 2, (kept, swap(passed, "core")), 30000, 200000, (), 4
-    )
-    rows = exchange(
-        call(
-            spread_kernel,
-            shape(64, 8, 128),
-            [VM, VM],
-            (exchange(partial, XZ), told),
-            40000,
-            200000,
-            (),
-            4,
-        ),
-        DXZ,
-    )
+    own_x, *sent_x = call(
+        join_kernel,
+        [shape(8, 8, 128, dtype=f32)] + [shape(8, 8, 128)] * 3,
+        [VM] * 2,
+        (kept, swap(passed, "core")),
+        30000,
+        200000,
+        (),
+        4,
+    )
+    got_x = [
+        lax.ppermute(one, "x", [(i, (i + k + 1) % 4) for i in range(4)])
+        for k, one in enumerate(sent_x)
+    ]
+    sent_z = call(sum_kernel, shape(8, 8, 8, 128), [VM] * 4, (own_x, *got_x), 30000, 200000, (), 4)
+    sent_rows = call(
+        spread_kernel,
+        shape(8, 8, 8, 128),
+        [VM, VM],
+        (exchange(sent_z, "z"), told),
+        60000,
+        260000,
+        (),
+        4,
+    )
+    rows = exchange(sent_rows, ("dp", "x")).reshape(64, 8, 128)
     raised = call(
         raise_kernel,
         shape(16, 896, dtype=f32),

time: 97.2 us -> 96.8 us (level)
  blocking collectives: 69.8 us -> 62.9 us
  starting transfers between devices: 3.97 us -> 8.33 us
  waiting for transfers between devices: 12.9 us -> 15 us
    all_to_all x4, blocking collectives: 69.8 us -> 62.9 us  [exchange(): return lax.all_to_all(value, axes, 0, 0, tiled=True)]
    ppermute x0 -> x3, starting transfers between devices: none -> 4.35 us  [body(): lax.ppermute(one, 'x', [(i, (i + k + 1) % 4) for i in range(4)])]
    ppermute x0 -> x3, waiting for transfers between devices: none -> 2.11 us  [body(): lax.ppermute(one, 'x', [(i, (i + k + 1) % 4) for i in range(4)])]
    pallas_call x9 -> x10, Pallas kernels: 6.13 us -> 6.13 us  [call(): pl.pallas_call(kernel, out_shape=outs, in_specs=specs, out_specs=[VM] * l...]
  transfers between devices with their start and end apart: 8 -> 11, of which waited for: 5 -> 8; matrix products, arithmetic and copies ran while one was open for 0% -> 0% of each run, Pallas kernels for 5% -> 5%
where the time goes in v6:
time: 96.8 us; the launch traced here: 96.5 us
  blocking collectives  62.9 us (65%)
  waiting for transfers between devices  15 us (15%)
  starting transfers between devices  8.33 us (9%)
  Pallas kernels  8.17 us (8%)
  local copies, waits for them, and re-layouts  1.93 us (2%)
    all_to_all x4, blocking collectives, exchange(): return lax.all_to_all(value, axes, 0, 0, tiled=True)  62.9 us
    ppermute x8, waiting for transfers between devices, swap(): return lax.ppermute(value, axis, [(0, 1), (1, 0)])  12.9 us
    pallas_call x10, Pallas kernels, call(): pl.pallas_call(kernel, out_shape=outs, in_specs=specs, out_specs=[VM] * l...  6.13 us
    ppermute x3, starting transfers between devices, body(): lax.ppermute(one, 'x', [(i, (i + k + 1) % 4) for i in range(4)])  4.35 us
    ppermute x8, starting transfers between devices, swap(): return lax.ppermute(value, axis, [(0, 1), (1, 0)])  3.97 us
    ppermute x3, waiting for transfers between devices, body(): lax.ppermute(one, 'x', [(i, (i + k + 1) % 4) for i in range(4)])  2.11 us
    pallas_call x1, Pallas kernels, body(): pl.pallas_call(stash_kernel, out_shape=pltpu.VMEM((HALF, 512), bf16), in_...  2.04 us
  transfers between devices with their start and end apart: 11, of which 8 were waited for; matrix products, arithmetic and copies ran while one was open for 0% of the time, Pallas kernels for 5%

profile of v6, /device:TPU:16, one launch (start us, length us, event | category | flops | bytes accessed | tf_op | source)
XLA Modules:
  0.0 96.5 jit_solution(11180035618045059823)
XLA Ops:
  0.0 0.0 collective-permute-start.2
  0.0 0.5 collective-permute-start.3
  0.5 0.0 collective-permute-start.4
  0.5 2.3 %shard_map.136 = (bf16[17,16,576]{2,1,0:T(8,128)(2,1)S(1)}, bf16[16,64,576]{2,1,0:T(8,128)(2,1)S(1)}) custom-call(bf16[8,64,576]{2,1,0:T(8,128)(2,1)} %bitcast.28, bf16[2,4,576]{2,1,0:T(4,128)(2,1)} %bitcast.29, bf16[2,4,112]{2,1,0:T(4,128)(2,1)} %bitcast.33, s32[2,4,8]{2,1,0:T(4,128)} %bitcast.30, f32[2,4,8]{2,1,0:T(4,128)} %bitcast.31, s32[1,4]{1,0:T(1,128)} %bitcast.35, ...), custom_call_target="tpu_custom_call" | custom-call | flops 19000000 | bytes 900000 | tf_op jit(solution)/shard_map/pallas_call | solution.py:27
  2.8 0.6 collective-permute-start.1
  3.4 2.1 %collective-permute-start = (bf16[17,16,576]{2,1,0:T(8,128)(2,1)S(1)}, bf16[17,16,576]{2,1,0:T(8,128)(2,1)S(1)}, u32[]{:S(2)}, u32[]{:S(2)}) collective-permute-start(bf16[17,16,576]{2,1,0:T(8,128)(2,1)S(1)} %get-tuple-element.17.refs_4_), channel_id=1, source_target_pairs={{0,128},{128,0},{1,129},{129,1},{2,130},{130,2},{3,131},{131,3},{4... | collective-permute-start | bytes 940040 | tf_op jit(solution)/shard_map/ppermute | solution.py:47
  5.5 0.0 collective-permute-done.2.refs_2_
  5.5 0.0 copy-start.4
  5.5 1.1 %collective-permute-done.3.refs_3_ = bf16[7168,128]{1,0:T(8,128)(2,1)S(1)} collective-permute-done((bf16[7168,128]{1,0:T(8,128)(2,1)}, bf16[7168,128]{1,0:T(8,128)(2,1)S(1)}, u32[]{:S(2)}, u32[]{:S(2)}) %collective-permute-start.3) | collective-permute-done | bytes 1835040 | tf_op jit(solution)/shard_map/ppermute | solution.py:47
  6.6 0.1 copy-done.4
  6.7 0.0 copy-start.5
  6.7 1.2 %copy-done.5 = bf16[7168,128]{1,0:T(8,128)(2,1)} copy-done((bf16[7168,128]{1,0:T(8,128)(2,1)}, bf16[7168,128]{1,0:T(8,128)(2,1)S(1)}, u32[]{:S(2)}) %copy-start.5) | copy-done | bytes 1835032
  8.0 2.0 %shard_map.137.rest_0_.weights = bf16[3584,512]{1,0:T(8,128)(2,1)S(1)} custom-call(bf16[7168,128]{1,0:T(8,128)(2,1)} %bitcast.24, bf16[7168,128]{1,0:T(8,128)(2,1)} %bitcast.26, bf16[7168,128]{1,0:T(8,128)(2,1)} %copy-done.4, bf16[7168,128]{1,0:T(8,128)(2,1)} %copy-done.5, bf16[17,16,576]{2,1,0:T(8,128)(2,1)S(1)} %get-tuple-element.17.refs_4_), custom_call_target="tpu_custom_call" | custom-call | bytes 7400000 | tf_op jit(solution)/shard_map/pallas_call | solution.py:375
  10.0 0.0 copy-start.2
  10.0 5.0 %collective-permute-done.q = bf16[17,16,576]{2,1,0:T(8,128)(2,1)S(1)} collective-permute-done((bf16[17,16,576]{2,1,0:T(8,128)(2,1)S(1)}, bf16[17,16,576]{2,1,0:T(8,128)(2,1)S(1)}, u32[]{:S(2)}, u32[]{:S(2)}) %collective-permute-start) | collective-permute-done | bytes 313376 | tf_op jit(solution)/shard_map/ppermute | solution.py:47
  15.1 0.0 collective-permute-done.1.keys_other
  15.1 0.0 collective-permute-done.4.rest_1_.down_other
  15.1 0.0 copy-start
  15.1 1.6 %shard_map.138 = (bf16[32,8,640]{2,1,0:T(8,128)(2,1)S(1)}, f32[16,128]{1,0:T(8,128)S(1)}) custom-call(bf16[17,16,576]{2,1,0:T(8,128)(2,1)S(1)} %collective-permute-done.q, bf16[16,64,576]{2,1,0:T(8,128)(2,1)S(1)} %get-tuple-element.18.keys_mine, bf16[16,64,576]{2,1,0:T(8,128)(2,1)S(1)} %collective-permute-done.1.keys_other, ...), custom_call_target="tpu_custom_call" | custom-call | flops 300000000 | bytes 4000000 | tf_op jit(solution)/shard_map/pallas_call | solution.py:27
  16.6 23.9 %all_to_all.20.got = bf16[32,8,640]{2,1,0:T(8,128)(2,1)S(1)} all-to-all(bf16[32,8,640]{2,1,0:T(8,128)(2,1)S(1)} %get-tuple-element.19), channel_id=1, replica_groups=mesh['role'=2,'dp'=2,'x'=4,'z'=8,'core'=2] {'x','z'}, dimensions={0} | all-to-all | bytes 655360 | tf_op jit(solution)/shard_map/all_to_all | solution.py:51
  40.6 0.0 copy-done.2
  40.6 0.0 copy-done
  40.6 0.5 shard_map.139
  41.1 0.0 copy-start.3
  41.1 0.1 collective-permute-start.5
  41.2 0.2 shard_map.140.kept
  41.4 1.0 %collective-permute-done.5.other = bf16[32,8,128]{2,1,0:T(8,128)(2,1)S(1)} collective-permute-done((bf16[32,8,128]{2,1,0:T(8,128)(2,1)S(1)}, bf16[32,8,128]{2,1,0:T(8,128)(2,1)S(1)}, u32[]{:S(2)}, u32[]{:S(2)}) %collective-permute-start.5) | collective-permute-done | bytes 65568 | tf_op jit(solution)/shard_map/ppermute | solution.py:47
  42.4 0.7 collective-permute-start.6
  43.1 2.0 %collective-permute-start.7 = (bf16[8,8,128]{2,1,0:T(8,128)(2,1)S(1)}, bf16[8,8,128]{2,1,0:T(8,128)(2,1)S(1)}, u32[]{:S(2)}, u32[]{:S(2)}) collective-permute-start(bf16[8,8,128]{2,1,0:T(8,128)(2,1)S(1)} %get-tuple-element.25), channel_id=1, source_target_pairs={{0,32},{16,48},{32,0},{48,16},{1,33},{17,49},{33,1},{49,17},{2,34}... | collective-permute-start | bytes 49160 | tf_op jit(solution)/shard_map/ppermute | solution.py:431
  45.2 1.6 %collective-permute-start.8 = (bf16[8,8,128]{2,1,0:T(8,128)(2,1)S(1)}, bf16[8,8,128]{2,1,0:T(8,128)(2,1)S(1)}, u32[]{:S(2)}, u32[]{:S(2)}) collective-permute-start(bf16[8,8,128]{2,1,0:T(8,128)(2,1)S(1)} %get-tuple-element.26), channel_id=1, source_target_pairs={{0,48},{16,0},{32,16},{48,32},{1,49},{17,1},{33,17},{49,33},{2,50}... | collective-permute-start | bytes 49160 | tf_op jit(solution)/shard_map/ppermute | solution.py:431
  46.8 0.7 collective-permute-done.6.first
  47.5 0.9 collective-permute-done.7.second
  48.4 0.5 collective-permute-done.8.third
  48.9 12.6 %all_to_all.21.got = bf16[8,8,8,128]{3,2,1,0:T(8,128)(2,1)S(1)} all-to-all(bf16[8,8,8,128]{3,2,1,0:T(8,128)(2,1)S(1)} %shard_map.142), channel_id=1, replica_groups=mesh['role'=2,'dp'=2,'x'=4,'z'=8,'core'=2] {'z'}, dimensions={0} | all-to-all | bytes 262144 | tf_op jit(solution)/shard_map/all_to_all | solution.py:51
  61.5 10.9 %all_to_all.22 = bf16[8,8,8,128]{3,2,1,0:T(8,128)(2,1)S(1)} all-to-all(bf16[8,8,8,128]{3,2,1,0:T(8,128)(2,1)S(1)} %shard_map.143), channel_id=1, replica_groups=mesh['role'=2,'dp'=2,'x'=4,'z'=8,'core'=2] {'dp','x'}, dimensions={0} | all-to-all | bytes 262144 | tf_op jit(solution)/shard_map/all_to_all | solution.py:51
  72.5 0.0 copy-done.3
  72.5 0.0 copy-start.1
  72.5 0.6 shard_map.144.mine
  73.1 0.0 collective-permute-start.9
  73.1 1.3 %collective-permute-done.9.other = f32[16,896]{1,0:T(8,128)S(1)} collective-permute-done((f32[16,896]{1,0:T(8,128)S(1)}, f32[16,896]{1,0:T(8,128)S(1)}, u32[]{:S(2)}, u32[]{:S(2)}) %collective-permute-start.9) | collective-permute-done | bytes 57376 | tf_op jit(solution)/shard_map/ppermute | solution.py:47
  74.3 0.0 copy-done.1
  74.3 0.8 shard_map.145
  75.1 15.5 %all_to_all.23.got = bf16[64,8,128]{2,1,0:T(8,128)(2,1)S(1)} all-to-all(bf16[64,8,128]{2,1,0:T(8,128)(2,1)S(1)} %get-tuple-element.27), channel_id=1, replica_groups=mesh['role'=2,'dp'=2,'x'=4,'z'=8,'core'=2] {'dp','x','z'}, dimensions={0} | all-to-all | bytes 262144 | tf_op jit(solution)/shard_map/all_to_all | solution.py:51
  90.7 0.1 shard_map.146
  90.7 0.7 collective-permute-start.10
  91.4 4.5 %collective-permute-done.10 = bf16[2,4,112]{2,1,0:T(4,128)(2,1)S(1)} collective-permute-done((bf16[2,4,112]{2,1,0:T(4,128)(2,1)S(1)}, bf16[2,4,112]{2,1,0:T(4,128)(2,1)S(1)}, u32[]{:S(2)}, u32[]{:S(2)}) %collective-permute-start.10) | collective-permute-done | bytes 1824 | tf_op jit(solution)/shard_map/ppermute | solution.py:47
  95.9 0.6 copy.17
  (3 shorter events, 0.1 us)
Async XLA Ops:
  0.0 5.5 %collective-permute-start.2 = (bf16[7168,128]{1,0:T(8,128)(2,1)}, bf16[7168,128]{1,0:T(8,128)(2,1)S(1)}, u32[]{:S(2)}, u32[]{:S(2)}) collective-permute-start(bf16[7168,128]{1,0:T(8,128)(2,1)} %bitcast.23), channel_id=1, source_target_pairs={{0,1},{1,0},{2,3},{3,2},{4,5},{5,4},{6,7},{7,6},{8,9},{9,8},{10,11... | collective-permute-start | bytes 5505032 | tf_op jit(solution)/shard_map/ppermute | solution.py:47
  0.0 6.6 %collective-permute-start.3 = (bf16[7168,128]{1,0:T(8,128)(2,1)}, bf16[7168,128]{1,0:T(8,128)(2,1)S(1)}, u32[]{:S(2)}, u32[]{:S(2)}) collective-permute-start(bf16[7168,128]{1,0:T(8,128)(2,1)} %bitcast.25), channel_id=1, source_target_pairs={{0,1},{1,0},{2,3},{3,2},{4,5},{5,4},{6,7},{7,6},{8,9},{9,8},{10,11... | collective-permute-start | bytes 5505032 | tf_op jit(solution)/shard_map/ppermute | solution.py:47
  0.5 14.6 %collective-permute-start.4 = (bf16[128,7168]{1,0:T(8,128)(2,1)}, bf16[128,7168]{1,0:T(8,128)(2,1)S(1)}, u32[]{:S(2)}, u32[]{:S(2)}) collective-permute-start(bf16[128,7168]{1,0:T(8,128)(2,1)} %bitcast.17), channel_id=1, source_target_pairs={{0,1},{1,0},{2,3},{3,2},{4,5},{5,4},{6,7},{7,6},{8,9},{9,8},{10,11... | collective-permute-start | bytes 5505032 | tf_op jit(solution)/shard_map/ppermute | solution.py:47
  2.8 12.3 %collective-permute-start.1 = (bf16[16,64,576]{2,1,0:T(8,128)(2,1)S(1)}, bf16[16,64,576]{2,1,0:T(8,128)(2,1)S(1)}, u32[]{:S(2)}, u32[]{:S(2)}) collective-permute-start(bf16[16,64,576]{2,1,0:T(8,128)(2,1)S(1)} %get-tuple-element.18.keys_mine), channel_id=1, source_target_pairs={{0,1},{1,0},{2,3},{3,2},{4,5},{5,4},{6,7},{7,6},{8,9},{9,8},{10,11... | collective-permute-start | bytes 3538952 | tf_op jit(solution)/shard_map/ppermute | solution.py:47
  3.4 11.7 %collective-permute-start = (bf16[17,16,576]{2,1,0:T(8,128)(2,1)S(1)}, bf16[17,16,576]{2,1,0:T(8,128)(2,1)S(1)}, u32[]{:S(2)}, u32[]{:S(2)}) collective-permute-start(bf16[17,16,576]{2,1,0:T(8,128)(2,1)S(1)} %get-tuple-element.17.refs_4_), channel_id=1, source_target_pairs={{0,128},{128,0},{1,129},{129,1},{2,130},{130,2},{3,131},{131,3},{4... | collective-permute-start | bytes 940040 | tf_op jit(solution)/shard_map/ppermute | solution.py:47
  5.5 1.3 %copy-start.4 = (bf16[7168,128]{1,0:T(8,128)(2,1)}, bf16[7168,128]{1,0:T(8,128)(2,1)S(1)}, u32[]{:S(2)}) copy-start(bf16[7168,128]{1,0:T(8,128)(2,1)S(1)} %collective-permute-done.2.refs_2_) | copy-start | bytes 5505028
  6.7 1.2 %copy-start.5 = (bf16[7168,128]{1,0:T(8,128)(2,1)}, bf16[7168,128]{1,0:T(8,128)(2,1)S(1)}, u32[]{:S(2)}) copy-start(bf16[7168,128]{1,0:T(8,128)(2,1)S(1)} %collective-permute-done.3.refs_3_) | copy-start | bytes 5505028
  10.0 30.6 %copy-start.2 = (bf16[1,512,128]{2,1,0:T(8,128)(2,1)S(1)}, bf16[1,512,128]{2,1,0:T(8,128)(2,1)}, u32[]{:S(2)}) copy-start(bf16[1,512,128]{2,1,0:T(8,128)(2,1)} %param.23) | copy-start | bytes 393220
  15.1 25.5 %copy-start = (bf16[128,7168]{1,0:T(8,128)(2,1)S(1)}, bf16[128,7168]{1,0:T(8,128)(2,1)}, u32[]{:S(2)}) copy-start(bf16[128,7168]{1,0:T(8,128)(2,1)} %proj.3) | copy-start | bytes 5505028
  41.1 31.4 %copy-start.3 = (f32[7168]{0:T(1024)S(1)}, f32[7168]{0:T(1024)}, u32[]{:S(2)}) copy-start(f32[7168]{0:T(1024)} %param.22) | copy-start | bytes 86020
  41.1 1.3 %collective-permute-start.5 = (bf16[32,8,128]{2,1,0:T(8,128)(2,1)S(1)}, bf16[32,8,128]{2,1,0:T(8,128)(2,1)S(1)}, u32[]{:S(2)}, u32[]{:S(2)}) collective-permute-start(bf16[32,8,128]{2,1,0:T(8,128)(2,1)S(1)} %get-tuple-element.22), channel_id=1, source_target_pairs={{0,1},{1,0},{2,3},{3,2},{4,5},{5,4},{6,7},{7,6},{8,9},{9,8},{10,11... | collective-permute-start | bytes 196616 | tf_op jit(solution)/shard_map/ppermute | solution.py:47
  42.4 5.0 %collective-permute-start.6 = (bf16[8,8,128]{2,1,0:T(8,128)(2,1)S(1)}, bf16[8,8,128]{2,1,0:T(8,128)(2,1)S(1)}, u32[]{:S(2)}, u32[]{:S(2)}) collective-permute-start(bf16[8,8,128]{2,1,0:T(8,128)(2,1)S(1)} %get-tuple-element.24), channel_id=1, source_target_pairs={{0,16},{16,32},{32,48},{48,0},{1,17},{17,33},{33,49},{49,1},{2,18}... | collective-permute-start | bytes 49160 | tf_op jit(solution)/shard_map/ppermute | solution.py:431
  43.1 5.2 %collective-permute-start.7 = (bf16[8,8,128]{2,1,0:T(8,128)(2,1)S(1)}, bf16[8,8,128]{2,1,0:T(8,128)(2,1)S(1)}, u32[]{:S(2)}, u32[]{:S(2)}) collective-permute-start(bf16[8,8,128]{2,1,0:T(8,128)(2,1)S(1)} %get-tuple-element.25), channel_id=1, source_target_pairs={{0,32},{16,48},{32,0},{48,16},{1,33},{17,49},{33,1},{49,17},{2,34}... | collective-permute-start | bytes 49160 | tf_op jit(solution)/shard_map/ppermute | solution.py:431
  45.2 3.7 %collective-permute-start.8 = (bf16[8,8,128]{2,1,0:T(8,128)(2,1)S(1)}, bf16[8,8,128]{2,1,0:T(8,128)(2,1)S(1)}, u32[]{:S(2)}, u32[]{:S(2)}) collective-permute-start(bf16[8,8,128]{2,1,0:T(8,128)(2,1)S(1)} %get-tuple-element.26), channel_id=1, source_target_pairs={{0,48},{16,0},{32,16},{48,32},{1,49},{17,1},{33,17},{49,33},{2,50}... | collective-permute-start | bytes 49160 | tf_op jit(solution)/shard_map/ppermute | solution.py:431
  72.5 1.8 %copy-start.1 = (bf16[1,128,7168]{2,1,0:T(8,128)(2,1)S(1)}, bf16[1,128,7168]{2,1,0:T(8,128)(2,1)}, u32[]{:S(2)}) copy-start(bf16[1,128,7168]{2,1,0:T(8,128)(2,1)} %param.27) | copy-start | bytes 5505028
  73.1 1.3 %collective-permute-start.9 = (f32[16,896]{1,0:T(8,128)S(1)}, f32[16,896]{1,0:T(8,128)S(1)}, u32[]{:S(2)}, u32[]{:S(2)}) collective-permute-start(f32[16,896]{1,0:T(8,128)S(1)} %shard_map.144.mine), channel_id=1, source_target_pairs={{0,1},{1,0},{2,3},{3,2},{4,5},{5,4},{6,7},{7,6},{8,9},{9,8},{10,11... | collective-permute-start | bytes 172040 | tf_op jit(solution)/shard_map/ppermute | solution.py:47
  90.7 5.2 %collective-permute-start.10 = (bf16[2,4,112]{2,1,0:T(4,128)(2,1)S(1)}, bf16[2,4,112]{2,1,0:T(4,128)(2,1)S(1)}, u32[]{:S(2)}, u32[]{:S(2)}) collective-permute-start(bf16[2,4,112]{2,1,0:T(4,128)(2,1)S(1)} %shard_map.146), channel_id=1, source_target_pairs={{0,128},{128,0},{1,129},{129,1},{2,130},{130,2},{3,131},{131,3},{4... | collective-permute-start | bytes 5384 | tf_op jit(solution)/shard_map/ppermute | solution.py:47
